TPU v7x, 32 devices: a whole 2x2x4 slice. The times are simulated.
32 devices in a mesh: groups: 2 (over y), seq: 4 (over x, core), chan: 4 (over z).
Axes of the slice: x: 2, y: 2, z: 4, core: 2. Of those that a mesh axis runs over, the one named last changes fastest.
Arguments:
- gate_input: bfloat16 [1024, 4096], P(('groups', 'seq'), 'chan'), parts along dimension 0, may hold values from -6 to 6
- value_input: bfloat16 [1024, 4096], P(('groups', 'seq'), 'chan'), parts along dimension 0, may hold values from -6 to 6
- short_filter: float32 [4096, 128], P('chan'), may hold values from -0.5 to 0.5
- long_filter: bfloat16 [512, 4096], P('seq', 'chan'), may hold values from -0.375 to 0.375
- query_weight: bfloat16 [32, 128, 128], P('chan'), may hold values from -0.5 to 0.5
- key_matrix: bfloat16 [1024, 4096], P(('groups', 'seq'), 'chan'), parts along dimension 0, may hold values from -200 to 200
- value_matrix: bfloat16 [1024, 4096], P(('groups', 'seq'), 'chan'), parts along dimension 0, may hold values from -6 to 6
Outputs:
- attended: bfloat16 [1024, 4096], P(('groups', 'seq'), 'chan'), parts along dimension 0
There are 2 independent parts, one for each index of `groups`. A program takes and returns all parts, laid end to end along the dimension named above; an argument that names none is the same for every part. Nothing has to cross between parts.
All inputs are finite; a program needn't handle non-finite values.
Results may differ from a plain program's by a relative error of at most 0.011.
Values may be sent and summed in bfloat16 or wider, within the bound.
No kernel may reach another device: no remote copies, remote signals or barrier semaphores. Data moves between devices by JAX's collectives and lax.ppermute only.
A program may use at most 64 MiB of HBM per device.

v0:
```python
import math

import jax
import jax.numpy as jnp
from jax import lax
from jax.sharding import PartitionSpec as P

HEAD_DIM = 128
TAPS = 128
RADIX = 128


HIGHEST = lax.Precision.HIGHEST


def shifted(value, axis, steps):
    count = lax.axis_size(axis)
    initial, last = (max(0, -steps), min(count, count - steps))
    return lax.ppermute(value, axis, [(source, source + steps) for source in range(initial, last)])


def unit_table(height, breadth, modulus, orient):
    product = (
        lax.broadcasted_iota(jnp.int32, (height, breadth), 0)
        * lax.broadcasted_iota(jnp.int32, (height, breadth), 1)
        % modulus
    )
    angles = 2.0 * math.pi / modulus * product.astype(jnp.float32)
    return (jnp.cos(angles), orient * jnp.sin(angles))


def block_table(factor, orient):
    inner_re, inner_im = unit_table(factor, factor, factor, orient)
    upper = jnp.concatenate([inner_re, inner_im], axis=1)
    lower = jnp.concatenate([-inner_im, inner_re], axis=1)
    return jnp.concatenate([upper, lower], axis=0)


def spectrum(signal, factor):
    channels, length = signal.shape
    full_length = 2 * length
    column_count = full_length // factor
    folded = signal.reshape(channels, column_count // 2, factor)
    outer_re, outer_im = unit_table(column_count, column_count // 2, column_count, -1.0)
    outer_both = jnp.concatenate([outer_re, outer_im], axis=0)
    first = jnp.einsum("kn,cnm->ckm", outer_both, folded, precision=HIGHEST)
    first_re = first[:, :column_count]
    first_im = first[:, column_count:]
    twist_re, twist_im = unit_table(column_count, factor, full_length, -1.0)
    mid_re = first_re * twist_re - first_im * twist_im
    mid_im = first_re * twist_im + first_im * twist_re
    joined = jnp.concatenate([mid_re, mid_im], axis=2)
    return jnp.einsum("ckn,nm->ckm", joined, block_table(factor, -1.0), precision=HIGHEST)


def inverse(spec_both, factor, length):
    channels = spec_both.shape[0]
    full_length = 2 * length
    column_count = full_length // factor
    mid = jnp.einsum("ckm,mn->ckn", spec_both, block_table(factor, 1.0), precision=HIGHEST)
    mid_re = mid[:, :, :factor]
    mid_im = mid[:, :, factor:]
    twist_re, twist_im = unit_table(column_count, factor, full_length, 1.0)
    turn_re = mid_re * twist_re - mid_im * twist_im
    turn_im = mid_re * twist_im + mid_im * twist_re
    outer_re, outer_im = unit_table(column_count // 2, column_count, column_count, 1.0)
    outer_both = jnp.concatenate([outer_re, -outer_im], axis=1)
    turned = jnp.concatenate([turn_re, turn_im], axis=1)
    result = jnp.einsum("nk,ckm->cnm", outer_both, turned, precision=HIGHEST)
    return result.reshape(channels, length) / full_length


def shards(
    gate_input, value_input, short_filter, long_filter, query_weight, key_matrix, value_matrix
):
    seq_rows, local_width = gate_input.shape
    last_rows = gate_input[seq_rows - (TAPS - 1) :]
    earlier = shifted(last_rows, "seq", 1)
    padded = jnp.concatenate([earlier, gate_input], axis=0).astype(jnp.float32)
    kernel = short_filter[:, ::-1].T[:, None, :]
    smoothed = lax.conv_general_dilated(
        padded[None],
        kernel,
        (1,),
        "VALID",
        dimension_numbers=("NHC", "HIO", "NHC"),
        feature_group_count=local_width,
        precision=HIGHEST,
    )[0]
    mixed_input = (smoothed * value_input.astype(jnp.float32)).astype(jnp.bfloat16)
    signal, kernel_line = (
        lax.all_to_all(mixed_input.T, "seq", split_axis=0, concat_axis=1, tiled=True),
        lax.all_to_all(long_filter.T, "seq", split_axis=0, concat_axis=1, tiled=True),
    )
    length = signal.shape[1]
    signal_both = spectrum(signal.astype(jnp.float32), RADIX)
    kernel_both = spectrum(kernel_line.astype(jnp.float32), RADIX)
    signal_re = signal_both[:, :, :RADIX]
    signal_im = signal_both[:, :, RADIX:]
    kernel_re = kernel_both[:, :, :RADIX]
    kernel_im = kernel_both[:, :, RADIX:]
    joint = jnp.concatenate(
        [
            signal_re * kernel_re - signal_im * kernel_im,
            signal_re * kernel_im + signal_im * kernel_re,
        ],
        axis=2,
    )
    conv_line = inverse(joint, RADIX, length).astype(jnp.bfloat16)
    my_index = lax.axis_index("seq")
    group_firsts = [my_index * seq_rows]
    conv_columns = lax.all_to_all(conv_line, "seq", split_axis=1, concat_axis=0, tiled=True)
    heads_here = local_width // HEAD_DIM
    conv_heads = conv_columns.reshape(heads_here, HEAD_DIM, seq_rows)
    query_heads = jnp.einsum(
        "hds,hde->hse", conv_heads, query_weight, preferred_element_type=jnp.float32
    ).astype(jnp.bfloat16)
    group_count = len(group_firsts)
    query_groups = [query_heads]
    key_heads = key_matrix.reshape(seq_rows, heads_here, HEAD_DIM).transpose(1, 0, 2)
    value_heads = value_matrix.reshape(seq_rows, heads_here, HEAD_DIM).transpose(1, 0, 2)
    score_scale = 1.0 / math.sqrt(HEAD_DIM)

    def attend_group(running, group_query, group_first, key_block, value_block, first_row):
        block_rows = key_block.shape[1]

        def compute(current):
            peak_value, weight_sum, weighted = current
            scores = (
                jnp.einsum(
                    "hqd,hkd->hqk", group_query, key_block, preferred_element_type=jnp.float32
                )
                * score_scale
            )
            key_pos = first_row + lax.iota(jnp.int32, block_rows)
            query_pos = group_first + lax.iota(jnp.int32, seq_rows)
            allowed = (key_pos[None, :] <= query_pos[:, None])[None]
            scores = jnp.where(allowed, scores, -1e30)
            new_peak = jnp.maximum(peak_value, jnp.max(scores, axis=2))
            weights = jnp.where(allowed, jnp.exp(scores - new_peak[:, :, None]), 0.0)
            rescale = jnp.exp(peak_value - new_peak)
            weight_sum = weight_sum * rescale + jnp.sum(weights, axis=2)
            weighted = weighted * rescale[:, :, None] + jnp.einsum(
                "hqk,hkd->hqd",
                weights.astype(jnp.bfloat16),
                value_block,
                preferred_element_type=jnp.float32,
            )
            return (new_peak, weight_sum, weighted)

        live = first_row <= group_first + seq_rows - 1
        return lax.cond(live, compute, lambda current: current, running)

    def attend(states, key_block, value_block, first_row):
        return tuple(
            (
                attend_group(
                    states[g], query_groups[g], group_firsts[g], key_block, value_block, first_row
                )
                for g in range(group_count)
            )
        )

    one_state = (
        jnp.full((heads_here, seq_rows), -1e30, jnp.float32),
        jnp.zeros((heads_here, seq_rows), jnp.float32),
        jnp.zeros((heads_here, seq_rows, HEAD_DIM), jnp.float32),
    )
    initial = tuple((one_state for g in range(group_count)))
    running = initial
    key_piece = lax.all_gather(key_heads, "seq", axis=1, tiled=True)
    value_piece = lax.all_gather(value_heads, "seq", axis=1, tiled=True)
    piece_rows = key_piece.shape[1]
    block_rows = 512
    block_count = piece_rows // block_rows
    key_blocks = key_piece.reshape(heads_here, block_count, block_rows, HEAD_DIM).transpose(
        1, 0, 2, 3
    )
    value_blocks = value_piece.reshape(heads_here, block_count, block_rows, HEAD_DIM).transpose(
        1, 0, 2, 3
    )

    def advance(current, element):
        key_block, value_block, position = element
        return (attend(current, key_block, value_block, position * block_rows), None)

    running, _ = lax.scan(
        advance, running, (key_blocks, value_blocks, lax.iota(jnp.int32, block_count))
    )
    outputs = [state[2] / state[1][:, :, None] for state in running]
    result = outputs[0]
    attended_rows = result.transpose(1, 0, 2).reshape(seq_rows, local_width).astype(jnp.bfloat16)
    return attended_rows


def solution(mesh):
    in_specs = (
        P(("groups", "seq"), "chan"),
        P(("groups", "seq"), "chan"),
        P("chan", None),
        P("seq", "chan"),
        P("chan", None, None),
        P(("groups", "seq"), "chan"),
        P(("groups", "seq"), "chan"),
    )
    out_specs = P(("groups", "seq"), "chan")
    return jax.shard_map(shards, mesh=mesh, in_specs=in_specs, out_specs=out_specs, check_vma=False)
```

profile of v0, /device:TPU:0, one launch (start us, length us, event | category | flops | bytes accessed | tf_op | source)
XLA Modules:
  0.0 73.8 jit_solution(403984494626430761)
XLA Ops:
  6.5 1.9 %copy.49 = bf16[128,1024]{0,1:T(8,128)(2,1)} copy(bf16[128,1024]{1,0:T(8,128)(2,1)} %param.14) | data formatting | bytes 524288 | tf_op args[5]
  8.5 1.0 %slice.33 = bf16[127,1024]{1,0:T(8,128)(2,1)S(1)} slice(bf16[128,1024]{1,0:T(8,128)(2,1)} %param.9), slice={[1:128], [0:1024]} | slice | bytes 520192 | tf_op jit(solution)/shard_map/slice | solution.py:77
  9.5 2.5 %collective-permute-start = (bf16[127,1024]{1,0:T(8,128)(2,1)S(1)}, bf16[127,1024]{1,0:T(8,128)(2,1)S(1)}, u32[]{:S(2)}, u32[]{:S(2)}) collective-permute-start(bf16[127,1024]{1,0:T(8,128)(2,1)S(1)} %slice.33), channel_id=1, source_target_pairs={{0,4},{4,8},{8,12},{1,5},{5,9},{9,13},{2,6},{6,10},{10,14},{3,7},{... | collective-permute-start | bytes 780296 | tf_op jit(solution)/shard_map/ppermute | solution.py:19
  12.0 1.8 %copy.40 = bf16[128,1024]{0,1:T(8,128)(2,1)} copy(bf16[128,1024]{1,0:T(8,128)(2,1)} %param.12) | data formatting | bytes 524288 | tf_op args[3]
  13.8 3.9 %all-to-all-start.1 = ((bf16[4,256,128]{2,1,0:T(8,128)(2,1)}), bf16[4,256,128]{2,1,0:T(8,128)(2,1)S(1)}, u32[]{:S(2)}, u32[]{:S(2)}) async-start(bf16[4,256,128]{2,1,0:T(8,128)(2,1)} %bitcast.10), calls=%async_computation.1 | async-start | bytes 524288 | tf_op jit(solution)/shard_map/all_to_all | solution.py:93
  17.7 0.8 %copy.50 = bf16[128,1024]{0,1:T(8,128)(2,1)} copy(bf16[128,1024]{1,0:T(8,128)(2,1)S(1)} %copy-done.3) | data formatting | bytes 524288 | tf_op args[6]
  20.8 5.6 %fusion.29 = f32[1,128,1024]{2,0,1:T(1,128)S(1)} fusion(f32[128,1,1024]{2,1,0:T(1,128)S(1)} %copy.36, bf16[1,255,1024]{2,1,0:T(8,128)(2,1)S(1)} %maximum_bitcast_fusion), kind=kOutput, calls=%fused_computation.44 | convolution fusion | flops 201326592 | bytes 1570816 | tf_op jit(solution)/shard_map/conv_general_dilated | solution.py:81
  26.6 0.8 %copy.60 = bf16[1024,128]{1,0:T(8,128)(2,1)} copy(bf16[1024,128]{0,1:T(8,128)(2,1)S(1)} %fusion.38) | data formatting | bytes 524288 | tf_op jit(solution)/shard_map/all_to_all | solution.py:92
  27.5 3.6 %all-to-all-start = ((bf16[4,256,128]{2,1,0:T(8,128)(2,1)}), bf16[4,256,128]{2,1,0:T(8,128)(2,1)S(1)}, u32[]{:S(2)}, u32[]{:S(2)}) async-start(bf16[4,256,128]{2,1,0:T(8,128)(2,1)} %bitcast.4), calls=%async_computation | async-start | bytes 524288 | tf_op jit(solution)/shard_map/all_to_all | solution.py:92
  31.0 1.1 %convolution_bitcast_fusion = f32[256,16,128]{2,1,0:T(8,128)S(1)} fusion(bf16[4,256,128]{2,1,0:T(8,128)(2,1)S(1)} %all-to-all-done.1, f32[8,4]{0,1:T(4,128)S(1)} %get-tuple-element.115, f32[8,4]{0,1:T(4,128)S(1)} %get-tuple-element.116), kind=kOutput, calls=%fused_computation.30 | convolution fusion | flops 25165888 | bytes 2359552 | tf_op jit(solution)/shard_map/kn,cnm->ckm/dot_general | solution.py:46
  32.2 4.9 %all-to-all-done = bf16[4,256,128]{2,1,0:T(8,128)(2,1)S(1)} async-done(((bf16[4,256,128]{2,1,0:T(8,128)(2,1)}), bf16[4,256,128]{2,1,0:T(8,128)(2,1)S(1)}, u32[]{:S(2)}, u32[]{:S(2)}) %all-to-all-start) | async-done | bytes 262176 | tf_op jit(solution)/shard_map/all_to_all | solution.py:92
  37.1 1.1 %convolution_bitcast_fusion.1 = f32[256,16,128]{2,1,0:T(8,128)S(1)} fusion(bf16[4,256,128]{2,1,0:T(8,128)(2,1)S(1)} %all-to-all-done, f32[8,4]{0,1:T(4,128)S(1)} %get-tuple-element.115, f32[8,4]{0,1:T(4,128)S(1)} %get-tuple-element.116), kind=kOutput, calls=%fused_computation.31 | convolution fusion | flops 25165888 | bytes 2359552 | tf_op jit(solution)/shard_map/kn,cnm->ckm/dot_general | solution.py:46
  38.9 2.6 %fusion.18 = f32[256,8,256]{0,2,1:T(8,128)S(1)} fusion(f32[256,8,256]{2,1,0:T(8,128)S(1)} %pad_maximum_fusion, f32[128,128]{0,1:T(8,128)S(1)} %get-tuple-element.120, f32[128,128]{0,1:T(8,128)S(1)} %fusion.57, f32[128,128]{0,1:T(8,128)S(1)} %get-tuple-element.119), kind=kOutput, calls=%fused_computation.28 | convolution fusion | flops 1610809344 | bytes 4390912 | tf_op jit(solution)/shard_map/ckn,nm->ckm/dot_general | solution.py:53
  41.5 2.6 %fusion.16 = f32[256,8,256]{0,2,1:T(8,128)S(1)} fusion(f32[256,8,256]{2,1,0:T(8,128)S(1)} %pad_maximum_fusion.1, f32[128,128]{0,1:T(8,128)S(1)} %get-tuple-element.120, f32[128,128]{0,1:T(8,128)S(1)} %fusion.57, f32[128,128]{0,1:T(8,128)S(1)} %get-tuple-element.119), kind=kOutput, calls=%fused_computation.26 | convolution fusion | flops 1610809344 | bytes 4390912 | tf_op jit(solution)/shard_map/ckn,nm->ckm/dot_general | solution.py:53
  44.5 1.5 %pad_maximum_fusion.2 = f32[256,8,256]{0,2,1:T(8,128)} fusion(f32[256,8,128]{0,2,1:T(8,128)S(1)} %get-tuple-element.106, f32[256,8,128]{0,2,1:T(8,128)S(1)} %get-tuple-element.105), kind=kLoop, calls=%fused_computation.21 | loop fusion | flops 524288 | bytes 4194304 | tf_op jit(solution)/shard_map/concatenate | solution.py:102
  46.0 2.5 %copy.56 = f32[256,8,256]{2,1,0:T(8,128)S(1)} copy(f32[256,8,256]{0,2,1:T(8,128)} %pad_maximum_fusion.2) | data formatting | bytes 4194304 | tf_op jit(solution)/shard_map/concatenate | solution.py:102
  48.4 1.9 %fusion.36 = f32[256,8,256]{2,1,0:T(8,128)S(1)} fusion(f32[256,8,256]{2,1,0:T(8,128)S(1)} %copy.56, f32[128,128]{0,1:T(8,128)S(1)} %get-tuple-element.120, f32[128,128]{0,1:T(8,128)S(1)} %get-tuple-element.122, f32[128,128]{0,1:T(8,128)S(1)} %get-tuple-element.121), kind=kOutput, calls=%fused_computation.58 | convolution fusion | flops 1610809344 | bytes 4390912 | tf_op jit(solution)/shard_map/ckm,mn->ckn/dot_general | solution.py:60
  50.6 1.3 %fusion.26 = bf16[256,4,128]{2,1,0:T(4,128)(2,1)S(1)} fusion(f32[256,8,128]{2,1,0:T(8,128)S(1)} %get-tuple-element.108, f32[256,8,128]{2,1,0:T(8,128)S(1)} %get-tuple-element.107, f32[4,8]{1,0:T(4,128)S(1)} %get-tuple-element.123, f32[4,8]{1,0:T(4,128)S(1)} %get-tuple-element.124), kind=kOutput, calls=%fused_computation.35 | convolution fusion | flops 25952320 | bytes 2359552 | tf_op jit(solution)/shard_map/nk,ckm->cnm/dot_general | solution.py:69
  52.6 3.4 %all-to-all-start.2 = ((bf16[256,4,128]{2,0,1:T(8,128)(2,1)}), bf16[256,4,128]{2,0,1:T(8,128)(2,1)S(1)}, u32[]{:S(2)}, u32[]{:S(2)}) async-start(bf16[256,4,128]{2,0,1:T(8,128)(2,1)} %copy.47), calls=%async_computation.2 | async-start | bytes 524288 | tf_op jit(solution)/shard_map/all_to_all | solution.py:112
  56.0 5.9 %all-to-all-done.2 = bf16[256,4,128]{2,0,1:T(8,128)(2,1)S(1)} async-done(((bf16[256,4,128]{2,0,1:T(8,128)(2,1)}), bf16[256,4,128]{2,0,1:T(8,128)(2,1)S(1)}, u32[]{:S(2)}, u32[]{:S(2)}) %all-to-all-start.2) | async-done | bytes 262176 | tf_op jit(solution)/shard_map/all_to_all | solution.py:112
  62.3 3.8 %conditional.1 = ((f32[8,128]{1,0:T(8,128)S(1)}, f32[8,128,128]{2,1,0:T(8,128)S(1)})) conditional(s32[]{:T(128)} %convert_element_type.104, (f32[8,128]{1,0:T(8,128)S(1)}, f32[8,128,128]{2,1,0:T(8,128)S(1)}) %tuple.22, (s32[]{:T(128)}, bf16[8,128,128]{2,1,0:T(8,128)(2,1)S(1)}, bf16[8,512,128]{1,2,0:T(8,128)(2,1)}, f32[8,128]{1,0:T(8,128)S(1)}, ...), branch_computations={%region_0.1_spmd, %region_1.4_spmd} | conditional | flops 275582080 | bytes 14206008 | solution.py:152
  62.5 1.9 %fusion = (f32[8,128]{1,0:T(8,128)S(1)}, f32[8,128,512]{2,1,0:T(8,128)S(1)}) fusion(pred[128,512]{1,0:T(8,128)(4,1)S(1)} %iota_compare_fusion, bf16[8,128,128]{2,1,0:T(8,128)(2,1)S(1)} %get-tuple-element.81, bf16[8,512,128]{1,2,0:T(8,128)(2,1)} %get-tuple-element.97), kind=kOutput, calls=%fused_computation.2 | convolution fusion | flops 135789568 | bytes 3477504 | tf_op jit(solution)/shard_map/while/body/eval_jaxpr/cond/branch_1_fun/hqd,hkd->hqk/dot_general | solution.py:130
  65.1 1.0 %convolution_add_fusion = f32[8,128,128]{2,1,0:T(8,128)S(1)} fusion(bf16[8,512,128]{1,2,0:T(8,128)(2,1)S(1)} %copy-done.5, f32[8,128,512]{2,1,0:T(8,128)S(1)} %get-tuple-element.104, f32[8,128]{1,0:T(8,128)S(1)} %broadcast_maximum_fusion, pred[128,512]{1,0:T(8,128)(4,1)S(1)} %iota_compare_fusion, f32[8,128,128]{2,1,0:T(8,128)S(1)} %get-tuple-element.83, ...), kind=kOutput, calls=%fused_computation.5 | convolution fusion | flops 137101312 | bytes 4268032 | tf_op jit(solution)/shard_map/while/body/eval_jaxpr/cond/branch_1_fun/hqk,hkd->hqd/dot_general | solution.py:143
  66.1 0.9 %copy_bitcast_fusion = bf16[128,1024]{1,0:T(8,128)(2,1)} fusion(f32[8,128,128]{2,1,0:T(8,128)S(1)} %get-tuple-element.87, f32[8,128]{1,0:T(8,128)S(1)} %get-tuple-element.88), kind=kLoop, calls=%fused_computation.60 | loop fusion | flops 262144 | bytes 790528 | tf_op jit(solution)/shard_map/convert_element_type | solution.py:192
  (45 shorter events, 5.6 us)
Async XLA Ops:
  6.5 55.4 %copy-start = (bf16[8,128,128]{2,1,0:T(8,128)(2,1)S(1)}, bf16[8,128,128]{2,1,0:T(8,128)(2,1)}, u32[]{:S(2)}) copy-start(bf16[8,128,128]{2,1,0:T(8,128)(2,1)} %param.13) | copy-start | bytes 786436
  6.5 11.1 %copy-start.3 = (bf16[128,1024]{1,0:T(8,128)(2,1)S(1)}, bf16[128,1024]{1,0:T(8,128)(2,1)}, u32[]{:S(2)}) copy-start(bf16[128,1024]{1,0:T(8,128)(2,1)} %param.15) | copy-start | bytes 786436
  6.5 12.5 %copy-start.2 = (f32[1024,128]{1,0:T(8,128)S(1)}, f32[1024,128]{1,0:T(8,128)}, u32[]{:S(2)}) copy-start(f32[1024,128]{1,0:T(8,128)} %param.11) | copy-start | bytes 1572868
  6.5 55.7 %all-gather.3.cloned.1.call-start = ((), (), s32[]{:S(2)}) async-start(), calls=%async_computation.3 | async-start | bytes 1310720 | tf_op jit(solution)/shard_map/all_gather | solution.py:171
  9.5 11.3 %copy-start.1 = (bf16[128,1024]{1,0:T(8,128)(2,1)S(1)}, bf16[128,1024]{1,0:T(8,128)(2,1)}, u32[]{:S(2)}) copy-start(bf16[128,1024]{1,0:T(8,128)(2,1)} %param.9) | copy-start | bytes 786436
  9.5 11.2 %collective-permute-start = (bf16[127,1024]{1,0:T(8,128)(2,1)S(1)}, bf16[127,1024]{1,0:T(8,128)(2,1)S(1)}, u32[]{:S(2)}, u32[]{:S(2)}) collective-permute-start(bf16[127,1024]{1,0:T(8,128)(2,1)S(1)} %slice.33), channel_id=1, source_target_pairs={{0,4},{4,8},{8,12},{1,5},{5,9},{9,13},{2,6},{6,10},{10,14},{3,7},{... | collective-permute-start | bytes 780296 | tf_op jit(solution)/shard_map/ppermute | solution.py:19
  13.8 13.7 %all-to-all-start.1 = ((bf16[4,256,128]{2,1,0:T(8,128)(2,1)}), bf16[4,256,128]{2,1,0:T(8,128)(2,1)S(1)}, u32[]{:S(2)}, u32[]{:S(2)}) async-start(bf16[4,256,128]{2,1,0:T(8,128)(2,1)} %bitcast.10), calls=%async_computation.1 | async-start | bytes 524288 | tf_op jit(solution)/shard_map/all_to_all | solution.py:93
  17.7 44.6 %all-gather.5.cloned.1.call-start = ((), (), s32[]{:S(2)}) async-start(), calls=%async_computation.4 | async-start | bytes 1310720 | tf_op jit(solution)/shard_map/all_gather | solution.py:172
  20.8 5.6 %copy-start.4 = (bf16[128,1024]{1,0:T(8,128)(2,1)S(1)}, bf16[128,1024]{1,0:T(8,128)(2,1)}, u32[]{:S(2)}) copy-start(bf16[128,1024]{1,0:T(8,128)(2,1)} %param.10) | copy-start | bytes 786436
  27.5 9.6 %all-to-all-start = ((bf16[4,256,128]{2,1,0:T(8,128)(2,1)}), bf16[4,256,128]{2,1,0:T(8,128)(2,1)S(1)}, u32[]{:S(2)}, u32[]{:S(2)}) async-start(bf16[4,256,128]{2,1,0:T(8,128)(2,1)} %bitcast.4), calls=%async_computation | async-start | bytes 524288 | tf_op jit(solution)/shard_map/all_to_all | solution.py:92
  52.6 9.4 %all-to-all-start.2 = ((bf16[256,4,128]{2,0,1:T(8,128)(2,1)}), bf16[256,4,128]{2,0,1:T(8,128)(2,1)S(1)}, u32[]{:S(2)}, u32[]{:S(2)}) async-start(bf16[256,4,128]{2,0,1:T(8,128)(2,1)} %copy.47), calls=%async_computation.2 | async-start | bytes 524288 | tf_op jit(solution)/shard_map/all_to_all | solution.py:112
  62.4 2.6 %copy-start.5 = (bf16[8,512,128]{1,2,0:T(8,128)(2,1)S(1)}, bf16[8,512,128]{1,2,0:T(8,128)(2,1)}, u32[]{:S(2)}) copy-start(bf16[8,512,128]{1,2,0:T(8,128)(2,1)} %get-tuple-element.100) | copy-start | bytes 3145732 | tf_op jit(solution)/shard_map/while/body/eval_jaxpr/cond
Sparse Core Ops, SparseCore 0:
  8.9 21.9 all-gather.2
  32.5 17.2 all-gather.4
where the time goes:
time: 74.4 us; the launch traced here: 73.8 us
  matrix products  19.4 us (26%)
  between operations  13.7 us (18%)
  starting transfers between devices  13.4 us (18%)
  waiting for transfers between devices  10.9 us (15%)
  local copies, waits for them, and re-layouts  10.8 us (15%)
  other arithmetic  5.68 us (8%)
    all_to_all x1, waiting for transfers between devices, shards(): lax.all_to_all(conv_line, 'seq', split_axis=1, concat_axis=0, tiled=True)  5.94 us
    conv_general_dilated x1, matrix products, shards(): lax.conv_general_dilated(padded[None], kernel, (1,), 'VALID', dimension_n...  5.61 us
    dot_general x2, matrix products, spectrum(): jnp.einsum('ckn,nm->ckm', joined, block_table(factor, -1.0), precision=HI...  5.23 us
    all_to_all x1, waiting for transfers between devices, shards(): lax.all_to_all(mixed_input.T, 'seq', split_axis=0, concat_axis=1, tiled=T...  4.85 us
    unnamed x13, local copies, waits for them, and re-layouts  4.55 us
    all_to_all x1, starting transfers between devices, shards(): lax.all_to_all(long_filter.T, 'seq', split_axis=0, concat_axis=1, tiled=T...  3.86 us
    all_to_all x1, starting transfers between devices, shards(): lax.all_to_all(mixed_input.T, 'seq', split_axis=0, concat_axis=1, tiled=T...  3.59 us
    all_to_all x1, starting transfers between devices, shards(): lax.all_to_all(conv_line, 'seq', split_axis=1, concat_axis=0, tiled=True)  3.41 us
  transfers between devices with their start and end apart: 6, of which 2 were waited for; matrix products, arithmetic and copies ran while one was open for 40% of the time, Pallas kernels for 0%

commit v1 on v0

--- a/solution.py
+++ b/solution.py
@@ -1,8 +1,13 @@
+import functools
 import math
 
 import jax
 import jax.numpy as jnp
+import ml_dtypes
+import numpy as np
 from jax import lax
+from jax.experimental import pallas as pl
+from jax.experimental.pallas import tpu as pltpu
 from jax.sharding import PartitionSpec as P
 
 HEAD_DIM = 128
@@ -70,7 +75,7 @@
     return result.reshape(channels, length) / full_length
 
 
-def shards(
+def general_shards(
     gate_input, value_input, short_filter, long_filter, query_weight, key_matrix, value_matrix
 ):
     seq_rows, local_width = gate_input.shape
@@ -193,6 +198,248 @@
     return attended_rows
 
 
+def block_tables(block):
+    angle = np.pi / block * (np.arange(block) + 0.5)
+    window = angle[:, None] * (np.arange(2 * block) - block)[None]
+    ahead = np.concatenate([np.cos(window), -np.sin(window)], axis=0)
+    inner = np.arange(block)[:, None] * angle[None]
+    back = np.concatenate([np.cos(inner), -np.sin(inner)], axis=1) / block
+
+    def pair(table):
+        high = table.astype(ml_dtypes.bfloat16)
+        rest = (table - high.astype(np.float64)).astype(ml_dtypes.bfloat16)
+        return np.concatenate([high, rest], axis=0)
+
+    return pair(ahead), pair(back)
+
+
+def two_parts(value):
+    high = value.astype(jnp.bfloat16)
+    return high, (value - high.astype(jnp.float32)).astype(jnp.bfloat16)
+
+
+def mxu(left, right):
+    return jnp.dot(left, right, preferred_element_type=jnp.float32)
+
+
+def folded_sum(stacked):
+    half = stacked.shape[0] // 2
+    return stacked[:half] + stacked[half:]
+
+
+def to_block(back, spec_re, spec_im, block):
+    re_high, re_rest = two_parts(spec_re)
+    im_high, im_rest = two_parts(spec_im)
+    main = mxu(back[:, :block], re_high) + mxu(back[:, block:], im_high)
+    small = mxu(back[:block, :block], re_rest) + mxu(back[:block, block:], im_rest)
+    return folded_sum(main) + small
+
+
+def conv_kernel(
+    place_ref, gate_ref, value_ref, filter_ref, *rest, count, block, head_dim
+):
+    arrived = rest[: count - 1]
+    taps_ref, weight_ref, ahead_ref, back_ref, query_ref = rest[count - 1 : count + 4]
+    gate_all, value_all, filter_all = rest[count + 4 :]
+    here = place_ref[0]
+    gate_all[0] = jnp.zeros_like(gate_ref)
+    filter_all[0] = jnp.zeros_like(filter_ref)
+    gate_all[here + 1] = gate_ref[...]
+    value_all[here] = value_ref[...]
+    filter_all[here + 1] = filter_ref[...]
+    for step, piece in enumerate(arrived, 1):
+        source = here ^ step
+        gate_all[source + 1] = piece[0]
+        value_all[source] = piece[1]
+        filter_all[source + 1] = piece[2]
+    ahead = ahead_ref[...]
+    first = ahead[:, block:]
+    back = back_ref[...]
+    turned = (((1,), (1,)), ((), ()))
+    taps_high, taps_rest = two_parts(taps_ref[...])
+    taps_spec = folded_sum(
+        lax.dot_general(first, taps_high, turned, preferred_element_type=jnp.float32)
+    ) + lax.dot_general(
+        first[: 2 * block], taps_rest, turned, preferred_element_type=jnp.float32
+    )
+    taps_re, taps_im = taps_spec[:block], taps_spec[block:]
+    lines = []
+    kernels = []
+    heads = weight_ref.shape[0]
+    for b in range(count):
+        window = jnp.concatenate([gate_all[b], gate_all[b + 1]], axis=0)
+        gate_spec = folded_sum(mxu(ahead, window))
+        gate_re, gate_im = gate_spec[:block], gate_spec[block:]
+        smoothed = to_block(
+            back,
+            gate_re * taps_re - gate_im * taps_im,
+            gate_re * taps_im + gate_im * taps_re,
+            block,
+        )
+        mixed = (smoothed * value_all[b].astype(jnp.float32)).astype(jnp.bfloat16)
+        lines.append(folded_sum(mxu(first, mixed)))
+        kernels.append(
+            folded_sum(
+                mxu(ahead, jnp.concatenate([filter_all[b], filter_all[b + 1]], axis=0))
+            )
+        )
+    for b in range(count):
+        total_re, total_im = 0.0, 0.0
+        for j in range(b + 1):
+            line, kernel = lines[j], kernels[b - j]
+            line_re, line_im = line[:block], line[block:]
+            kernel_re, kernel_im = kernel[:block], kernel[block:]
+            total_re = total_re + (line_re * kernel_re - line_im * kernel_im)
+            total_im = total_im + (line_re * kernel_im + line_im * kernel_re)
+        conv_out = to_block(back, total_re, total_im, block).astype(jnp.bfloat16)
+        for h in range(heads):
+            columns = slice(h * head_dim, (h + 1) * head_dim)
+            query_ref[b, :, columns] = mxu(conv_out[:, columns], weight_ref[h]).astype(
+                jnp.bfloat16
+            )
+
+
+def attend_kernel(place_ref, query_ref, key_ref, value_ref, *rest, count, block, head_dim):
+    arrived = rest[: count - 1]
+    outs = rest[count - 1 : 2 * count - 1]
+    key_all, value_all, out_all = rest[2 * count - 1 :]
+    here = place_ref[0]
+    key_all[here] = key_ref[...]
+    value_all[here] = value_ref[...]
+    for step, piece in enumerate(arrived, 1):
+        key_all[here ^ step] = piece[0]
+        value_all[here ^ step] = piece[1]
+    width = query_ref.shape[2]
+    turned = (((1,), (1,)), ((), ()))
+    scale = 1.0 / math.sqrt(head_dim)
+    row = lax.broadcasted_iota(jnp.int32, (block, block), 0)
+    column = lax.broadcasted_iota(jnp.int32, (block, block), 1)
+    allowed = column <= row
+    for h in range(width // head_dim):
+        columns = slice(h * head_dim, (h + 1) * head_dim)
+        for b in range(count):
+            query = query_ref[b, :, columns]
+            scores = []
+            for j in range(b + 1):
+                part = (
+                    lax.dot_general(
+                        query,
+                        key_all[j, :, columns],
+                        turned,
+                        preferred_element_type=jnp.float32,
+                    )
+                    * scale
+                )
+                scores.append(jnp.where(allowed, part, -1e30) if j == b else part)
+            peak = functools.reduce(jnp.maximum, scores)
+            peak = jnp.max(peak, axis=1, keepdims=True)
+            weights = [jnp.exp(part - peak) for part in scores]
+            weights[b] = jnp.where(allowed, weights[b], 0.0)
+            weight_sum = jnp.sum(functools.reduce(jnp.add, weights), axis=1, keepdims=True)
+            total = functools.reduce(
+                jnp.add,
+                [
+                    mxu(weights[j].astype(jnp.bfloat16), value_all[j, :, columns])
+                    for j in range(b + 1)
+                ],
+            )
+            out_all[b, :, columns] = (total / weight_sum).astype(jnp.bfloat16)
+    for step, out in enumerate(outs):
+        out[...] = out_all[here ^ step]
+
+
+def join_kernel(place_ref, *rest):
+    pieces, out_ref = rest[:-1], rest[-1]
+    here = place_ref[0]
+    width = pieces[0].shape[1]
+    for step, piece in enumerate(pieces):
+        start = pl.multiple_of((here ^ step) * width, width)
+        out_ref[:, pl.ds(start, width)] = piece[...]
+
+
+WHOLE = pl.BlockSpec(memory_space=pltpu.VMEM)
+
+
+def head_shards(
+    gate_input, value_input, short_filter, long_filter, query_weight, key_matrix, value_matrix
+):
+    count = lax.axis_size("seq")
+    block, local_width = gate_input.shape
+    width = local_width // count
+    heads = width // HEAD_DIM
+    here = lax.axis_index("seq")
+    place = here.astype(jnp.int32).reshape(1)
+
+    def columns_of(value, owner):
+        return lax.dynamic_slice_in_dim(value, owner * width, width, axis=1)
+
+    def swap(value, step):
+        return lax.ppermute(value, "seq", [(i, i ^ step) for i in range(count)])
+
+    def swap_columns(arrays):
+        return [
+            swap(jnp.stack([columns_of(a, here ^ step) for a in arrays]), step)
+            for step in range(1, count)
+        ]
+
+    arrived = swap_columns([gate_input, value_input, long_filter])
+    arrived_later = swap_columns([key_matrix, value_matrix])
+    ahead, back = block_tables(block)
+    mine = pl.BlockSpec((block, width), lambda i, p: (0, p[0]))
+    scratch = lambda n: pltpu.VMEM((n, block, width), jnp.bfloat16)
+    params = pltpu.CompilerParams(vmem_limit_bytes=32 * 1024 * 1024)
+    queries = pl.pallas_call(
+        functools.partial(conv_kernel, count=count, block=block, head_dim=HEAD_DIM),
+        out_shape=jax.ShapeDtypeStruct((count, block, width), jnp.bfloat16),
+        grid_spec=pltpu.PrefetchScalarGridSpec(
+            num_scalar_prefetch=1,
+            grid=(1,),
+            in_specs=[mine] * 3
+            + [WHOLE] * (count - 1)
+            + [
+                pl.BlockSpec((width, TAPS), lambda i, p: (p[0], 0)),
+                pl.BlockSpec((heads, HEAD_DIM, HEAD_DIM), lambda i, p: (p[0], 0, 0)),
+            ]
+            + [WHOLE] * 2,
+            out_specs=WHOLE,
+            scratch_shapes=[scratch(count + 1), scratch(count), scratch(count + 1)],
+        ),
+        compiler_params=params,
+    )(
+        place, gate_input, value_input, long_filter, *arrived, short_filter, query_weight,
+        jnp.asarray(ahead), jnp.asarray(back),
+    )
+    pieces = pl.pallas_call(
+        functools.partial(attend_kernel, count=count, block=block, head_dim=HEAD_DIM),
+        out_shape=[jax.ShapeDtypeStruct((block, width), jnp.bfloat16)] * count,
+        grid_spec=pltpu.PrefetchScalarGridSpec(
+            num_scalar_prefetch=1,
+            grid=(1,),
+            in_specs=[WHOLE] + [mine] * 2 + [WHOLE] * (count - 1),
+            out_specs=[WHOLE] * count,
+            scratch_shapes=[scratch(count)] * 3,
+        ),
+        compiler_params=params,
+    )(place, queries, key_matrix, value_matrix, *arrived_later)
+    pieces = [pieces[0]] + [swap(pieces[step], step) for step in range(1, count)]
+    return pl.pallas_call(
+        join_kernel,
+        out_shape=jax.ShapeDtypeStruct((block, local_width), jnp.bfloat16),
+        in_specs=[pl.BlockSpec(memory_space=pltpu.SMEM)] + [WHOLE] * count,
+        out_specs=WHOLE,
+        compiler_params=params,
+    )(place, *pieces)
+
+
+def shards(*arrays):
+    count = lax.axis_size("seq")
+    block, local_width = arrays[0].shape
+    even = local_width % (count * HEAD_DIM) == 0
+    if even and count & (count - 1) == 0 and block == TAPS:
+        return head_shards(*arrays)
+    return general_shards(*arrays)
+
+
 def solution(mesh):
     in_specs = (
         P(("groups", "seq"), "chan"),

time: 74.4 us -> 29.5 us (0.40)
  matrix products: 19.4 us -> 0 us
  between operations: 13.7 us -> 0.15 us
  local copies, waits for them, and re-layouts: 10.8 us -> 2.08 us
  Pallas kernels: 0 us -> 7.01 us
  starting transfers between devices: 13.4 us -> 7.43 us
  other arithmetic: 5.68 us -> 0.12 us
  waiting for transfers between devices: 10.9 us -> 12.5 us
    dot_general x9 -> x0, matrix products: 13.8 us -> none  [the longest x2 5.23 us: spectrum(): jnp.einsum('ckn,nm->ckm', joined, block_table(factor, -1.0), precision=HI...]
    ppermute x1 -> x9, waiting for transfers between devices: 0.01 us -> 12.5 us  [swap(): return lax.ppermute(value, 'seq', [(i, i ^ step) for i in range(count)])]
    all_to_all x3 -> x0, starting transfers between devices: 10.9 us -> none  [the longest x1 3.86 us: shards(): lax.all_to_all(long_filter.T, 'seq', split_axis=0, concat_axis=1, tiled=T...]
    all_to_all x3 -> x0, waiting for transfers between devices: 10.8 us -> none  [the longest x1 5.94 us: shards(): lax.all_to_all(conv_line, 'seq', split_axis=1, concat_axis=0, tiled=True)]
    pallas_call x0 -> x3, Pallas kernels: none -> 7.01 us  [the longest x1 4.11 us: head_shards(): pl.pallas_call(functools.partial(conv_kernel, count=count, block=block, h...]
    conv_general_dilated x1 -> x0, matrix products: 5.61 us -> none  [shards(): lax.conv_general_dilated(padded[None], kernel, (1,), 'VALID', dimension_n...]
    ppermute x1 -> x9, starting transfers between devices: 2.5 us -> 7.43 us  [swap(): return lax.ppermute(value, 'seq', [(i, i ^ step) for i in range(count)])]
    unnamed x13 -> x18, local copies, waits for them, and re-layouts: 4.55 us -> 0.12 us
  transfers between devices with their start and end apart: 6 -> 9, of which waited for: 2 -> 5; matrix products, arithmetic and copies ran while one was open for 40% -> 1% of each run, Pallas kernels for 0% -> 14%
where the time goes in v1:
time: 29.5 us; the launch traced here: 29.3 us
  waiting for transfers between devices  12.5 us (42%)
  starting transfers between devices  7.43 us (25%)
  Pallas kernels  7.01 us (24%)
  local copies, waits for them, and re-layouts  2.08 us (7%)
    ppermute x9, waiting for transfers between devices, swap(): return lax.ppermute(value, 'seq', [(i, i ^ step) for i in range(count)])  12.5 us
    ppermute x9, starting transfers between devices, swap(): return lax.ppermute(value, 'seq', [(i, i ^ step) for i in range(count)])  7.43 us
    pallas_call x1, Pallas kernels, head_shards(): pl.pallas_call(functools.partial(conv_kernel, count=count, block=block, h...  4.11 us
    pallas_call x1, Pallas kernels, head_shards(): pl.pallas_call(functools.partial(attend_kernel, count=count, block=block,...  2.17 us
    another operation x3, local copies, waits for them, and re-layouts, swap_columns(): jnp.stack([columns_of(a, here ^ step) for a in arrays])  1.96 us
    pallas_call x1, Pallas kernels, head_shards(): pl.pallas_call(join_kernel, out_shape=jax.ShapeDtypeStruct((block, local_...  0.73 us
  transfers between devices with their start and end apart: 9, of which 5 were waited for; matrix products, arithmetic and copies ran while one was open for 1% of the time, Pallas kernels for 14%

profile of v1, /device:TPU:0, one launch (start us, length us, event | category | flops | bytes accessed | tf_op | source)
XLA Modules:
  0.0 29.3 jit_solution(15336743763563474524)
XLA Ops:
  0.0 1.0 %dynamic-slice_bitcast_fusion.8 = (bf16[1,128,256]{2,1,0:T(8,128)(2,1)S(1)}, bf16[1,128,256]{2,1,0:T(8,128)(2,1)S(1)}, bf16[1,128,256]{2,1,0:T(8,128)(2,1)S(1)}) fusion(bf16[128,1024]{1,0:T(8,128)(2,1)} %gate_ref.1, s32[]{:T(128)S(6)} %select_n.8, s32[]{:T(128)S(6)} %select_n.7, s32[]{:T(128)S(6)} %select_n.6), kind=kLoop, calls=%fused_computation.14 | loop fusion | bytes 393228 | tf_op jit(solution)/shard_map/stack | solution.py:381
  1.0 0.1 copy-done.1
  1.0 0.9 %dynamic-slice_bitcast_fusion.6 = (bf16[1,128,256]{2,1,0:T(8,128)(2,1)S(1)}, bf16[1,128,256]{2,1,0:T(8,128)(2,1)S(1)}, bf16[1,128,256]{2,1,0:T(8,128)(2,1)S(1)},...) fusion(bf16[128,1024]{1,0:T(8,128)(2,1)} %filter_ref.1, ...), kind=kLoop, calls=%fused_computation.12 | loop fusion | bytes 786444 | tf_op jit(solution)/shard_map/stack | solution.py:381
  2.0 0.5 %collective-permute-start = (bf16[3,128,256]{2,1,0:T(8,128)(2,1)S(1)}, bf16[3,128,256]{2,1,0:T(8,128)(2,1)S(1)}, u32[]{:S(2)}, u32[]{:S(2)}) collective-permute-start(bf16[3,128,256]{2,1,0:T(8,128)(2,1)S(1)} %pad_maximum_fusion), channel_id=1, source_target_pairs={{0,4},{4,0},{8,12},{12,8},{1,5},{5,1},{9,13},{13,9},{2,6},{6,2},{1... | collective-permute-start | bytes 589832 | tf_op jit(solution)/shard_map/ppermute | solution.py:377
  2.6 0.0 copy-start.3
  2.6 2.6 %collective-permute-start.1 = (bf16[3,128,256]{2,1,0:T(8,128)(2,1)S(1)}, bf16[3,128,256]{2,1,0:T(8,128)(2,1)S(1)}, u32[]{:S(2)}, u32[]{:S(2)}) collective-permute-start(bf16[3,128,256]{2,1,0:T(8,128)(2,1)S(1)} %pad_maximum_fusion.1), channel_id=1, source_target_pairs={{0,8},{4,12},{8,0},{12,4},{1,9},{5,13},{9,1},{13,5},{2,10},{6,14},... | collective-permute-start | bytes 589832 | tf_op jit(solution)/shard_map/ppermute | solution.py:377
  5.2 0.2 collective-permute-start.2
  5.4 0.1 dynamic-slice_bitcast_fusion
  5.5 0.0 copy-start.6
  5.5 0.2 collective-permute-start.3
  5.7 2.0 %collective-permute-start.4 = (bf16[2,128,256]{2,1,0:T(8,128)(2,1)S(1)}, bf16[2,128,256]{2,1,0:T(8,128)(2,1)S(1)}, u32[]{:S(2)}, u32[]{:S(2)}) collective-permute-start(bf16[2,128,256]{2,1,0:T(8,128)(2,1)S(1)} %pad_maximum_fusion.4), channel_id=1, source_target_pairs={{0,8},{4,12},{8,0},{12,4},{1,9},{5,13},{9,1},{13,5},{2,10},{6,14},... | collective-permute-start | bytes 393224 | tf_op jit(solution)/shard_map/ppermute | solution.py:377
  7.7 0.0 collective-permute-done.rest_0_
  7.7 0.1 collective-permute-start.5
  7.8 3.1 %collective-permute-done.1.rest_1_ = bf16[3,128,256]{2,1,0:T(8,128)(2,1)S(1)} collective-permute-done((bf16[3,128,256]{2,1,0:T(8,128)(2,1)S(1)}, bf16[3,128,256]{2,1,0:T(8,128)(2,1)S(1)}, u32[]{:S(2)}, u32[]{:S(2)}) %collective-permute-start.1) | collective-permute-done | bytes 196640 | tf_op jit(solution)/shard_map/ppermute | solution.py:377
  10.9 3.8 %collective-permute-done.2.rest_2_ = bf16[3,128,256]{2,1,0:T(8,128)(2,1)S(1)} collective-permute-done((bf16[3,128,256]{2,1,0:T(8,128)(2,1)S(1)}, bf16[3,128,256]{2,1,0:T(8,128)(2,1)S(1)}, u32[]{:S(2)}, u32[]{:S(2)}) %collective-permute-start.2) | collective-permute-done | bytes 196640 | tf_op jit(solution)/shard_map/ppermute | solution.py:377
  14.8 4.1 %shard_map.91.query_ref = bf16[4,128,256]{2,1,0:T(8,128)(2,1)S(1)} custom-call(s32[1]{0:T(128)} %bitcast.place_ref, bf16[128,1024]{1,0:T(8,128)(2,1)S(1)} %copy-done, bf16[128,1024]{1,0:T(8,128)(2,1)S(1)} %copy-done.1, bf16[128,1024]{1,0:T(8,128)(2,1)S(1)} %copy-done.2, bf16[3,128,256]{2,1,0:T(8,128)(2,1)S(1)} %collective-permute-done.rest_0_, ...), custom_call_target="tpu_custom_call" | custom-call | tf_op jit(solution)/shard_map/pallas_call | solution.py:391
  18.9 1.4 %collective-permute-done.5.rest_2_ = bf16[2,128,256]{2,1,0:T(8,128)(2,1)S(1)} collective-permute-done((bf16[2,128,256]{2,1,0:T(8,128)(2,1)S(1)}, bf16[2,128,256]{2,1,0:T(8,128)(2,1)S(1)}, u32[]{:S(2)}, u32[]{:S(2)}) %collective-permute-start.5) | collective-permute-done | bytes 131104 | tf_op jit(solution)/shard_map/ppermute | solution.py:377
  20.3 2.2 %shard_map.92 = (bf16[128,256]{1,0:T(8,128)(2,1)S(1)}, bf16[128,256]{1,0:T(8,128)(2,1)S(1)}, bf16[128,256]{1,0:T(8,128)(2,1)S(1)}, bf16[128,256]{1,0:T(8,128)(2,1)S(1)}) custom-call(s32[1]{0:T(128)} %bitcast.place_ref, bf16[4,128,256]{2,1,0:T(8,128)(2,1)S(1)} %shard_map.91.query_ref, bf16[128,1024]{1,0:T(8,128)(2,1)S(1)} %copy-done.3, ...), custom_call_target="tpu_custom_call" | custom-call | tf_op jit(solution)/shard_map/pallas_call | solution.py:412
  22.5 0.2 collective-permute-start.6
  22.7 1.7 %collective-permute-start.7 = (bf16[128,256]{1,0:T(8,128)(2,1)S(1)}, bf16[128,256]{1,0:T(8,128)(2,1)S(1)}, u32[]{:S(2)}, u32[]{:S(2)}) collective-permute-start(bf16[128,256]{1,0:T(8,128)(2,1)S(1)} %get-tuple-element.11), channel_id=1, source_target_pairs={{0,8},{4,12},{8,0},{12,4},{1,9},{5,13},{9,1},{13,5},{2,10},{6,14},... | collective-permute-start | bytes 196616 | tf_op jit(solution)/shard_map/ppermute | solution.py:377
  24.4 0.1 collective-permute-start.8
  24.4 2.6 %collective-permute-done.7.rest_2_ = bf16[128,256]{1,0:T(8,128)(2,1)S(1)} collective-permute-done((bf16[128,256]{1,0:T(8,128)(2,1)S(1)}, bf16[128,256]{1,0:T(8,128)(2,1)S(1)}, u32[]{:S(2)}, u32[]{:S(2)}) %collective-permute-start.7) | collective-permute-done | bytes 65568 | tf_op jit(solution)/shard_map/ppermute | solution.py:377
  27.1 1.5 %collective-permute-done.8.rest_3_ = bf16[128,256]{1,0:T(8,128)(2,1)S(1)} collective-permute-done((bf16[128,256]{1,0:T(8,128)(2,1)S(1)}, bf16[128,256]{1,0:T(8,128)(2,1)S(1)}, u32[]{:S(2)}, u32[]{:S(2)}) %collective-permute-start.8) | collective-permute-done | bytes 65568 | tf_op jit(solution)/shard_map/ppermute | solution.py:377
  28.6 0.7 %shard_map.93 = bf16[128,1024]{1,0:T(8,128)(2,1)} custom-call(s32[1]{0:T(128)} %bitcast.place_ref, bf16[128,256]{1,0:T(8,128)(2,1)S(1)} %get-tuple-element.9.rest_0_, bf16[128,256]{1,0:T(8,128)(2,1)S(1)} %collective-permute-done.6.rest_1_, bf16[128,256]{1,0:T(8,128)(2,1)S(1)} %collective-permute-done.7.rest_2_, ...), custom_call_target="tpu_custom_call" | custom-call | tf_op jit(solution)/shard_map/pallas_call | solution.py:425
  (24 shorter events, 0.2 us)
Async XLA Ops:
  0.0 1.0 %copy-start.1 = (bf16[128,1024]{1,0:T(8,128)(2,1)S(1)}, bf16[128,1024]{1,0:T(8,128)(2,1)}, u32[]{:S(2)}) copy-start(bf16[128,1024]{1,0:T(8,128)(2,1)} %value_ref.2) | copy-start | bytes 786436
  2.0 5.7 %collective-permute-start = (bf16[3,128,256]{2,1,0:T(8,128)(2,1)S(1)}, bf16[3,128,256]{2,1,0:T(8,128)(2,1)S(1)}, u32[]{:S(2)}, u32[]{:S(2)}) collective-permute-start(bf16[3,128,256]{2,1,0:T(8,128)(2,1)S(1)} %pad_maximum_fusion), channel_id=1, source_target_pairs={{0,4},{4,0},{8,12},{12,8},{1,5},{5,1},{9,13},{13,9},{2,6},{6,2},{1... | collective-permute-start | bytes 589832 | tf_op jit(solution)/shard_map/ppermute | solution.py:377
  2.5 2.8 %copy-start.4 = (bf16[128,1024]{1,0:T(8,128)(2,1)S(1)}, bf16[128,1024]{1,0:T(8,128)(2,1)}, u32[]{:S(2)}) copy-start(bf16[128,1024]{1,0:T(8,128)(2,1)} %value_ref.3) | copy-start | bytes 786436
  2.6 2.8 %copy-start.3 = (bf16[128,1024]{1,0:T(8,128)(2,1)S(1)}, bf16[128,1024]{1,0:T(8,128)(2,1)}, u32[]{:S(2)}) copy-start(bf16[128,1024]{1,0:T(8,128)(2,1)} %key_ref.1) | copy-start | bytes 786436
  2.6 8.3 %collective-permute-start.1 = (bf16[3,128,256]{2,1,0:T(8,128)(2,1)S(1)}, bf16[3,128,256]{2,1,0:T(8,128)(2,1)S(1)}, u32[]{:S(2)}, u32[]{:S(2)}) collective-permute-start(bf16[3,128,256]{2,1,0:T(8,128)(2,1)S(1)} %pad_maximum_fusion.1), channel_id=1, source_target_pairs={{0,8},{4,12},{8,0},{12,4},{1,9},{5,13},{9,1},{13,5},{2,10},{6,14},... | collective-permute-start | bytes 589832 | tf_op jit(solution)/shard_map/ppermute | solution.py:377
  5.2 9.5 %copy-start.8 = (bf16[256,256]{1,0:T(8,128)(2,1)S(1)}, bf16[256,256]{1,0:T(8,128)(2,1)}, u32[]{:S(2)}) copy-start(bf16[256,256]{1,0:T(8,128)(2,1)} %constant.22.clone.rest_6_) | copy-start | bytes 393220
  5.2 9.5 %collective-permute-start.2 = (bf16[3,128,256]{2,1,0:T(8,128)(2,1)S(1)}, bf16[3,128,256]{2,1,0:T(8,128)(2,1)S(1)}, u32[]{:S(2)}, u32[]{:S(2)}) collective-permute-start(bf16[3,128,256]{2,1,0:T(8,128)(2,1)S(1)} %pad_maximum_fusion.2), channel_id=1, source_target_pairs={{0,12},{4,8},{8,4},{12,0},{1,13},{5,9},{9,5},{13,1},{2,14},{6,10},... | collective-permute-start | bytes 589832 | tf_op jit(solution)/shard_map/ppermute | solution.py:377
  5.4 9.3 %copy-start.5 = (f32[1024,128]{1,0:T(8,128)S(1)}, f32[1024,128]{1,0:T(8,128)}, u32[]{:S(2)}) copy-start(f32[1024,128]{1,0:T(8,128)} %rest_3_.1) | copy-start | bytes 1572868
  5.4 9.3 %copy-start.7 = (bf16[512,256]{1,0:T(8,128)(2,1)S(1)}, bf16[512,256]{1,0:T(8,128)(2,1)}, u32[]{:S(2)}) copy-start(bf16[512,256]{1,0:T(8,128)(2,1)} %constant.21.clone.rest_5_) | copy-start | bytes 786436
  5.5 9.3 %copy-start.6 = (bf16[8,128,128]{2,1,0:T(8,128)(2,1)S(1)}, bf16[8,128,128]{2,1,0:T(8,128)(2,1)}, u32[]{:S(2)}) copy-start(bf16[8,128,128]{2,1,0:T(8,128)(2,1)} %rest_4_.1) | copy-start | bytes 786436
  5.5 13.4 %collective-permute-start.3 = (bf16[2,128,256]{2,1,0:T(8,128)(2,1)S(1)}, bf16[2,128,256]{2,1,0:T(8,128)(2,1)S(1)}, u32[]{:S(2)}, u32[]{:S(2)}) collective-permute-start(bf16[2,128,256]{2,1,0:T(8,128)(2,1)S(1)} %pad_maximum_fusion.3), channel_id=1, source_target_pairs={{0,4},{4,0},{8,12},{12,8},{1,5},{5,1},{9,13},{13,9},{2,6},{6,2},{1... | collective-permute-start | bytes 393224 | tf_op jit(solution)/shard_map/ppermute | solution.py:377
  5.7 9.0 %copy-start = (bf16[128,1024]{1,0:T(8,128)(2,1)S(1)}, bf16[128,1024]{1,0:T(8,128)(2,1)}, u32[]{:S(2)}) copy-start(bf16[128,1024]{1,0:T(8,128)(2,1)} %gate_ref.1) | copy-start | bytes 786436
  5.7 9.1 %copy-start.2 = (bf16[128,1024]{1,0:T(8,128)(2,1)S(1)}, bf16[128,1024]{1,0:T(8,128)(2,1)}, u32[]{:S(2)}) copy-start(bf16[128,1024]{1,0:T(8,128)(2,1)} %filter_ref.1) | copy-start | bytes 786436
  5.7 13.2 %collective-permute-start.4 = (bf16[2,128,256]{2,1,0:T(8,128)(2,1)S(1)}, bf16[2,128,256]{2,1,0:T(8,128)(2,1)S(1)}, u32[]{:S(2)}, u32[]{:S(2)}) collective-permute-start(bf16[2,128,256]{2,1,0:T(8,128)(2,1)S(1)} %pad_maximum_fusion.4), channel_id=1, source_target_pairs={{0,8},{4,12},{8,0},{12,4},{1,9},{5,13},{9,1},{13,5},{2,10},{6,14},... | collective-permute-start | bytes 393224 | tf_op jit(solution)/shard_map/ppermute | solution.py:377
  7.7 12.6 %collective-permute-start.5 = (bf16[2,128,256]{2,1,0:T(8,128)(2,1)S(1)}, bf16[2,128,256]{2,1,0:T(8,128)(2,1)S(1)}, u32[]{:S(2)}, u32[]{:S(2)}) collective-permute-start(bf16[2,128,256]{2,1,0:T(8,128)(2,1)S(1)} %pad_maximum_fusion.5), channel_id=1, source_target_pairs={{0,12},{4,8},{8,4},{12,0},{1,13},{5,9},{9,5},{13,1},{2,14},{6,10},... | collective-permute-start | bytes 393224 | tf_op jit(solution)/shard_map/ppermute | solution.py:377
  22.5 1.9 %collective-permute-start.6 = (bf16[128,256]{1,0:T(8,128)(2,1)S(1)}, bf16[128,256]{1,0:T(8,128)(2,1)S(1)}, u32[]{:S(2)}, u32[]{:S(2)}) collective-permute-start(bf16[128,256]{1,0:T(8,128)(2,1)S(1)} %get-tuple-element.10), channel_id=1, source_target_pairs={{0,4},{4,0},{8,12},{12,8},{1,5},{5,1},{9,13},{13,9},{2,6},{6,2},{1... | collective-permute-start | bytes 196616 | tf_op jit(solution)/shard_map/ppermute | solution.py:377
  22.7 4.4 %collective-permute-start.7 = (bf16[128,256]{1,0:T(8,128)(2,1)S(1)}, bf16[128,256]{1,0:T(8,128)(2,1)S(1)}, u32[]{:S(2)}, u32[]{:S(2)}) collective-permute-start(bf16[128,256]{1,0:T(8,128)(2,1)S(1)} %get-tuple-element.11), channel_id=1, source_target_pairs={{0,8},{4,12},{8,0},{12,4},{1,9},{5,13},{9,1},{13,5},{2,10},{6,14},... | collective-permute-start | bytes 196616 | tf_op jit(solution)/shard_map/ppermute | solution.py:377
  24.4 4.2 %collective-permute-start.8 = (bf16[128,256]{1,0:T(8,128)(2,1)S(1)}, bf16[128,256]{1,0:T(8,128)(2,1)S(1)}, u32[]{:S(2)}, u32[]{:S(2)}) collective-permute-start(bf16[128,256]{1,0:T(8,128)(2,1)S(1)} %get-tuple-element.12), channel_id=1, source_target_pairs={{0,12},{4,8},{8,4},{12,0},{1,13},{5,9},{9,5},{13,1},{2,14},{6,10},... | collective-permute-start | bytes 196616 | tf_op jit(solution)/shard_map/ppermute | solution.py:377

commit v2 on v1

--- a/solution.py
+++ b/solution.py
@@ -235,23 +235,39 @@
     return folded_sum(main) + small
 
 
+def pack_kernel(place_ref, *rest, steps, width):
+    sources, outs, sem = rest[: -len(steps) - 1], rest[-len(steps) - 1 : -1], rest[-1]
+    here = place_ref[0]
+    copies = []
+    for (step, first, last), out in zip(steps, outs):
+        columns = pl.ds(pl.multiple_of((here ^ step) * width, width), width)
+        for n, source in enumerate(sources[first:last]):
+            rows = source.shape[0]
+            copies.append(
+                pltpu.make_async_copy(
+                    source.at[:, columns], out.at[n * rows : (n + 1) * rows], sem.at[len(copies)]
+                )
+            )
+    for copy in copies:
+        copy.start()
+    for copy in copies:
+        copy.wait()
+
+
 def conv_kernel(
-    place_ref, gate_ref, value_ref, filter_ref, *rest, count, block, head_dim
+    place_ref, own_ref, near_ref, *rest, count, block, head_dim
 ):
-    arrived = rest[: count - 1]
-    taps_ref, weight_ref, ahead_ref, back_ref, query_ref = rest[count - 1 : count + 4]
-    gate_all, value_all, filter_all = rest[count + 4 :]
+    arrived = rest[: count - 2]
+    taps_ref, weight_ref, ahead_ref, back_ref, query_ref = rest[count - 2 : count + 3]
+    gate_all, value_all, filter_all = rest[count + 3 :]
     here = place_ref[0]
-    gate_all[0] = jnp.zeros_like(gate_ref)
-    filter_all[0] = jnp.zeros_like(filter_ref)
-    gate_all[here + 1] = gate_ref[...]
-    value_all[here] = value_ref[...]
-    filter_all[here + 1] = filter_ref[...]
-    for step, piece in enumerate(arrived, 1):
+    gate_all[0] = jnp.zeros(gate_all.shape[1:], gate_all.dtype)
+    filter_all[0] = jnp.zeros(filter_all.shape[1:], filter_all.dtype)
+    for step, piece in enumerate((own_ref, near_ref, *arrived)):
         source = here ^ step
-        gate_all[source + 1] = piece[0]
-        value_all[source] = piece[1]
-        filter_all[source + 1] = piece[2]
+        gate_all[source + 1] = piece[:block]
+        value_all[source] = piece[block : 2 * block]
+        filter_all[source + 1] = piece[2 * block : 3 * block]
     ahead = ahead_ref[...]
     first = ahead[:, block:]
     back = back_ref[...]
@@ -299,16 +315,14 @@
             )
 
 
-def attend_kernel(place_ref, query_ref, key_ref, value_ref, *rest, count, block, head_dim):
-    arrived = rest[: count - 1]
-    outs = rest[count - 1 : 2 * count - 1]
-    key_all, value_all, out_all = rest[2 * count - 1 :]
+def weigh_kernel(place_ref, query_ref, own_ref, near_ref, *rest, count, block, head_dim):
+    arrived = rest[: count - 2]
+    weight_ref, part_ref, key_all = rest[count - 2 :]
     here = place_ref[0]
-    key_all[here] = key_ref[...]
-    value_all[here] = value_ref[...]
-    for step, piece in enumerate(arrived, 1):
-        key_all[here ^ step] = piece[0]
-        value_all[here ^ step] = piece[1]
+    for step, piece in enumerate((own_ref, near_ref)):
+        key_all[here ^ step] = piece[3 * block : 4 * block]
+    for step, piece in enumerate(arrived, 2):
+        key_all[here ^ step] = piece[...]
     width = query_ref.shape[2]
     turned = (((1,), (1,)), ((), ()))
     scale = 1.0 / math.sqrt(head_dim)
@@ -336,14 +350,34 @@
             weights = [jnp.exp(part - peak) for part in scores]
             weights[b] = jnp.where(allowed, weights[b], 0.0)
             weight_sum = jnp.sum(functools.reduce(jnp.add, weights), axis=1, keepdims=True)
-            total = functools.reduce(
-                jnp.add,
-                [
-                    mxu(weights[j].astype(jnp.bfloat16), value_all[j, :, columns])
-                    for j in range(b + 1)
-                ],
-            )
-            out_all[b, :, columns] = (total / weight_sum).astype(jnp.bfloat16)
+            part_ref[h, b] = jnp.broadcast_to(1.0 / weight_sum, (block, head_dim))
+            for j in range(b + 1):
+                weight_ref[h, b, :, j * block : (j + 1) * block] = weights[j].astype(
+                    jnp.bfloat16
+                )
+
+
+def sum_kernel(
+    place_ref, weight_ref, part_ref, own_ref, near_ref, *rest, count, block, head_dim
+):
+    arrived = rest[: count - 2]
+    outs = rest[count - 2 : 2 * count - 2]
+    value_all, out_all = rest[2 * count - 2 :]
+    here = place_ref[0]
+
+    def rows_of(b):
+        return pl.ds(pl.multiple_of(b * block, block), block)
+
+    for step, piece in enumerate((own_ref, near_ref)):
+        value_all[rows_of(here ^ step)] = piece[4 * block : 5 * block]
+    for step, piece in enumerate(arrived, 2):
+        value_all[rows_of(here ^ step)] = piece[...]
+    for h in range(value_all.shape[1] // head_dim):
+        columns = slice(h * head_dim, (h + 1) * head_dim)
+        for b in range(count):
+            seen = (b + 1) * block
+            total = mxu(weight_ref[h, b, :, :seen], value_all[:seen, columns])
+            out_all[b, :, columns] = (total * part_ref[h, b]).astype(jnp.bfloat16)
     for step, out in enumerate(outs):
         out[...] = out_all[here ^ step]
 
@@ -370,32 +404,50 @@
     here = lax.axis_index("seq")
     place = here.astype(jnp.int32).reshape(1)
 
-    def columns_of(value, owner):
-        return lax.dynamic_slice_in_dim(value, owner * width, width, axis=1)
-
     def swap(value, step):
         return lax.ppermute(value, "seq", [(i, i ^ step) for i in range(count)])
 
-    def swap_columns(arrays):
-        return [
-            swap(jnp.stack([columns_of(a, here ^ step) for a in arrays]), step)
-            for step in range(1, count)
-        ]
-
-    arrived = swap_columns([gate_input, value_input, long_filter])
-    arrived_later = swap_columns([key_matrix, value_matrix])
+    def packed(arrays, steps, after=()):
+        return pl.pallas_call(
+            functools.partial(pack_kernel, steps=steps, width=width),
+            out_shape=[
+                pltpu.VMEM(((last - first) * block, width), jnp.bfloat16)
+                for _, first, last in steps
+            ],
+            in_specs=[pl.BlockSpec(memory_space=pltpu.SMEM)]
+            + [pl.BlockSpec(memory_space=pl.ANY)] * (len(arrays) + len(after)),
+            out_specs=[WHOLE] * len(steps),
+            scratch_shapes=[
+                pltpu.SemaphoreType.DMA((sum(last - first for _, first, last in steps),))
+            ],
+            compiler_params=params,
+        )(place, *[pltpu.with_memory_space_constraint(a, pltpu.HBM) for a in arrays], *after)
+
     ahead, back = block_tables(block)
-    mine = pl.BlockSpec((block, width), lambda i, p: (0, p[0]))
     scratch = lambda n: pltpu.VMEM((n, block, width), jnp.bfloat16)
     params = pltpu.CompilerParams(vmem_limit_bytes=32 * 1024 * 1024)
+    far = range(2, count)
+    streams = [gate_input, value_input, long_filter]
+    *first, own, near, k2, k3, v2, v3 = packed(
+        streams + [key_matrix, value_matrix],
+        [(step, 0, 3) for step in far]
+        + [(0, 0, 5), (1, 0, 5)]
+        + [(step, 3, 4) for step in far]
+        + [(step, 4, 5) for step in far],
+    )
+    later = [k2, k3, v2, v3]
+    arrived = [swap(piece, step) for step, piece in zip(far, first)]
+    near = swap(near, 1)
+    near, *later = lax.optimization_barrier((near, *later))
+    later = [swap(piece, step) for step, piece in zip([*far, *far], later)]
+    arrived_keys, arrived_values = later[: len(far)], later[len(far) :]
     queries = pl.pallas_call(
         functools.partial(conv_kernel, count=count, block=block, head_dim=HEAD_DIM),
         out_shape=jax.ShapeDtypeStruct((count, block, width), jnp.bfloat16),
         grid_spec=pltpu.PrefetchScalarGridSpec(
             num_scalar_prefetch=1,
             grid=(1,),
-            in_specs=[mine] * 3
-            + [WHOLE] * (count - 1)
+            in_specs=[WHOLE] * count
             + [
                 pl.BlockSpec((width, TAPS), lambda i, p: (p[0], 0)),
                 pl.BlockSpec((heads, HEAD_DIM, HEAD_DIM), lambda i, p: (p[0], 0, 0)),
@@ -405,23 +457,39 @@
             scratch_shapes=[scratch(count + 1), scratch(count), scratch(count + 1)],
         ),
         compiler_params=params,
-    )(
-        place, gate_input, value_input, long_filter, *arrived, short_filter, query_weight,
-        jnp.asarray(ahead), jnp.asarray(back),
-    )
+    )(place, own, near, *arrived, short_filter, query_weight, jnp.asarray(ahead), jnp.asarray(back))
+    weights, parts = pl.pallas_call(
+        functools.partial(weigh_kernel, count=count, block=block, head_dim=HEAD_DIM),
+        out_shape=[
+            jax.ShapeDtypeStruct((heads, count, block, count * block), jnp.bfloat16),
+            jax.ShapeDtypeStruct((heads, count, block, HEAD_DIM), jnp.float32),
+        ],
+        grid_spec=pltpu.PrefetchScalarGridSpec(
+            num_scalar_prefetch=1,
+            grid=(1,),
+            in_specs=[WHOLE] * (count + 1),
+            out_specs=[WHOLE] * 2,
+            scratch_shapes=[scratch(count)],
+        ),
+        compiler_params=params,
+    )(place, queries, own, near, *arrived_keys)
     pieces = pl.pallas_call(
-        functools.partial(attend_kernel, count=count, block=block, head_dim=HEAD_DIM),
+        functools.partial(sum_kernel, count=count, block=block, head_dim=HEAD_DIM),
         out_shape=[jax.ShapeDtypeStruct((block, width), jnp.bfloat16)] * count,
         grid_spec=pltpu.PrefetchScalarGridSpec(
             num_scalar_prefetch=1,
             grid=(1,),
-            in_specs=[WHOLE] + [mine] * 2 + [WHOLE] * (count - 1),
+            in_specs=[WHOLE] * (count + 2),
             out_specs=[WHOLE] * count,
-            scratch_shapes=[scratch(count)] * 3,
+            scratch_shapes=[
+                pltpu.VMEM((count * block, width), jnp.bfloat16),
+                scratch(count),
+            ],
         ),
         compiler_params=params,
-    )(place, queries, key_matrix, value_matrix, *arrived_later)
-    pieces = [pieces[0]] + [swap(pieces[step], step) for step in range(1, count)]
+    )(place, weights, parts, own, near, *arrived_values)
+    swapped = {step: swap(pieces[step], step) for step in [*far, 1]}
+    pieces = [pieces[0]] + [swapped[step] for step in range(1, count)]
     return pl.pallas_call(
         join_kernel,
         out_shape=jax.ShapeDtypeStruct((block, local_width), jnp.bfloat16),
@@ -435,7 +503,7 @@
     count = lax.axis_size("seq")
     block, local_width = arrays[0].shape
     even = local_width % (count * HEAD_DIM) == 0
-    if even and count & (count - 1) == 0 and block == TAPS:
+    if even and count > 1 and count & (count - 1) == 0 and block == TAPS:
         return head_shards(*arrays)
     return general_shards(*arrays)
 

time: 29.5 us -> 27.2 us (0.922)
  waiting for transfers between devices: 12.5 us -> 10 us
  local copies, waits for them, and re-layouts: 2.08 us -> 0.01 us
  starting transfers between devices: 7.43 us -> 9.3 us
  Pallas kernels: 7.01 us -> 7.64 us
    ppermute x9 -> x10, waiting for transfers between devices: 12.5 us -> 10 us  [swap(): return lax.ppermute(value, 'seq', [(i, i ^ step) for i in range(count)])]
    another operation x3 -> x0, local copies, waits for them, and re-layouts: 1.96 us -> none  [swap_columns(): jnp.stack([columns_of(a, here ^ step) for a in arrays])]
    ppermute x9 -> x10, starting transfers between devices: 7.43 us -> 9.3 us  [swap(): return lax.ppermute(value, 'seq', [(i, i ^ step) for i in range(count)])]
    pallas_call x1 -> x3, Pallas kernels: 2.17 us -> 2.79 us  [the longest x1 1.6 us: packed(): pl.pallas_call(functools.partial(pack_kernel, steps=steps, width=width),...]
  transfers between devices with their start and end apart: 9 -> 10, of which waited for: 5 -> 5; matrix products, arithmetic and copies ran while one was open for 1% -> 0% of each run, Pallas kernels for 14% -> 18%
where the time goes in v2:
time: 27.2 us; the launch traced here: 27.1 us
  waiting for transfers between devices  10 us (37%)
  starting transfers between devices  9.3 us (34%)
  Pallas kernels  7.64 us (28%)
    ppermute x10, waiting for transfers between devices, swap(): return lax.ppermute(value, 'seq', [(i, i ^ step) for i in range(count)])  10 us
    ppermute x10, starting transfers between devices, swap(): return lax.ppermute(value, 'seq', [(i, i ^ step) for i in range(count)])  9.3 us
    pallas_call x1, Pallas kernels, head_shards(): pl.pallas_call(functools.partial(conv_kernel, count=count, block=block, h...  4.11 us
    pallas_call x1, Pallas kernels, packed(): pl.pallas_call(functools.partial(pack_kernel, steps=steps, width=width),...  1.6 us
    pallas_call x1, Pallas kernels, head_shards(): pl.pallas_call(functools.partial(weigh_kernel, count=count, block=block,...  0.83 us
    pallas_call x1, Pallas kernels, head_shards(): pl.pallas_call(join_kernel, out_shape=jax.ShapeDtypeStruct((block, local_...  0.73 us
  transfers between devices with their start and end apart: 10, of which 5 were waited for; matrix products, arithmetic and copies ran while one was open for 0% of the time, Pallas kernels for 18%

profile of v2, /device:TPU:0, one launch (start us, length us, event | category | flops | bytes accessed | tf_op | source)
XLA Modules:
  0.0 27.1 jit_solution(16864905988516555775)
XLA Ops:
  0.0 1.6 %shard_map.91 = (bf16[384,256]{1,0:T(8,128)(2,1)S(1)}, bf16[384,256]{1,0:T(8,128)(2,1)S(1)}, bf16[640,256]{1,0:T(8,128)(2,1)S(1)}, bf16[640,256]{1,0:T(8,128)(2,...) custom-call(s32[1]{0:T(128)} %bitcast.place_ref, ...), custom_call_target="tpu_custom_call" | custom-call | tf_op jit(solution)/shard_map/pallas_call | solution.py:411
  1.6 0.5 %collective-permute-start = (bf16[640,256]{1,0:T(8,128)(2,1)S(1)}, bf16[640,256]{1,0:T(8,128)(2,1)S(1)}, u32[]{:S(2)}, u32[]{:S(2)}) collective-permute-start(bf16[640,256]{1,0:T(8,128)(2,1)S(1)} %get-tuple-element.25), channel_id=1, source_target_pairs={{0,4},{4,0},{8,12},{12,8},{1,5},{5,1},{9,13},{13,9},{2,6},{6,2},{1... | collective-permute-start | bytes 983048 | tf_op jit(solution)/shard_map/ppermute | solution.py:408
  2.1 2.6 %collective-permute-start.1 = (bf16[384,256]{1,0:T(8,128)(2,1)S(1)}, bf16[384,256]{1,0:T(8,128)(2,1)S(1)}, u32[]{:S(2)}, u32[]{:S(2)}) collective-permute-start(bf16[384,256]{1,0:T(8,128)(2,1)S(1)} %get-tuple-element.31), channel_id=1, source_target_pairs={{0,8},{4,12},{8,0},{12,4},{1,9},{5,13},{9,1},{13,5},{2,10},{6,14},... | collective-permute-start | bytes 589832 | tf_op jit(solution)/shard_map/ppermute | solution.py:408
  4.7 0.1 collective-permute-start.2
  4.8 0.0 collective-permute-done.near_ref
  4.8 1.7 %collective-permute-start.3 = (bf16[128,256]{1,0:T(8,128)(2,1)S(1)}, bf16[128,256]{1,0:T(8,128)(2,1)S(1)}, u32[]{:S(2)}, u32[]{:S(2)}) collective-permute-start(bf16[128,256]{1,0:T(8,128)(2,1)S(1)} %get-tuple-element.33), channel_id=1, source_target_pairs={{0,8},{4,12},{8,0},{12,4},{1,9},{5,13},{9,1},{13,5},{2,10},{6,14},... | collective-permute-start | bytes 196616 | tf_op jit(solution)/shard_map/ppermute | solution.py:408
  6.5 0.0 collective-permute-start.4
  6.5 1.7 %collective-permute-start.5 = (bf16[128,256]{1,0:T(8,128)(2,1)S(1)}, bf16[128,256]{1,0:T(8,128)(2,1)S(1)}, u32[]{:S(2)}, u32[]{:S(2)}) collective-permute-start(bf16[128,256]{1,0:T(8,128)(2,1)S(1)} %get-tuple-element.37), channel_id=1, source_target_pairs={{0,8},{4,12},{8,0},{12,4},{1,9},{5,13},{9,1},{13,5},{2,10},{6,14},... | collective-permute-start | bytes 196616 | tf_op jit(solution)/shard_map/ppermute | solution.py:408
  8.2 2.3 %collective-permute-done.1.rest_0_ = bf16[384,256]{1,0:T(8,128)(2,1)S(1)} collective-permute-done((bf16[384,256]{1,0:T(8,128)(2,1)S(1)}, bf16[384,256]{1,0:T(8,128)(2,1)S(1)}, u32[]{:S(2)}, u32[]{:S(2)}) %collective-permute-start.1) | collective-permute-done | bytes 196640 | tf_op jit(solution)/shard_map/ppermute | solution.py:408
  10.5 0.8 %collective-permute-start.6 = (bf16[128,256]{1,0:T(8,128)(2,1)S(1)}, bf16[128,256]{1,0:T(8,128)(2,1)S(1)}, u32[]{:S(2)}, u32[]{:S(2)}) collective-permute-start(bf16[128,256]{1,0:T(8,128)(2,1)S(1)} %get-tuple-element.38), channel_id=1, source_target_pairs={{0,12},{4,8},{8,4},{12,0},{1,13},{5,9},{9,5},{13,1},{2,14},{6,10},... | collective-permute-start | bytes 196616 | tf_op jit(solution)/shard_map/ppermute | solution.py:408
  11.2 2.9 %collective-permute-done.2.rest_1_ = bf16[384,256]{1,0:T(8,128)(2,1)S(1)} collective-permute-done((bf16[384,256]{1,0:T(8,128)(2,1)S(1)}, bf16[384,256]{1,0:T(8,128)(2,1)S(1)}, u32[]{:S(2)}, u32[]{:S(2)}) %collective-permute-start.2) | collective-permute-done | bytes 196640 | tf_op jit(solution)/shard_map/ppermute | solution.py:408
  14.2 4.1 %shard_map.92.query_ref = bf16[4,128,256]{2,1,0:T(8,128)(2,1)S(1)} custom-call(s32[1]{0:T(128)} %bitcast.place_ref, bf16[640,256]{1,0:T(8,128)(2,1)S(1)} %get-tuple-element.24.own_ref, bf16[640,256]{1,0:T(8,128)(2,1)S(1)} %collective-permute-done.near_ref, bf16[384,256]{1,0:T(8,128)(2,1)S(1)} %collective-permute-done.1.rest_0_, ...), custom_call_target="tpu_custom_call" | custom-call | tf_op jit(solution)/shard_map/pallas_call | solution.py:444
  18.3 0.0 collective-permute-done.3.rest_0_
  18.3 0.8 %shard_map.93 = (bf16[2,4,128,512]{3,2,1,0:T(8,128)(2,1)S(1)}, f32[2,4,128,128]{3,2,1,0:T(8,128)S(1)}) custom-call(s32[1]{0:T(128)} %bitcast.place_ref, bf16[4,128,256]{2,1,0:T(8,128)(2,1)S(1)} %shard_map.92.query_ref, bf16[640,256]{1,0:T(8,128)(2,1)S(1)} %get-tuple-element.24.own_ref, bf16[640,256]{1,0:T(8,128)(2,1)S(1)} %collective-permute-done.near_ref, ...), custom_call_target="tpu_custom_call" | custom-call | tf_op jit(solution)/shard_map/pallas_call | solution.py:461
  19.2 0.0 collective-permute-done.5.rest_0_
  19.2 0.6 %collective-permute-done.6.rest_1_ = bf16[128,256]{1,0:T(8,128)(2,1)S(1)} collective-permute-done((bf16[128,256]{1,0:T(8,128)(2,1)S(1)}, bf16[128,256]{1,0:T(8,128)(2,1)S(1)}, u32[]{:S(2)}, u32[]{:S(2)}) %collective-permute-start.6) | collective-permute-done | bytes 65568 | tf_op jit(solution)/shard_map/ppermute | solution.py:408
  19.8 0.4 %shard_map.94 = (bf16[128,256]{1,0:T(8,128)(2,1)S(1)}, bf16[128,256]{1,0:T(8,128)(2,1)S(1)}, bf16[128,256]{1,0:T(8,128)(2,1)S(1)}, bf16[128,256]{1,0:T(8,128)(2,1)S(1)}) custom-call(s32[1]{0:T(128)} %bitcast.place_ref, bf16[2,4,128,512]{3,2,1,0:T(8,128)(2,1)S(1)} %get-tuple-element.35.weight_ref, f32[2,4,128,128]{3,2,1,0:T(8,128)S(1)} %get-tuple-element.36.part_ref, ...), custom_call_target="tpu_custom_call" | custom-call | tf_op jit(solution)/shard_map/pallas_call | solution.py:476
  20.1 0.2 collective-permute-start.7
  20.3 1.7 %collective-permute-start.8 = (bf16[128,256]{1,0:T(8,128)(2,1)S(1)}, bf16[128,256]{1,0:T(8,128)(2,1)S(1)}, u32[]{:S(2)}, u32[]{:S(2)}) collective-permute-start(bf16[128,256]{1,0:T(8,128)(2,1)S(1)} %get-tuple-element.41), channel_id=1, source_target_pairs={{0,8},{4,12},{8,0},{12,4},{1,9},{5,13},{9,1},{13,5},{2,10},{6,14},... | collective-permute-start | bytes 196616 | tf_op jit(solution)/shard_map/ppermute | solution.py:408
  22.1 0.0 collective-permute-start.9
  22.1 0.0 collective-permute-done.7.rest_1_
  22.1 2.6 %collective-permute-done.8.rest_2_ = bf16[128,256]{1,0:T(8,128)(2,1)S(1)} collective-permute-done((bf16[128,256]{1,0:T(8,128)(2,1)S(1)}, bf16[128,256]{1,0:T(8,128)(2,1)S(1)}, u32[]{:S(2)}, u32[]{:S(2)}) %collective-permute-start.8) | collective-permute-done | bytes 65568 | tf_op jit(solution)/shard_map/ppermute | solution.py:408
  24.7 1.6 %collective-permute-done.9.rest_3_ = bf16[128,256]{1,0:T(8,128)(2,1)S(1)} collective-permute-done((bf16[128,256]{1,0:T(8,128)(2,1)S(1)}, bf16[128,256]{1,0:T(8,128)(2,1)S(1)}, u32[]{:S(2)}, u32[]{:S(2)}) %collective-permute-start.9) | collective-permute-done | bytes 65568 | tf_op jit(solution)/shard_map/ppermute | solution.py:408
  26.3 0.7 %shard_map.95 = bf16[128,1024]{1,0:T(8,128)(2,1)} custom-call(s32[1]{0:T(128)} %bitcast.place_ref, bf16[128,256]{1,0:T(8,128)(2,1)S(1)} %get-tuple-element.39.rest_0_, bf16[128,256]{1,0:T(8,128)(2,1)S(1)} %collective-permute-done.7.rest_1_, bf16[128,256]{1,0:T(8,128)(2,1)S(1)} %collective-permute-done.8.rest_2_, ...), custom_call_target="tpu_custom_call" | custom-call | tf_op jit(solution)/shard_map/pallas_call | solution.py:493
  (9 shorter events, 0.0 us)
Async XLA Ops:
  0.0 14.2 %copy-start = (f32[1024,128]{1,0:T(8,128)S(1)}, f32[1024,128]{1,0:T(8,128)}, u32[]{:S(2)}) copy-start(f32[1024,128]{1,0:T(8,128)} %rest_2_.3) | copy-start | bytes 1572868
  0.0 14.2 %copy-start.1 = (bf16[8,128,128]{2,1,0:T(8,128)(2,1)S(1)}, bf16[8,128,128]{2,1,0:T(8,128)(2,1)}, u32[]{:S(2)}) copy-start(bf16[8,128,128]{2,1,0:T(8,128)(2,1)} %rest_3_.3) | copy-start | bytes 786436
  0.0 14.2 %copy-start.2 = (bf16[512,256]{1,0:T(8,128)(2,1)S(1)}, bf16[512,256]{1,0:T(8,128)(2,1)}, u32[]{:S(2)}) copy-start(bf16[512,256]{1,0:T(8,128)(2,1)} %constant.9.clone.rest_4_) | copy-start | bytes 786436
  0.0 14.2 %copy-start.3 = (bf16[256,256]{1,0:T(8,128)(2,1)S(1)}, bf16[256,256]{1,0:T(8,128)(2,1)}, u32[]{:S(2)}) copy-start(bf16[256,256]{1,0:T(8,128)(2,1)} %constant.10.clone.rest_5_) | copy-start | bytes 393220
  1.6 3.2 %collective-permute-start = (bf16[640,256]{1,0:T(8,128)(2,1)S(1)}, bf16[640,256]{1,0:T(8,128)(2,1)S(1)}, u32[]{:S(2)}, u32[]{:S(2)}) collective-permute-start(bf16[640,256]{1,0:T(8,128)(2,1)S(1)} %get-tuple-element.25), channel_id=1, source_target_pairs={{0,4},{4,0},{8,12},{12,8},{1,5},{5,1},{9,13},{13,9},{2,6},{6,2},{1... | collective-permute-start | bytes 983048 | tf_op jit(solution)/shard_map/ppermute | solution.py:408
  2.1 8.3 %collective-permute-start.1 = (bf16[384,256]{1,0:T(8,128)(2,1)S(1)}, bf16[384,256]{1,0:T(8,128)(2,1)S(1)}, u32[]{:S(2)}, u32[]{:S(2)}) collective-permute-start(bf16[384,256]{1,0:T(8,128)(2,1)S(1)} %get-tuple-element.31), channel_id=1, source_target_pairs={{0,8},{4,12},{8,0},{12,4},{1,9},{5,13},{9,1},{13,5},{2,10},{6,14},... | collective-permute-start | bytes 589832 | tf_op jit(solution)/shard_map/ppermute | solution.py:408
  4.7 9.4 %collective-permute-start.2 = (bf16[384,256]{1,0:T(8,128)(2,1)S(1)}, bf16[384,256]{1,0:T(8,128)(2,1)S(1)}, u32[]{:S(2)}, u32[]{:S(2)}) collective-permute-start(bf16[384,256]{1,0:T(8,128)(2,1)S(1)} %get-tuple-element.32), channel_id=1, source_target_pairs={{0,12},{4,8},{8,4},{12,0},{1,13},{5,9},{9,5},{13,1},{2,14},{6,10},... | collective-permute-start | bytes 589832 | tf_op jit(solution)/shard_map/ppermute | solution.py:408
  4.8 13.5 %collective-permute-start.3 = (bf16[128,256]{1,0:T(8,128)(2,1)S(1)}, bf16[128,256]{1,0:T(8,128)(2,1)S(1)}, u32[]{:S(2)}, u32[]{:S(2)}) collective-permute-start(bf16[128,256]{1,0:T(8,128)(2,1)S(1)} %get-tuple-element.33), channel_id=1, source_target_pairs={{0,8},{4,12},{8,0},{12,4},{1,9},{5,13},{9,1},{13,5},{2,10},{6,14},... | collective-permute-start | bytes 196616 | tf_op jit(solution)/shard_map/ppermute | solution.py:408
  6.5 11.8 %collective-permute-start.4 = (bf16[128,256]{1,0:T(8,128)(2,1)S(1)}, bf16[128,256]{1,0:T(8,128)(2,1)S(1)}, u32[]{:S(2)}, u32[]{:S(2)}) collective-permute-start(bf16[128,256]{1,0:T(8,128)(2,1)S(1)} %get-tuple-element.34), channel_id=1, source_target_pairs={{0,12},{4,8},{8,4},{12,0},{1,13},{5,9},{9,5},{13,1},{2,14},{6,10},... | collective-permute-start | bytes 196616 | tf_op jit(solution)/shard_map/ppermute | solution.py:408
  6.5 12.6 %collective-permute-start.5 = (bf16[128,256]{1,0:T(8,128)(2,1)S(1)}, bf16[128,256]{1,0:T(8,128)(2,1)S(1)}, u32[]{:S(2)}, u32[]{:S(2)}) collective-permute-start(bf16[128,256]{1,0:T(8,128)(2,1)S(1)} %get-tuple-element.37), channel_id=1, source_target_pairs={{0,8},{4,12},{8,0},{12,4},{1,9},{5,13},{9,1},{13,5},{2,10},{6,14},... | collective-permute-start | bytes 196616 | tf_op jit(solution)/shard_map/ppermute | solution.py:408
  10.5 9.3 %collective-permute-start.6 = (bf16[128,256]{1,0:T(8,128)(2,1)S(1)}, bf16[128,256]{1,0:T(8,128)(2,1)S(1)}, u32[]{:S(2)}, u32[]{:S(2)}) collective-permute-start(bf16[128,256]{1,0:T(8,128)(2,1)S(1)} %get-tuple-element.38), channel_id=1, source_target_pairs={{0,12},{4,8},{8,4},{12,0},{1,13},{5,9},{9,5},{13,1},{2,14},{6,10},... | collective-permute-start | bytes 196616 | tf_op jit(solution)/shard_map/ppermute | solution.py:408
  20.1 1.9 %collective-permute-start.7 = (bf16[128,256]{1,0:T(8,128)(2,1)S(1)}, bf16[128,256]{1,0:T(8,128)(2,1)S(1)}, u32[]{:S(2)}, u32[]{:S(2)}) collective-permute-start(bf16[128,256]{1,0:T(8,128)(2,1)S(1)} %get-tuple-element.40), channel_id=1, source_target_pairs={{0,4},{4,0},{8,12},{12,8},{1,5},{5,1},{9,13},{13,9},{2,6},{6,2},{1... | collective-permute-start | bytes 196616 | tf_op jit(solution)/shard_map/ppermute | solution.py:408
  20.3 4.4 %collective-permute-start.8 = (bf16[128,256]{1,0:T(8,128)(2,1)S(1)}, bf16[128,256]{1,0:T(8,128)(2,1)S(1)}, u32[]{:S(2)}, u32[]{:S(2)}) collective-permute-start(bf16[128,256]{1,0:T(8,128)(2,1)S(1)} %get-tuple-element.41), channel_id=1, source_target_pairs={{0,8},{4,12},{8,0},{12,4},{1,9},{5,13},{9,1},{13,5},{2,10},{6,14},... | collective-permute-start | bytes 196616 | tf_op jit(solution)/shard_map/ppermute | solution.py:408
  22.1 4.3 %collective-permute-start.9 = (bf16[128,256]{1,0:T(8,128)(2,1)S(1)}, bf16[128,256]{1,0:T(8,128)(2,1)S(1)}, u32[]{:S(2)}, u32[]{:S(2)}) collective-permute-start(bf16[128,256]{1,0:T(8,128)(2,1)S(1)} %get-tuple-element.42), channel_id=1, source_target_pairs={{0,12},{4,8},{8,4},{12,0},{1,13},{5,9},{9,5},{13,1},{2,14},{6,10},... | collective-permute-start | bytes 196616 | tf_op jit(solution)/shard_map/ppermute | solution.py:408

commit v3 on v2

--- a/solution.py
+++ b/solution.py
@@ -227,21 +227,24 @@
     return stacked[:half] + stacked[half:]
 
 
+def wide_mxu(table, value):
+    half = table.shape[0] // 2
+    wide = jnp.concatenate([table[:half], table[half:]], axis=1)
+    return mxu(wide, jnp.concatenate([value, value], axis=0))
+
+
 def to_block(back, spec_re, spec_im, block):
-    re_high, re_rest = two_parts(spec_re)
-    im_high, im_rest = two_parts(spec_im)
-    main = mxu(back[:, :block], re_high) + mxu(back[:, block:], im_high)
-    small = mxu(back[:block, :block], re_rest) + mxu(back[:block, block:], im_rest)
-    return folded_sum(main) + small
-
-
-def pack_kernel(place_ref, *rest, steps, width):
-    sources, outs, sem = rest[: -len(steps) - 1], rest[-len(steps) - 1 : -1], rest[-1]
+    high, rest = two_parts(jnp.concatenate([spec_re, spec_im], axis=0))
+    return folded_sum(mxu(back, high)) + mxu(back[:block], rest)
+
+
+def pack_kernel(place_ref, *rest, parts, width):
+    outs, sem = rest[-len(parts) - 1 : -1], rest[-1]
     here = place_ref[0]
     copies = []
-    for (step, first, last), out in zip(steps, outs):
+    for (step, first, last), out in zip(parts, outs):
         columns = pl.ds(pl.multiple_of((here ^ step) * width, width), width)
-        for n, source in enumerate(sources[first:last]):
+        for n, source in enumerate(rest[first:last]):
             rows = source.shape[0]
             copies.append(
                 pltpu.make_async_copy(
@@ -272,7 +275,10 @@
     first = ahead[:, block:]
     back = back_ref[...]
     turned = (((1,), (1,)), ((), ()))
-    taps_high, taps_rest = two_parts(taps_ref[...])
+    width = own_ref.shape[1]
+    heads = width // head_dim
+    taps = taps_ref[pl.ds(pl.multiple_of(here * width, width), width)]
+    taps_high, taps_rest = two_parts(taps)
     taps_spec = folded_sum(
         lax.dot_general(first, taps_high, turned, preferred_element_type=jnp.float32)
     ) + lax.dot_general(
@@ -281,10 +287,9 @@
     taps_re, taps_im = taps_spec[:block], taps_spec[block:]
     lines = []
     kernels = []
-    heads = weight_ref.shape[0]
     for b in range(count):
         window = jnp.concatenate([gate_all[b], gate_all[b + 1]], axis=0)
-        gate_spec = folded_sum(mxu(ahead, window))
+        gate_spec = wide_mxu(ahead, window)
         gate_re, gate_im = gate_spec[:block], gate_spec[block:]
         smoothed = to_block(
             back,
@@ -293,11 +298,9 @@
             block,
         )
         mixed = (smoothed * value_all[b].astype(jnp.float32)).astype(jnp.bfloat16)
-        lines.append(folded_sum(mxu(first, mixed)))
+        lines.append(wide_mxu(first, mixed))
         kernels.append(
-            folded_sum(
-                mxu(ahead, jnp.concatenate([filter_all[b], filter_all[b + 1]], axis=0))
-            )
+            wide_mxu(ahead, jnp.concatenate([filter_all[b], filter_all[b + 1]], axis=0))
         )
     for b in range(count):
         total_re, total_im = 0.0, 0.0
@@ -310,7 +313,7 @@
         conv_out = to_block(back, total_re, total_im, block).astype(jnp.bfloat16)
         for h in range(heads):
             columns = slice(h * head_dim, (h + 1) * head_dim)
-            query_ref[b, :, columns] = mxu(conv_out[:, columns], weight_ref[h]).astype(
+            query_ref[b, :, columns] = mxu(conv_out[:, columns], weight_ref[here * heads + h]).astype(
                 jnp.bfloat16
             )
 
@@ -319,10 +322,8 @@
     arrived = rest[: count - 2]
     weight_ref, part_ref, key_all = rest[count - 2 :]
     here = place_ref[0]
-    for step, piece in enumerate((own_ref, near_ref)):
-        key_all[here ^ step] = piece[3 * block : 4 * block]
-    for step, piece in enumerate(arrived, 2):
-        key_all[here ^ step] = piece[...]
+    for step, piece in enumerate((own_ref, near_ref, *arrived)):
+        key_all[here ^ step] = piece[:block]
     width = query_ref.shape[2]
     turned = (((1,), (1,)), ((), ()))
     scale = 1.0 / math.sqrt(head_dim)
@@ -368,10 +369,8 @@
     def rows_of(b):
         return pl.ds(pl.multiple_of(b * block, block), block)
 
-    for step, piece in enumerate((own_ref, near_ref)):
-        value_all[rows_of(here ^ step)] = piece[4 * block : 5 * block]
-    for step, piece in enumerate(arrived, 2):
-        value_all[rows_of(here ^ step)] = piece[...]
+    for step, piece in enumerate((own_ref, near_ref, *arrived)):
+        value_all[rows_of(here ^ step)] = piece[-block:]
     for h in range(value_all.shape[1] // head_dim):
         columns = slice(h * head_dim, (h + 1) * head_dim)
         for b in range(count):
@@ -407,18 +406,18 @@
     def swap(value, step):
         return lax.ppermute(value, "seq", [(i, i ^ step) for i in range(count)])
 
-    def packed(arrays, steps, after=()):
+    def packed(arrays, parts, after=()):
         return pl.pallas_call(
-            functools.partial(pack_kernel, steps=steps, width=width),
+            functools.partial(pack_kernel, parts=parts, width=width),
             out_shape=[
                 pltpu.VMEM(((last - first) * block, width), jnp.bfloat16)
-                for _, first, last in steps
+                for _, first, last in parts
             ],
             in_specs=[pl.BlockSpec(memory_space=pltpu.SMEM)]
             + [pl.BlockSpec(memory_space=pl.ANY)] * (len(arrays) + len(after)),
-            out_specs=[WHOLE] * len(steps),
+            out_specs=[WHOLE] * len(parts),
             scratch_shapes=[
-                pltpu.SemaphoreType.DMA((sum(last - first for _, first, last in steps),))
+                pltpu.SemaphoreType.DMA((sum(last - first for _, first, last in parts),))
             ],
             compiler_params=params,
         )(place, *[pltpu.with_memory_space_constraint(a, pltpu.HBM) for a in arrays], *after)
@@ -428,17 +427,20 @@
     params = pltpu.CompilerParams(vmem_limit_bytes=32 * 1024 * 1024)
     far = range(2, count)
     streams = [gate_input, value_input, long_filter]
-    *first, own, near, k2, k3, v2, v3 = packed(
-        streams + [key_matrix, value_matrix],
-        [(step, 0, 3) for step in far]
-        + [(0, 0, 5), (1, 0, 5)]
-        + [(step, 3, 4) for step in far]
-        + [(step, 4, 5) for step in far],
-    )
-    later = [k2, k3, v2, v3]
-    arrived = [swap(piece, step) for step, piece in zip(far, first)]
+    first, near = packed(streams, [(far[0], 0, 3), (1, 0, 3)])
     near = swap(near, 1)
-    near, *later = lax.optimization_barrier((near, *later))
+    own, *others = packed(
+        [*streams, key_matrix, value_matrix],
+        [(0, 0, 3)]
+        + [(step, 0, 3) for step in far[1:]]
+        + [(0, 3, 5), (1, 3, 5)]
+        + [(step, n, n + 1) for n in (3, 4) for step in far],
+        after=[near],
+    )
+    arrived = [swap(piece, step) for step, piece in zip(far, [first, *others])]
+    own_later, near_later, *later = others[len(far) - 1 :]
+    near_later = swap(near_later, 1)
+    near_later, *later = lax.optimization_barrier((near_later, *later))
     later = [swap(piece, step) for step, piece in zip([*far, *far], later)]
     arrived_keys, arrived_values = later[: len(far)], later[len(far) :]
     queries = pl.pallas_call(
@@ -448,11 +450,7 @@
             num_scalar_prefetch=1,
             grid=(1,),
             in_specs=[WHOLE] * count
-            + [
-                pl.BlockSpec((width, TAPS), lambda i, p: (p[0], 0)),
-                pl.BlockSpec((heads, HEAD_DIM, HEAD_DIM), lambda i, p: (p[0], 0, 0)),
-            ]
-            + [WHOLE] * 2,
+            + [WHOLE] * 4,
             out_specs=WHOLE,
             scratch_shapes=[scratch(count + 1), scratch(count), scratch(count + 1)],
         ),
@@ -472,7 +470,7 @@
             scratch_shapes=[scratch(count)],
         ),
         compiler_params=params,
-    )(place, queries, own, near, *arrived_keys)
+    )(place, queries, own_later, near_later, *arrived_keys)
     pieces = pl.pallas_call(
         functools.partial(sum_kernel, count=count, block=block, head_dim=HEAD_DIM),
         out_shape=[jax.ShapeDtypeStruct((block, width), jnp.bfloat16)] * count,
@@ -487,7 +485,7 @@
             ],
         ),
         compiler_params=params,
-    )(place, weights, parts, own, near, *arrived_values)
+    )(place, weights, parts, own_later, near_later, *arrived_values)
     swapped = {step: swap(pieces[step], step) for step in [*far, 1]}
     pieces = [pieces[0]] + [swapped[step] for step in range(1, count)]
     return pl.pallas_call(

time: 27.2 us -> 26.8 us (0.985)
  waiting for transfers between devices: 10 us -> 8.78 us
  starting transfers between devices: 9.3 us -> 10.1 us
    ppermute x10 -> x11, waiting for transfers between devices: 10 us -> 8.78 us  [swap(): return lax.ppermute(value, 'seq', [(i, i ^ step) for i in range(count)])]
    pallas_call x1, Pallas kernels: 4.11 us -> 3.29 us  [head_shards(): pl.pallas_call(functools.partial(conv_kernel, count=count, block=block, h...]
    pallas_call x1 -> x2, Pallas kernels: 1.6 us -> 2.38 us  [packed(): pl.pallas_call(functools.partial(pack_kernel, parts=parts, width=width),...]
    ppermute x10 -> x11, starting transfers between devices: 9.3 us -> 10.1 us  [swap(): return lax.ppermute(value, 'seq', [(i, i ^ step) for i in range(count)])]
  transfers between devices with their start and end apart: 10 -> 11, of which waited for: 5 -> 6; matrix products, arithmetic and copies ran while one was open for 0% -> 0% of each run, Pallas kernels for 18% -> 21%
where the time goes in v3:
time: 26.8 us; the launch traced here: 26.5 us
  starting transfers between devices  10.1 us (38%)
  waiting for transfers between devices  8.78 us (33%)
  Pallas kernels  7.6 us (28%)
    ppermute x11, starting transfers between devices, swap(): return lax.ppermute(value, 'seq', [(i, i ^ step) for i in range(count)])  10.1 us
    ppermute x11, waiting for transfers between devices, swap(): return lax.ppermute(value, 'seq', [(i, i ^ step) for i in range(count)])  8.78 us
    pallas_call x1, Pallas kernels, head_shards(): pl.pallas_call(functools.partial(conv_kernel, count=count, block=block, h...  3.29 us
    pallas_call x2, Pallas kernels, packed(): pl.pallas_call(functools.partial(pack_kernel, parts=parts, width=width),...  2.38 us
    pallas_call x1, Pallas kernels, head_shards(): pl.pallas_call(functools.partial(weigh_kernel, count=count, block=block,...  0.84 us
    pallas_call x1, Pallas kernels, head_shards(): pl.pallas_call(join_kernel, out_shape=jax.ShapeDtypeStruct((block, local_...  0.73 us
  transfers between devices with their start and end apart: 11, of which 6 were waited for; matrix products, arithmetic and copies ran while one was open for 0% of the time, Pallas kernels for 21%

profile of v3, /device:TPU:0, one launch (start us, length us, event | category | flops | bytes accessed | tf_op | source)
XLA Modules:
  0.0 26.5 jit_solution(9581021492118184845)
XLA Ops:
  0.0 1.1 %shard_map.91 = (bf16[384,256]{1,0:T(8,128)(2,1)S(1)}, bf16[384,256]{1,0:T(8,128)(2,1)S(1)}) custom-call(s32[1]{0:T(128)} %bitcast.place_ref, bf16[128,1024]{1,0:T(8,128)(2,1)} %rest_0_.3, bf16[128,1024]{1,0:T(8,128)(2,1)} %rest_1_.3, bf16[128,1024]{1,0:T(8,128)(2,1)} %rest_2_.4), custom_call_target="tpu_custom_call" | custom-call | tf_op jit(solution)/shard_map/pallas_call | solution.py:410
  1.1 0.5 %collective-permute-start = (bf16[384,256]{1,0:T(8,128)(2,1)S(1)}, bf16[384,256]{1,0:T(8,128)(2,1)S(1)}, u32[]{:S(2)}, u32[]{:S(2)}) collective-permute-start(bf16[384,256]{1,0:T(8,128)(2,1)S(1)} %get-tuple-element.26), channel_id=1, source_target_pairs={{0,4},{4,0},{8,12},{12,8},{1,5},{5,1},{9,13},{13,9},{2,6},{6,2},{1... | collective-permute-start | bytes 589832 | tf_op jit(solution)/shard_map/ppermute | solution.py:407
  1.6 2.6 %collective-permute-start.1 = (bf16[384,256]{1,0:T(8,128)(2,1)S(1)}, bf16[384,256]{1,0:T(8,128)(2,1)S(1)}, u32[]{:S(2)}, u32[]{:S(2)}) collective-permute-start(bf16[384,256]{1,0:T(8,128)(2,1)S(1)} %get-tuple-element.28), channel_id=1, source_target_pairs={{0,8},{4,12},{8,0},{12,4},{1,9},{5,13},{9,1},{13,5},{2,10},{6,14},... | collective-permute-start | bytes 589832 | tf_op jit(solution)/shard_map/ppermute | solution.py:407
  4.2 0.0 collective-permute-done.rest_5_.near_ref
  4.2 1.3 %shard_map.92 = (bf16[384,256]{1,0:T(8,128)(2,1)S(1)}, bf16[384,256]{1,0:T(8,128)(2,1)S(1)}, bf16[256,256]{1,0:T(8,128)(2,1)S(1)}, bf16[256,256]{1,0:T(8,128)(2,...) custom-call(s32[1]{0:T(128)} %bitcast.place_ref, ...), custom_call_target="tpu_custom_call" | custom-call | tf_op jit(solution)/shard_map/pallas_call | solution.py:410
  5.5 0.2 collective-permute-start.3
  5.8 1.2 %collective-permute-start.2 = (bf16[384,256]{1,0:T(8,128)(2,1)S(1)}, bf16[384,256]{1,0:T(8,128)(2,1)S(1)}, u32[]{:S(2)}, u32[]{:S(2)}) collective-permute-start(bf16[384,256]{1,0:T(8,128)(2,1)S(1)} %get-tuple-element.29), channel_id=1, source_target_pairs={{0,12},{4,8},{8,4},{12,0},{1,13},{5,9},{9,5},{13,1},{2,14},{6,10},... | collective-permute-start | bytes 589832 | tf_op jit(solution)/shard_map/ppermute | solution.py:407
  7.0 1.2 %collective-permute-start.4 = (bf16[128,256]{1,0:T(8,128)(2,1)S(1)}, bf16[128,256]{1,0:T(8,128)(2,1)S(1)}, u32[]{:S(2)}, u32[]{:S(2)}) collective-permute-start(bf16[128,256]{1,0:T(8,128)(2,1)S(1)} %get-tuple-element.37), channel_id=1, source_target_pairs={{0,8},{4,12},{8,0},{12,4},{1,9},{5,13},{9,1},{13,5},{2,10},{6,14},... | collective-permute-start | bytes 196616 | tf_op jit(solution)/shard_map/ppermute | solution.py:407
  8.3 0.3 %collective-permute-start.5 = (bf16[128,256]{1,0:T(8,128)(2,1)S(1)}, bf16[128,256]{1,0:T(8,128)(2,1)S(1)}, u32[]{:S(2)}, u32[]{:S(2)}) collective-permute-start(bf16[128,256]{1,0:T(8,128)(2,1)S(1)} %get-tuple-element.38), channel_id=1, source_target_pairs={{0,12},{4,8},{8,4},{12,0},{1,13},{5,9},{9,5},{13,1},{2,14},{6,10},... | collective-permute-start | bytes 196616 | tf_op jit(solution)/shard_map/ppermute | solution.py:407
  8.5 1.2 %collective-permute-start.6 = (bf16[128,256]{1,0:T(8,128)(2,1)S(1)}, bf16[128,256]{1,0:T(8,128)(2,1)S(1)}, u32[]{:S(2)}, u32[]{:S(2)}) collective-permute-start(bf16[128,256]{1,0:T(8,128)(2,1)S(1)} %get-tuple-element.41), channel_id=1, source_target_pairs={{0,8},{4,12},{8,0},{12,4},{1,9},{5,13},{9,1},{13,5},{2,10},{6,14},... | collective-permute-start | bytes 196616 | tf_op jit(solution)/shard_map/ppermute | solution.py:407
  9.8 0.2 collective-permute-done.1.rest_0_
  9.9 0.8 %collective-permute-start.7 = (bf16[128,256]{1,0:T(8,128)(2,1)S(1)}, bf16[128,256]{1,0:T(8,128)(2,1)S(1)}, u32[]{:S(2)}, u32[]{:S(2)}) collective-permute-start(bf16[128,256]{1,0:T(8,128)(2,1)S(1)} %get-tuple-element.42), channel_id=1, source_target_pairs={{0,12},{4,8},{8,4},{12,0},{1,13},{5,9},{9,5},{13,1},{2,14},{6,10},... | collective-permute-start | bytes 196616 | tf_op jit(solution)/shard_map/ppermute | solution.py:407
  10.7 3.0 %collective-permute-done.2.rest_1_ = bf16[384,256]{1,0:T(8,128)(2,1)S(1)} collective-permute-done((bf16[384,256]{1,0:T(8,128)(2,1)S(1)}, bf16[384,256]{1,0:T(8,128)(2,1)S(1)}, u32[]{:S(2)}, u32[]{:S(2)}) %collective-permute-start.2) | collective-permute-done | bytes 196640 | tf_op jit(solution)/shard_map/ppermute | solution.py:407
  13.7 3.3 %shard_map.93.query_ref = bf16[4,128,256]{2,1,0:T(8,128)(2,1)S(1)} custom-call(s32[1]{0:T(128)} %bitcast.place_ref, bf16[384,256]{1,0:T(8,128)(2,1)S(1)} %get-tuple-element.27.own_ref, bf16[384,256]{1,0:T(8,128)(2,1)S(1)} %collective-permute-done.rest_5_.near_ref, bf16[384,256]{1,0:T(8,128)(2,1)S(1)} %collective-permute-done.1.rest_0_, ...), custom_call_target="tpu_custom_call" | custom-call | tf_op jit(solution)/shard_map/pallas_call | solution.py:446
  17.0 0.8 %shard_map.94 = (bf16[2,4,128,512]{3,2,1,0:T(8,128)(2,1)S(1)}, f32[2,4,128,128]{3,2,1,0:T(8,128)S(1)}) custom-call(s32[1]{0:T(128)} %bitcast.place_ref, bf16[4,128,256]{2,1,0:T(8,128)(2,1)S(1)} %shard_map.93.query_ref, bf16[256,256]{1,0:T(8,128)(2,1)S(1)} %get-tuple-element.30.own_ref, bf16[256,256]{1,0:T(8,128)(2,1)S(1)} %collective-permute-done.3.near_ref, ...), custom_call_target="tpu_custom_call" | custom-call | tf_op jit(solution)/shard_map/pallas_call | solution.py:459
  17.9 0.5 %collective-permute-done.6.rest_0_ = bf16[128,256]{1,0:T(8,128)(2,1)S(1)} collective-permute-done((bf16[128,256]{1,0:T(8,128)(2,1)S(1)}, bf16[128,256]{1,0:T(8,128)(2,1)S(1)}, u32[]{:S(2)}, u32[]{:S(2)}) %collective-permute-start.6) | collective-permute-done | bytes 65568 | tf_op jit(solution)/shard_map/ppermute | solution.py:407
  18.4 0.9 %collective-permute-done.7.rest_1_ = bf16[128,256]{1,0:T(8,128)(2,1)S(1)} collective-permute-done((bf16[128,256]{1,0:T(8,128)(2,1)S(1)}, bf16[128,256]{1,0:T(8,128)(2,1)S(1)}, u32[]{:S(2)}, u32[]{:S(2)}) %collective-permute-start.7) | collective-permute-done | bytes 65568 | tf_op jit(solution)/shard_map/ppermute | solution.py:407
  19.3 0.4 %shard_map.95 = (bf16[128,256]{1,0:T(8,128)(2,1)S(1)}, bf16[128,256]{1,0:T(8,128)(2,1)S(1)}, bf16[128,256]{1,0:T(8,128)(2,1)S(1)}, bf16[128,256]{1,0:T(8,128)(2,1)S(1)}) custom-call(s32[1]{0:T(128)} %bitcast.place_ref, bf16[2,4,128,512]{3,2,1,0:T(8,128)(2,1)S(1)} %get-tuple-element.39.weight_ref, f32[2,4,128,128]{3,2,1,0:T(8,128)S(1)} %get-tuple-element.40.part_ref, ...), custom_call_target="tpu_custom_call" | custom-call | tf_op jit(solution)/shard_map/pallas_call | solution.py:474
  19.7 0.2 collective-permute-start.8
  19.9 1.7 %collective-permute-start.9 = (bf16[128,256]{1,0:T(8,128)(2,1)S(1)}, bf16[128,256]{1,0:T(8,128)(2,1)S(1)}, u32[]{:S(2)}, u32[]{:S(2)}) collective-permute-start(bf16[128,256]{1,0:T(8,128)(2,1)S(1)} %get-tuple-element.45), channel_id=1, source_target_pairs={{0,8},{4,12},{8,0},{12,4},{1,9},{5,13},{9,1},{13,5},{2,10},{6,14},... | collective-permute-start | bytes 196616 | tf_op jit(solution)/shard_map/ppermute | solution.py:407
  21.6 0.1 collective-permute-start.10
  21.6 2.6 %collective-permute-done.9.rest_2_ = bf16[128,256]{1,0:T(8,128)(2,1)S(1)} collective-permute-done((bf16[128,256]{1,0:T(8,128)(2,1)S(1)}, bf16[128,256]{1,0:T(8,128)(2,1)S(1)}, u32[]{:S(2)}, u32[]{:S(2)}) %collective-permute-start.9) | collective-permute-done | bytes 65568 | tf_op jit(solution)/shard_map/ppermute | solution.py:407
  24.3 1.5 %collective-permute-done.10.rest_3_ = bf16[128,256]{1,0:T(8,128)(2,1)S(1)} collective-permute-done((bf16[128,256]{1,0:T(8,128)(2,1)S(1)}, bf16[128,256]{1,0:T(8,128)(2,1)S(1)}, u32[]{:S(2)}, u32[]{:S(2)}) %collective-permute-start.10) | collective-permute-done | bytes 65568 | tf_op jit(solution)/shard_map/ppermute | solution.py:407
  25.8 0.7 %shard_map.96 = bf16[128,1024]{1,0:T(8,128)(2,1)} custom-call(s32[1]{0:T(128)} %bitcast.place_ref, bf16[128,256]{1,0:T(8,128)(2,1)S(1)} %get-tuple-element.43.rest_0_, bf16[128,256]{1,0:T(8,128)(2,1)S(1)} %collective-permute-done.8.rest_1_, bf16[128,256]{1,0:T(8,128)(2,1)S(1)} %collective-permute-done.9.rest_2_, ...), custom_call_target="tpu_custom_call" | custom-call | tf_op jit(solution)/shard_map/pallas_call | solution.py:491
  (12 shorter events, 0.0 us)
Async XLA Ops:
  1.1 3.1 %collective-permute-start = (bf16[384,256]{1,0:T(8,128)(2,1)S(1)}, bf16[384,256]{1,0:T(8,128)(2,1)S(1)}, u32[]{:S(2)}, u32[]{:S(2)}) collective-permute-start(bf16[384,256]{1,0:T(8,128)(2,1)S(1)} %get-tuple-element.26), channel_id=1, source_target_pairs={{0,4},{4,0},{8,12},{12,8},{1,5},{5,1},{9,13},{13,9},{2,6},{6,2},{1... | collective-permute-start | bytes 589832 | tf_op jit(solution)/shard_map/ppermute | solution.py:407
  1.6 12.1 %copy-start = (f32[1024,128]{1,0:T(8,128)S(1)}, f32[1024,128]{1,0:T(8,128)}, u32[]{:S(2)}) copy-start(f32[1024,128]{1,0:T(8,128)} %rest_2_.5) | copy-start | bytes 1572868
  1.6 12.1 %copy-start.1 = (bf16[8,128,128]{2,1,0:T(8,128)(2,1)S(1)}, bf16[8,128,128]{2,1,0:T(8,128)(2,1)}, u32[]{:S(2)}) copy-start(bf16[8,128,128]{2,1,0:T(8,128)(2,1)} %rest_3_.3) | copy-start | bytes 786436
  1.6 12.1 %copy-start.2 = (bf16[512,256]{1,0:T(8,128)(2,1)S(1)}, bf16[512,256]{1,0:T(8,128)(2,1)}, u32[]{:S(2)}) copy-start(bf16[512,256]{1,0:T(8,128)(2,1)} %constant.9.clone.rest_4_) | copy-start | bytes 786436
  1.6 12.1 %copy-start.3 = (bf16[256,256]{1,0:T(8,128)(2,1)S(1)}, bf16[256,256]{1,0:T(8,128)(2,1)}, u32[]{:S(2)}) copy-start(bf16[256,256]{1,0:T(8,128)(2,1)} %constant.10.clone.rest_5_) | copy-start | bytes 393220
  1.6 8.4 %collective-permute-start.1 = (bf16[384,256]{1,0:T(8,128)(2,1)S(1)}, bf16[384,256]{1,0:T(8,128)(2,1)S(1)}, u32[]{:S(2)}, u32[]{:S(2)}) collective-permute-start(bf16[384,256]{1,0:T(8,128)(2,1)S(1)} %get-tuple-element.28), channel_id=1, source_target_pairs={{0,8},{4,12},{8,0},{12,4},{1,9},{5,13},{9,1},{13,5},{2,10},{6,14},... | collective-permute-start | bytes 589832 | tf_op jit(solution)/shard_map/ppermute | solution.py:407
  5.5 1.5 %collective-permute-start.3 = (bf16[256,256]{1,0:T(8,128)(2,1)S(1)}, bf16[256,256]{1,0:T(8,128)(2,1)S(1)}, u32[]{:S(2)}, u32[]{:S(2)}) collective-permute-start(bf16[256,256]{1,0:T(8,128)(2,1)S(1)} %get-tuple-element.31), channel_id=1, source_target_pairs={{0,4},{4,0},{8,12},{12,8},{1,5},{5,1},{9,13},{13,9},{2,6},{6,2},{1... | collective-permute-start | bytes 393224 | tf_op jit(solution)/shard_map/ppermute | solution.py:407
  5.8 7.9 %collective-permute-start.2 = (bf16[384,256]{1,0:T(8,128)(2,1)S(1)}, bf16[384,256]{1,0:T(8,128)(2,1)S(1)}, u32[]{:S(2)}, u32[]{:S(2)}) collective-permute-start(bf16[384,256]{1,0:T(8,128)(2,1)S(1)} %get-tuple-element.29), channel_id=1, source_target_pairs={{0,12},{4,8},{8,4},{12,0},{1,13},{5,9},{9,5},{13,1},{2,14},{6,10},... | collective-permute-start | bytes 589832 | tf_op jit(solution)/shard_map/ppermute | solution.py:407
  7.0 10.0 %collective-permute-start.4 = (bf16[128,256]{1,0:T(8,128)(2,1)S(1)}, bf16[128,256]{1,0:T(8,128)(2,1)S(1)}, u32[]{:S(2)}, u32[]{:S(2)}) collective-permute-start(bf16[128,256]{1,0:T(8,128)(2,1)S(1)} %get-tuple-element.37), channel_id=1, source_target_pairs={{0,8},{4,12},{8,0},{12,4},{1,9},{5,13},{9,1},{13,5},{2,10},{6,14},... | collective-permute-start | bytes 196616 | tf_op jit(solution)/shard_map/ppermute | solution.py:407
  8.3 8.8 %collective-permute-start.5 = (bf16[128,256]{1,0:T(8,128)(2,1)S(1)}, bf16[128,256]{1,0:T(8,128)(2,1)S(1)}, u32[]{:S(2)}, u32[]{:S(2)}) collective-permute-start(bf16[128,256]{1,0:T(8,128)(2,1)S(1)} %get-tuple-element.38), channel_id=1, source_target_pairs={{0,12},{4,8},{8,4},{12,0},{1,13},{5,9},{9,5},{13,1},{2,14},{6,10},... | collective-permute-start | bytes 196616 | tf_op jit(solution)/shard_map/ppermute | solution.py:407
  8.5 9.8 %collective-permute-start.6 = (bf16[128,256]{1,0:T(8,128)(2,1)S(1)}, bf16[128,256]{1,0:T(8,128)(2,1)S(1)}, u32[]{:S(2)}, u32[]{:S(2)}) collective-permute-start(bf16[128,256]{1,0:T(8,128)(2,1)S(1)} %get-tuple-element.41), channel_id=1, source_target_pairs={{0,8},{4,12},{8,0},{12,4},{1,9},{5,13},{9,1},{13,5},{2,10},{6,14},... | collective-permute-start | bytes 196616 | tf_op jit(solution)/shard_map/ppermute | solution.py:407
  9.9 9.4 %collective-permute-start.7 = (bf16[128,256]{1,0:T(8,128)(2,1)S(1)}, bf16[128,256]{1,0:T(8,128)(2,1)S(1)}, u32[]{:S(2)}, u32[]{:S(2)}) collective-permute-start(bf16[128,256]{1,0:T(8,128)(2,1)S(1)} %get-tuple-element.42), channel_id=1, source_target_pairs={{0,12},{4,8},{8,4},{12,0},{1,13},{5,9},{9,5},{13,1},{2,14},{6,10},... | collective-permute-start | bytes 196616 | tf_op jit(solution)/shard_map/ppermute | solution.py:407
  19.7 1.9 %collective-permute-start.8 = (bf16[128,256]{1,0:T(8,128)(2,1)S(1)}, bf16[128,256]{1,0:T(8,128)(2,1)S(1)}, u32[]{:S(2)}, u32[]{:S(2)}) collective-permute-start(bf16[128,256]{1,0:T(8,128)(2,1)S(1)} %get-tuple-element.44), channel_id=1, source_target_pairs={{0,4},{4,0},{8,12},{12,8},{1,5},{5,1},{9,13},{13,9},{2,6},{6,2},{1... | collective-permute-start | bytes 196616 | tf_op jit(solution)/shard_map/ppermute | solution.py:407
  19.9 4.4 %collective-permute-start.9 = (bf16[128,256]{1,0:T(8,128)(2,1)S(1)}, bf16[128,256]{1,0:T(8,128)(2,1)S(1)}, u32[]{:S(2)}, u32[]{:S(2)}) collective-permute-start(bf16[128,256]{1,0:T(8,128)(2,1)S(1)} %get-tuple-element.45), channel_id=1, source_target_pairs={{0,8},{4,12},{8,0},{12,4},{1,9},{5,13},{9,1},{13,5},{2,10},{6,14},... | collective-permute-start | bytes 196616 | tf_op jit(solution)/shard_map/ppermute | solution.py:407
  21.6 4.3 %collective-permute-start.10 = (bf16[128,256]{1,0:T(8,128)(2,1)S(1)}, bf16[128,256]{1,0:T(8,128)(2,1)S(1)}, u32[]{:S(2)}, u32[]{:S(2)}) collective-permute-start(bf16[128,256]{1,0:T(8,128)(2,1)S(1)} %get-tuple-element.46), channel_id=1, source_target_pairs={{0,12},{4,8},{8,4},{12,0},{1,13},{5,9},{9,5},{13,1},{2,14},{6,10},... | collective-permute-start | bytes 196616 | tf_op jit(solution)/shard_map/ppermute | solution.py:407

commit v4 on v3

--- a/solution.py
+++ b/solution.py
@@ -238,17 +238,20 @@
     return folded_sum(mxu(back, high)) + mxu(back[:block], rest)
 
 
-def pack_kernel(place_ref, *rest, parts, width):
+def pack_kernel(*rest, parts, width):
     outs, sem = rest[-len(parts) - 1 : -1], rest[-1]
-    here = place_ref[0]
+    here, group = lax.axis_index("seq"), lax.axis_index("groups")
     copies = []
-    for (step, first, last), out in zip(parts, outs):
-        columns = pl.ds(pl.multiple_of((here ^ step) * width, width), width)
-        for n, source in enumerate(rest[first:last]):
+    for (step, columns, shared, arrays), out in zip(parts, outs):
+        start = (here ^ step) * width
+        if shared:
+            start = start + group * columns
+        chosen = pl.ds(pl.multiple_of(start, HEAD_DIM), columns)
+        for n, source in enumerate(rest[i] for i in arrays):
             rows = source.shape[0]
             copies.append(
                 pltpu.make_async_copy(
-                    source.at[:, columns], out.at[n * rows : (n + 1) * rows], sem.at[len(copies)]
+                    source.at[:, chosen], out.at[n * rows : (n + 1) * rows], sem.at[len(copies)]
                 )
             )
     for copy in copies:
@@ -257,26 +260,25 @@
         copy.wait()
 
 
-def conv_kernel(
-    place_ref, own_ref, near_ref, *rest, count, block, head_dim
-):
+def own_columns(ref, here, width):
+    return ref[:, pl.ds(pl.multiple_of(here * width, width), width)]
+
+
+def smooth_kernel(gate_ref, value_ref, near_ref, *rest, count, block):
     arrived = rest[: count - 2]
-    taps_ref, weight_ref, ahead_ref, back_ref, query_ref = rest[count - 2 : count + 3]
-    gate_all, value_all, filter_all = rest[count + 3 :]
-    here = place_ref[0]
+    taps_ref, ahead_ref, back_ref, mixed_ref, gate_all, value_all = rest[count - 2 :]
+    here = lax.axis_index("seq")
     gate_all[0] = jnp.zeros(gate_all.shape[1:], gate_all.dtype)
-    filter_all[0] = jnp.zeros(filter_all.shape[1:], filter_all.dtype)
-    for step, piece in enumerate((own_ref, near_ref, *arrived)):
-        source = here ^ step
-        gate_all[source + 1] = piece[:block]
-        value_all[source] = piece[block : 2 * block]
-        filter_all[source + 1] = piece[2 * block : 3 * block]
+    width = near_ref.shape[1]
+    gate_all[here + 1] = own_columns(gate_ref, here, width)
+    value_all[here] = own_columns(value_ref, here, width)
+    for step, piece in enumerate((near_ref, *arrived), 1):
+        gate_all[(here ^ step) + 1] = piece[:block]
+        value_all[here ^ step] = piece[block : 2 * block]
     ahead = ahead_ref[...]
+    back = back_ref[...]
     first = ahead[:, block:]
-    back = back_ref[...]
     turned = (((1,), (1,)), ((), ()))
-    width = own_ref.shape[1]
-    heads = width // head_dim
     taps = taps_ref[pl.ds(pl.multiple_of(here * width, width), width)]
     taps_high, taps_rest = two_parts(taps)
     taps_spec = folded_sum(
@@ -285,8 +287,6 @@
         first[: 2 * block], taps_rest, turned, preferred_element_type=jnp.float32
     )
     taps_re, taps_im = taps_spec[:block], taps_spec[block:]
-    lines = []
-    kernels = []
     for b in range(count):
         window = jnp.concatenate([gate_all[b], gate_all[b + 1]], axis=0)
         gate_spec = wide_mxu(ahead, window)
@@ -297,8 +297,32 @@
             gate_re * taps_im + gate_im * taps_re,
             block,
         )
-        mixed = (smoothed * value_all[b].astype(jnp.float32)).astype(jnp.bfloat16)
-        lines.append(wide_mxu(first, mixed))
+        mixed_ref[b] = (smoothed * value_all[b].astype(jnp.float32)).astype(jnp.bfloat16)
+
+
+def conv_kernel(mixed_ref, own_ref, near_ref, *rest, count, groups, block, head_dim):
+    far = count - 2
+    shares = rest[:groups]
+    weight_ref, ahead_ref, back_ref, query_ref, filter_all = rest[groups:]
+    here = lax.axis_index("seq")
+    group = lax.axis_index("groups") if groups > 1 else 0
+    filter_all[0] = jnp.zeros(filter_all.shape[1:], filter_all.dtype)
+    filter_all[here + 1] = own_columns(own_ref, here, near_ref.shape[1])
+    filter_all[(here ^ 1) + 1] = near_ref[2 * block : 3 * block]
+    for shift, share in enumerate(shares):
+        columns = share.shape[1]
+        start = lax.rem(group + groups - shift, groups) * columns
+        chosen = pl.ds(pl.multiple_of(start, head_dim), columns)
+        for n in range(far):
+            filter_all[(here ^ (n + 2)) + 1, :, chosen] = share[n * block : (n + 1) * block]
+    ahead = ahead_ref[...]
+    back = back_ref[...]
+    first = ahead[:, block:]
+    heads = mixed_ref.shape[2] // head_dim
+    lines = []
+    kernels = []
+    for b in range(count):
+        lines.append(wide_mxu(first, mixed_ref[b]))
         kernels.append(
             wide_mxu(ahead, jnp.concatenate([filter_all[b], filter_all[b + 1]], axis=0))
         )
@@ -313,17 +337,19 @@
         conv_out = to_block(back, total_re, total_im, block).astype(jnp.bfloat16)
         for h in range(heads):
             columns = slice(h * head_dim, (h + 1) * head_dim)
-            query_ref[b, :, columns] = mxu(conv_out[:, columns], weight_ref[here * heads + h]).astype(
-                jnp.bfloat16
-            )
-
-
-def weigh_kernel(place_ref, query_ref, own_ref, near_ref, *rest, count, block, head_dim):
+            query_ref[b, :, columns] = mxu(
+                conv_out[:, columns], weight_ref[here * heads + h]
+            ).astype(jnp.bfloat16)
+
+
+def weigh_kernel(query_ref, own_ref, near_ref, *rest, count, block, head_dim):
     arrived = rest[: count - 2]
     weight_ref, part_ref, key_all = rest[count - 2 :]
-    here = place_ref[0]
-    for step, piece in enumerate((own_ref, near_ref, *arrived)):
-        key_all[here ^ step] = piece[:block]
+    here = lax.axis_index("seq")
+    key_all[here] = own_columns(own_ref, here, near_ref.shape[1])
+    for step, piece in enumerate((near_ref, *arrived), 1):
+        first = max(piece.shape[0] - 2 * block, 0)
+        key_all[here ^ step] = piece[first : first + block]
     width = query_ref.shape[2]
     turned = (((1,), (1,)), ((), ()))
     scale = 1.0 / math.sqrt(head_dim)
@@ -359,17 +385,18 @@
 
 
 def sum_kernel(
-    place_ref, weight_ref, part_ref, own_ref, near_ref, *rest, count, block, head_dim
+    weight_ref, part_ref, own_ref, near_ref, *rest, count, block, head_dim
 ):
     arrived = rest[: count - 2]
     outs = rest[count - 2 : 2 * count - 2]
     value_all, out_all = rest[2 * count - 2 :]
-    here = place_ref[0]
+    here = lax.axis_index("seq")
 
     def rows_of(b):
         return pl.ds(pl.multiple_of(b * block, block), block)
 
-    for step, piece in enumerate((own_ref, near_ref, *arrived)):
+    value_all[rows_of(here)] = own_columns(own_ref, here, near_ref.shape[1])
+    for step, piece in enumerate((near_ref, *arrived), 1):
         value_all[rows_of(here ^ step)] = piece[-block:]
     for h in range(value_all.shape[1] // head_dim):
         columns = slice(h * head_dim, (h + 1) * head_dim)
@@ -381,13 +408,17 @@
         out[...] = out_all[here ^ step]
 
 
-def join_kernel(place_ref, *rest):
-    pieces, out_ref = rest[:-1], rest[-1]
-    here = place_ref[0]
-    width = pieces[0].shape[1]
-    for step, piece in enumerate(pieces):
-        start = pl.multiple_of((here ^ step) * width, width)
-        out_ref[:, pl.ds(start, width)] = piece[...]
+def join_kernel(*rest, steps, width):
+    pieces, out_ref, sem = rest[: len(steps)], rest[-2], rest[-1]
+    here = lax.axis_index("seq")
+    copies = []
+    for n, (step, piece) in enumerate(zip(steps, pieces)):
+        columns = pl.ds(pl.multiple_of((here ^ step) * width, width), width)
+        copies.append(pltpu.make_async_copy(piece, out_ref.at[:, columns], sem.at[n]))
+    for copy in copies:
+        copy.start()
+    for copy in copies:
+        copy.wait()
 
 
 WHOLE = pl.BlockSpec(memory_space=pltpu.VMEM)
@@ -401,7 +432,7 @@
     width = local_width // count
     heads = width // HEAD_DIM
     here = lax.axis_index("seq")
-    place = here.astype(jnp.int32).reshape(1)
+    groups = lax.axis_size("groups") if heads % lax.axis_size("groups") == 0 else 1
 
     def swap(value, step):
         return lax.ppermute(value, "seq", [(i, i ^ step) for i in range(count)])
@@ -410,91 +441,108 @@
         return pl.pallas_call(
             functools.partial(pack_kernel, parts=parts, width=width),
             out_shape=[
-                pltpu.VMEM(((last - first) * block, width), jnp.bfloat16)
-                for _, first, last in parts
+                pltpu.VMEM((len(chosen) * block, columns), jnp.bfloat16)
+                for _, columns, _, chosen in parts
             ],
-            in_specs=[pl.BlockSpec(memory_space=pltpu.SMEM)]
-            + [pl.BlockSpec(memory_space=pl.ANY)] * (len(arrays) + len(after)),
+            in_specs=[pl.BlockSpec(memory_space=pl.ANY)] * (len(arrays) + len(after)),
             out_specs=[WHOLE] * len(parts),
             scratch_shapes=[
-                pltpu.SemaphoreType.DMA((sum(last - first for _, first, last in parts),))
+                pltpu.SemaphoreType.DMA((sum(len(chosen) for *_, chosen in parts),))
             ],
             compiler_params=params,
-        )(place, *[pltpu.with_memory_space_constraint(a, pltpu.HBM) for a in arrays], *after)
+        )(*[pltpu.with_memory_space_constraint(a, pltpu.HBM) for a in arrays], *after)
 
     ahead, back = block_tables(block)
     scratch = lambda n: pltpu.VMEM((n, block, width), jnp.bfloat16)
     params = pltpu.CompilerParams(vmem_limit_bytes=32 * 1024 * 1024)
     far = range(2, count)
-    streams = [gate_input, value_input, long_filter]
-    first, near = packed(streams, [(far[0], 0, 3), (1, 0, 3)])
+    share = width // groups
+    every = (0, 1, 2, 3, 4)
+    pieces = packed(
+        [gate_input, value_input, long_filter, key_matrix, value_matrix],
+        [(step, share, True, (2,)) for step in far]
+        + [(step, width, False, (0, 1)) for step in far]
+        + [(1, width, False, every)]
+        + [(step, width, False, (3, 4)) for step in far[:-1]]
+        + [(far[-1], width, False, (n,)) for n in (3, 4)],
+    )
+    filters, streams, near, later = (
+        pieces[: len(far)],
+        pieces[len(far) : 2 * len(far)],
+        pieces[2 * len(far)],
+        pieces[2 * len(far) + 1 :],
+    )
     near = swap(near, 1)
-    own, *others = packed(
-        [*streams, key_matrix, value_matrix],
-        [(0, 0, 3)]
-        + [(step, 0, 3) for step in far[1:]]
-        + [(0, 3, 5), (1, 3, 5)]
-        + [(step, n, n + 1) for n in (3, 4) for step in far],
-        after=[near],
-    )
-    arrived = [swap(piece, step) for step, piece in zip(far, [first, *others])]
-    own_later, near_later, *later = others[len(far) - 1 :]
-    near_later = swap(near_later, 1)
-    near_later, *later = lax.optimization_barrier((near_later, *later))
-    later = [swap(piece, step) for step, piece in zip([*far, *far], later)]
-    arrived_keys, arrived_values = later[: len(far)], later[len(far) :]
+    filters = [swap(piece, step) for step, piece in zip(far, filters)]
+    arrived = [swap(piece, step) for step, piece in zip(far, streams)]
+    near, *rest = lax.optimization_barrier((near, *filters, *later))
+    filters, later = rest[: len(far)], rest[len(far) :]
+    shares = [jnp.concatenate(filters)]
+    for shift in range(1, groups):
+        shares.append(
+            lax.ppermute(
+                shares[0], "groups", [(i, (i + shift) % groups) for i in range(groups)]
+            )
+        )
+    later = [swap(piece, step) for step, piece in zip([*far, far[-1]], later)]
+    arrived_keys, arrived_values = later[:-1], [*later[:-2], later[-1]]
+    tables = jnp.asarray(ahead), jnp.asarray(back)
+    streamed = jax.ShapeDtypeStruct((count, block, width), jnp.bfloat16)
+    mixed = pl.pallas_call(
+        functools.partial(smooth_kernel, count=count, block=block),
+        out_shape=streamed,
+        in_specs=[WHOLE] * (count + 4),
+        out_specs=WHOLE,
+        scratch_shapes=[scratch(count + 1), scratch(count)],
+        compiler_params=params,
+    )(gate_input, value_input, near, *arrived, short_filter, *tables)
     queries = pl.pallas_call(
-        functools.partial(conv_kernel, count=count, block=block, head_dim=HEAD_DIM),
-        out_shape=jax.ShapeDtypeStruct((count, block, width), jnp.bfloat16),
-        grid_spec=pltpu.PrefetchScalarGridSpec(
-            num_scalar_prefetch=1,
-            grid=(1,),
-            in_specs=[WHOLE] * count
-            + [WHOLE] * 4,
-            out_specs=WHOLE,
-            scratch_shapes=[scratch(count + 1), scratch(count), scratch(count + 1)],
+        functools.partial(
+            conv_kernel, count=count, groups=groups, block=block, head_dim=HEAD_DIM
         ),
+        out_shape=streamed,
+        in_specs=[WHOLE] * (groups + 6),
+        out_specs=WHOLE,
+        scratch_shapes=[scratch(count + 1)],
         compiler_params=params,
-    )(place, own, near, *arrived, short_filter, query_weight, jnp.asarray(ahead), jnp.asarray(back))
+    )(mixed, long_filter, near, *shares, query_weight, *tables)
     weights, parts = pl.pallas_call(
         functools.partial(weigh_kernel, count=count, block=block, head_dim=HEAD_DIM),
         out_shape=[
             jax.ShapeDtypeStruct((heads, count, block, count * block), jnp.bfloat16),
             jax.ShapeDtypeStruct((heads, count, block, HEAD_DIM), jnp.float32),
         ],
-        grid_spec=pltpu.PrefetchScalarGridSpec(
-            num_scalar_prefetch=1,
-            grid=(1,),
-            in_specs=[WHOLE] * (count + 1),
-            out_specs=[WHOLE] * 2,
-            scratch_shapes=[scratch(count)],
-        ),
+        in_specs=[WHOLE] * (count + 1),
+        out_specs=[WHOLE] * 2,
+        scratch_shapes=[scratch(count)],
         compiler_params=params,
-    )(place, queries, own_later, near_later, *arrived_keys)
+    )(queries, key_matrix, near, *arrived_keys)
     pieces = pl.pallas_call(
         functools.partial(sum_kernel, count=count, block=block, head_dim=HEAD_DIM),
         out_shape=[jax.ShapeDtypeStruct((block, width), jnp.bfloat16)] * count,
-        grid_spec=pltpu.PrefetchScalarGridSpec(
-            num_scalar_prefetch=1,
-            grid=(1,),
-            in_specs=[WHOLE] * (count + 2),
-            out_specs=[WHOLE] * count,
-            scratch_shapes=[
-                pltpu.VMEM((count * block, width), jnp.bfloat16),
-                scratch(count),
-            ],
-        ),
+        in_specs=[WHOLE] * (count + 2),
+        out_specs=[WHOLE] * count,
+        scratch_shapes=[
+            pltpu.VMEM((count * block, width), jnp.bfloat16),
+            scratch(count),
+        ],
         compiler_params=params,
-    )(place, weights, parts, own_later, near_later, *arrived_values)
+    )(weights, parts, value_matrix, near, *arrived_values)
     swapped = {step: swap(pieces[step], step) for step in [*far, 1]}
     pieces = [pieces[0]] + [swapped[step] for step in range(1, count)]
-    return pl.pallas_call(
-        join_kernel,
-        out_shape=jax.ShapeDtypeStruct((block, local_width), jnp.bfloat16),
-        in_specs=[pl.BlockSpec(memory_space=pltpu.SMEM)] + [WHOLE] * count,
-        out_specs=WHOLE,
-        compiler_params=params,
-    )(place, *pieces)
+
+    def joined(steps, *before):
+        return pl.pallas_call(
+            functools.partial(join_kernel, steps=steps, width=width),
+            out_shape=pltpu.HBM((block, local_width), jnp.bfloat16),
+            in_specs=[WHOLE] * len(steps) + [pl.BlockSpec(memory_space=pl.ANY)] * len(before),
+            out_specs=pl.BlockSpec(memory_space=pl.ANY),
+            scratch_shapes=[pltpu.SemaphoreType.DMA((len(steps),))],
+            input_output_aliases={len(steps): 0} if before else {},
+            compiler_params=params,
+        )(*[pieces[step] for step in steps], *before)
+
+    return joined(tuple(far), joined((0, 1)))
 
 
 def shards(*arrays):

time: 26.8 us -> 26.4 us (0.985)
  Pallas kernels: 7.6 us -> 6.85 us
  starting transfers between devices: 10.1 us -> 10.8 us
  waiting for transfers between devices: 8.78 us -> 8.36 us
    ppermute x0 -> x1, starting transfers between devices: none -> 1.72 us  [head_shards(): lax.ppermute(shares[0], 'groups', [(i, (i + shift) % groups) for i in ran...]
    ppermute x11, starting transfers between devices: 10.1 us -> 9.1 us  [swap(): return lax.ppermute(value, 'seq', [(i, i ^ step) for i in range(count)])]
    pallas_call x2 -> x1, Pallas kernels: 2.38 us -> 1.45 us  [packed(): pl.pallas_call(functools.partial(pack_kernel, parts=parts, width=width),...]
    ppermute x11, waiting for transfers between devices: 8.78 us -> 8.36 us  [swap(): return lax.ppermute(value, 'seq', [(i, i ^ step) for i in range(count)])]
    pallas_call x2 -> x4, Pallas kernels: 4.02 us -> 4.19 us  [the longest x1 1.56 us: head_shards(): pl.pallas_call(functools.partial(conv_kernel, count=count, groups=groups,...]
  transfers between devices with their start and end apart: 11 -> 12, of which waited for: 6 -> 8; matrix products, arithmetic and copies ran while one was open for 0% -> 0% of each run, Pallas kernels for 21% -> 17%
where the time goes in v4:
time: 26.4 us; the launch traced here: 26.2 us
  starting transfers between devices  10.8 us (41%)
  waiting for transfers between devices  8.36 us (32%)
  Pallas kernels  6.85 us (26%)
    ppermute x11, starting transfers between devices, swap(): return lax.ppermute(value, 'seq', [(i, i ^ step) for i in range(count)])  9.1 us
    ppermute x11, waiting for transfers between devices, swap(): return lax.ppermute(value, 'seq', [(i, i ^ step) for i in range(count)])  8.36 us
    ppermute x1, starting transfers between devices, head_shards(): lax.ppermute(shares[0], 'groups', [(i, (i + shift) % groups) for i in ran...  1.72 us
    pallas_call x1, Pallas kernels, head_shards(): pl.pallas_call(functools.partial(conv_kernel, count=count, groups=groups,...  1.56 us
    pallas_call x1, Pallas kernels, packed(): pl.pallas_call(functools.partial(pack_kernel, parts=parts, width=width),...  1.45 us
    pallas_call x2, Pallas kernels, joined(): pl.pallas_call(functools.partial(join_kernel, steps=steps, width=width),...  1.33 us
    pallas_call x1, Pallas kernels, head_shards(): pl.pallas_call(functools.partial(smooth_kernel, count=count, block=block)...  1.3 us
    pallas_call x1, Pallas kernels, head_shards(): pl.pallas_call(functools.partial(weigh_kernel, count=count, block=block,...  0.84 us
  transfers between devices with their start and end apart: 12, of which 8 were waited for; matrix products, arithmetic and copies ran while one was open for 0% of the time, Pallas kernels for 17%

profile of v4, /device:TPU:0, one launch (start us, length us, event | category | flops | bytes accessed | tf_op | source)
XLA Modules:
  0.0 26.2 jit_solution(7619578583468345946)
XLA Ops:
  0.0 1.4 %shard_map.91 = (bf16[128,128]{1,0:T(8,128)(2,1)S(1)}, bf16[128,128]{1,0:T(8,128)(2,1)S(1)}, bf16[256,256]{1,0:T(8,128)(2,1)S(1)}, bf16[256,256]{1,0:T(8,128)(2,...) custom-call(bf16[128,1024]{1,0:T(8,128)(2,1)} %gate_ref.1, ...), custom_call_target="tpu_custom_call" | custom-call | tf_op jit(solution)/shard_map/pallas_call | solution.py:441
  1.5 0.5 %collective-permute-start = (bf16[640,256]{1,0:T(8,128)(2,1)S(1)}, bf16[640,256]{1,0:T(8,128)(2,1)S(1)}, u32[]{:S(2)}, u32[]{:S(2)}) collective-permute-start(bf16[640,256]{1,0:T(8,128)(2,1)S(1)} %get-tuple-element.25), channel_id=1, source_target_pairs={{0,4},{4,0},{8,12},{12,8},{1,5},{5,1},{9,13},{13,9},{2,6},{6,2},{1... | collective-permute-start | bytes 983048 | tf_op jit(solution)/shard_map/ppermute | solution.py:438
  2.0 2.6 %collective-permute-start.1 = (bf16[128,128]{1,0:T(8,128)(2,1)S(1)}, bf16[128,128]{1,0:T(8,128)(2,1)S(1)}, u32[]{:S(2)}, u32[]{:S(2)}) collective-permute-start(bf16[128,128]{1,0:T(8,128)(2,1)S(1)} %get-tuple-element.26), channel_id=1, source_target_pairs={{0,8},{4,12},{8,0},{12,4},{1,9},{5,13},{9,1},{13,5},{2,10},{6,14},... | collective-permute-start | bytes 98312 | tf_op jit(solution)/shard_map/ppermute | solution.py:438
  4.6 1.7 %collective-permute-start.3 = (bf16[256,256]{1,0:T(8,128)(2,1)S(1)}, bf16[256,256]{1,0:T(8,128)(2,1)S(1)}, u32[]{:S(2)}, u32[]{:S(2)}) collective-permute-start(bf16[256,256]{1,0:T(8,128)(2,1)S(1)} %get-tuple-element.32), channel_id=1, source_target_pairs={{0,8},{4,12},{8,0},{12,4},{1,9},{5,13},{9,1},{13,5},{2,10},{6,14},... | collective-permute-start | bytes 393224 | tf_op jit(solution)/shard_map/ppermute | solution.py:438
  6.6 1.4 %collective-permute-done.2 = bf16[128,128]{1,0:T(8,128)(2,1)S(1)} collective-permute-done((bf16[128,128]{1,0:T(8,128)(2,1)S(1)}, bf16[128,128]{1,0:T(8,128)(2,1)S(1)}, u32[]{:S(2)}, u32[]{:S(2)}) %collective-permute-start.2) | collective-permute-done | bytes 32800 | tf_op jit(solution)/shard_map/ppermute | solution.py:438
  7.9 0.8 %collective-permute-start.6 = (bf16[256,256]{1,0:T(8,128)(2,1)S(1)}, bf16[256,256]{1,0:T(8,128)(2,1)S(1)}, u32[]{:S(2)}, u32[]{:S(2)}) collective-permute-start(bf16[256,256]{1,0:T(8,128)(2,1)S(1)} %get-tuple-element.36), channel_id=1, source_target_pairs={{0,8},{4,12},{8,0},{12,4},{1,9},{5,13},{9,1},{13,5},{2,10},{6,14},... | collective-permute-start | bytes 393224 | tf_op jit(solution)/shard_map/ppermute | solution.py:438
  8.8 1.7 %collective-permute-start.5 = (bf16[256,128]{1,0:T(8,128)(2,1)S(1)}, bf16[256,128]{1,0:T(8,128)(2,1)S(1)}, u32[]{:S(2)}, u32[]{:S(2)}) collective-permute-start(bf16[256,128]{1,0:T(8,128)(2,1)S(1)} %constant_dynamic-update-slice_fusion.rest_0_), channel_id=1, source_target_pairs={{0,16},{16,0},{1,17},{17,1},{2,18},{18,2},{3,19},{19,3},{4,20},{20... | collective-permute-start | bytes 196616 | tf_op jit(solution)/shard_map/ppermute | solution.py:483
  10.5 0.6 %collective-permute-start.7 = (bf16[128,256]{1,0:T(8,128)(2,1)S(1)}, bf16[128,256]{1,0:T(8,128)(2,1)S(1)}, u32[]{:S(2)}, u32[]{:S(2)}) collective-permute-start(bf16[128,256]{1,0:T(8,128)(2,1)S(1)} %get-tuple-element.37), channel_id=1, source_target_pairs={{0,12},{4,8},{8,4},{12,0},{1,13},{5,9},{9,5},{13,1},{2,14},{6,10},... | collective-permute-start | bytes 196616 | tf_op jit(solution)/shard_map/ppermute | solution.py:438
  11.1 0.3 %collective-permute-done.3.rest_0_ = bf16[256,256]{1,0:T(8,128)(2,1)S(1)} collective-permute-done((bf16[256,256]{1,0:T(8,128)(2,1)S(1)}, bf16[256,256]{1,0:T(8,128)(2,1)S(1)}, u32[]{:S(2)}, u32[]{:S(2)}) %collective-permute-start.3) | collective-permute-done | bytes 131104 | tf_op jit(solution)/shard_map/ppermute | solution.py:438
  11.4 0.8 %collective-permute-start.8 = (bf16[128,256]{1,0:T(8,128)(2,1)S(1)}, bf16[128,256]{1,0:T(8,128)(2,1)S(1)}, u32[]{:S(2)}, u32[]{:S(2)}) collective-permute-start(bf16[128,256]{1,0:T(8,128)(2,1)S(1)} %get-tuple-element.40), channel_id=1, source_target_pairs={{0,12},{4,8},{8,4},{12,0},{1,13},{5,9},{9,5},{13,1},{2,14},{6,10},... | collective-permute-start | bytes 196616 | tf_op jit(solution)/shard_map/ppermute | solution.py:438
  12.2 1.3 %collective-permute-done.4.rest_1_ = bf16[256,256]{1,0:T(8,128)(2,1)S(1)} collective-permute-done((bf16[256,256]{1,0:T(8,128)(2,1)S(1)}, bf16[256,256]{1,0:T(8,128)(2,1)S(1)}, u32[]{:S(2)}, u32[]{:S(2)}) %collective-permute-start.4) | collective-permute-done | bytes 131104 | tf_op jit(solution)/shard_map/ppermute | solution.py:438
  13.6 1.3 %shard_map.92.mixed_ref = bf16[4,128,256]{2,1,0:T(8,128)(2,1)S(1)} custom-call(bf16[128,1024]{1,0:T(8,128)(2,1)S(1)} %copy-done, bf16[128,1024]{1,0:T(8,128)(2,1)S(1)} %copy-done.1, bf16[640,256]{1,0:T(8,128)(2,1)S(1)} %collective-permute-done.near_ref, bf16[256,256]{1,0:T(8,128)(2,1)S(1)} %collective-permute-done.3.rest_0_, ...), custom_call_target="tpu_custom_call" | custom-call | tf_op jit(solution)/shard_map/pallas_call | solution.py:491
  14.9 1.6 %shard_map.93.query_ref = bf16[4,128,256]{2,1,0:T(8,128)(2,1)S(1)} custom-call(bf16[4,128,256]{2,1,0:T(8,128)(2,1)S(1)} %shard_map.92.mixed_ref, bf16[128,1024]{1,0:T(8,128)(2,1)S(1)} %copy-done.4, bf16[640,256]{1,0:T(8,128)(2,1)S(1)} %collective-permute-done.near_ref, bf16[256,128]{1,0:T(8,128)(2,1)S(1)} %constant_dynamic-update-slice_fusion.rest_0_, ...), custom_call_target="tpu_custom_call" | custom-call | tf_op jit(solution)/shard_map/pallas_call | solution.py:499
  16.5 1.3 %collective-permute-done.7.rest_1_ = bf16[128,256]{1,0:T(8,128)(2,1)S(1)} collective-permute-done((bf16[128,256]{1,0:T(8,128)(2,1)S(1)}, bf16[128,256]{1,0:T(8,128)(2,1)S(1)}, u32[]{:S(2)}, u32[]{:S(2)}) %collective-permute-start.7) | collective-permute-done | bytes 65568 | tf_op jit(solution)/shard_map/ppermute | solution.py:438
  17.8 0.8 %shard_map.94 = (bf16[2,4,128,512]{3,2,1,0:T(8,128)(2,1)S(1)}, f32[2,4,128,128]{3,2,1,0:T(8,128)S(1)}) custom-call(bf16[4,128,256]{2,1,0:T(8,128)(2,1)S(1)} %shard_map.93.query_ref, bf16[128,1024]{1,0:T(8,128)(2,1)S(1)} %copy-done.3, bf16[640,256]{1,0:T(8,128)(2,1)S(1)} %collective-permute-done.near_ref, ...), custom_call_target="tpu_custom_call" | custom-call | tf_op jit(solution)/shard_map/pallas_call | solution.py:509
  18.6 0.6 %collective-permute-done.8.rest_1_ = bf16[128,256]{1,0:T(8,128)(2,1)S(1)} collective-permute-done((bf16[128,256]{1,0:T(8,128)(2,1)S(1)}, bf16[128,256]{1,0:T(8,128)(2,1)S(1)}, u32[]{:S(2)}, u32[]{:S(2)}) %collective-permute-start.8) | collective-permute-done | bytes 65568 | tf_op jit(solution)/shard_map/ppermute | solution.py:438
  19.2 0.4 %shard_map.95 = (bf16[128,256]{1,0:T(8,128)(2,1)S(1)}, bf16[128,256]{1,0:T(8,128)(2,1)S(1)}, bf16[128,256]{1,0:T(8,128)(2,1)S(1)}, bf16[128,256]{1,0:T(8,128)(2,1)S(1)}) custom-call(bf16[2,4,128,512]{3,2,1,0:T(8,128)(2,1)S(1)} %get-tuple-element.38.weight_ref, f32[2,4,128,128]{3,2,1,0:T(8,128)S(1)} %get-tuple-element.39.part_ref, ...), custom_call_target="tpu_custom_call" | custom-call | tf_op jit(solution)/shard_map/pallas_call | solution.py:520
  19.5 0.3 %collective-permute-start.11 = (bf16[128,256]{1,0:T(8,128)(2,1)S(1)}, bf16[128,256]{1,0:T(8,128)(2,1)S(1)}, u32[]{:S(2)}, u32[]{:S(2)}) collective-permute-start(bf16[128,256]{1,0:T(8,128)(2,1)S(1)} %get-tuple-element.44), channel_id=1, source_target_pairs={{0,4},{4,0},{8,12},{12,8},{1,5},{5,1},{9,13},{13,9},{2,6},{6,2},{1... | collective-permute-start | bytes 196616 | tf_op jit(solution)/shard_map/ppermute | solution.py:438
  19.9 1.3 %collective-permute-start.9 = (bf16[128,256]{1,0:T(8,128)(2,1)S(1)}, bf16[128,256]{1,0:T(8,128)(2,1)S(1)}, u32[]{:S(2)}, u32[]{:S(2)}) collective-permute-start(bf16[128,256]{1,0:T(8,128)(2,1)S(1)} %get-tuple-element.41), channel_id=1, source_target_pairs={{0,8},{4,12},{8,0},{12,4},{1,9},{5,13},{9,1},{13,5},{2,10},{6,14},... | collective-permute-start | bytes 196616 | tf_op jit(solution)/shard_map/ppermute | solution.py:438
  21.2 0.3 %collective-permute-start.10 = (bf16[128,256]{1,0:T(8,128)(2,1)S(1)}, bf16[128,256]{1,0:T(8,128)(2,1)S(1)}, u32[]{:S(2)}, u32[]{:S(2)}) collective-permute-start(bf16[128,256]{1,0:T(8,128)(2,1)S(1)} %get-tuple-element.42), channel_id=1, source_target_pairs={{0,12},{4,8},{8,4},{12,0},{1,13},{5,9},{9,5},{13,1},{2,14},{6,10},... | collective-permute-start | bytes 196616 | tf_op jit(solution)/shard_map/ppermute | solution.py:438
  21.5 0.7 %shard_map.96.rest_2_ = bf16[128,1024]{1,0:T(8,128)(2,1)} custom-call(bf16[128,256]{1,0:T(8,128)(2,1)S(1)} %get-tuple-element.43.rest_0_, bf16[128,256]{1,0:T(8,128)(2,1)S(1)} %collective-permute-done.11.rest_1_), custom_call_target="tpu_custom_call" | custom-call | tf_op jit(solution)/shard_map/pallas_call | solution.py:535
  22.1 2.0 %collective-permute-done.9.rest_0_ = bf16[128,256]{1,0:T(8,128)(2,1)S(1)} collective-permute-done((bf16[128,256]{1,0:T(8,128)(2,1)S(1)}, bf16[128,256]{1,0:T(8,128)(2,1)S(1)}, u32[]{:S(2)}, u32[]{:S(2)}) %collective-permute-start.9) | collective-permute-done | bytes 65568 | tf_op jit(solution)/shard_map/ppermute | solution.py:438
  24.1 1.4 %collective-permute-done.10.rest_1_ = bf16[128,256]{1,0:T(8,128)(2,1)S(1)} collective-permute-done((bf16[128,256]{1,0:T(8,128)(2,1)S(1)}, bf16[128,256]{1,0:T(8,128)(2,1)S(1)}, u32[]{:S(2)}, u32[]{:S(2)}) %collective-permute-start.10) | collective-permute-done | bytes 65568 | tf_op jit(solution)/shard_map/ppermute | solution.py:438
  25.6 0.7 %shard_map.97 = bf16[128,1024]{1,0:T(8,128)(2,1)} custom-call(bf16[128,256]{1,0:T(8,128)(2,1)S(1)} %collective-permute-done.9.rest_0_, bf16[128,256]{1,0:T(8,128)(2,1)S(1)} %collective-permute-done.10.rest_1_, bf16[128,1024]{1,0:T(8,128)(2,1)} %shard_map.96.rest_2_), custom_call_target="tpu_custom_call", output_to_operand_aliasing={{}: (2, {})} | custom-call | tf_op jit(solution)/shard_map/pallas_call | solution.py:535
  (27 shorter events, 0.3 us)
Async XLA Ops:
  0.0 13.5 %copy-start.6 = (f32[1024,128]{1,0:T(8,128)S(1)}, f32[1024,128]{1,0:T(8,128)}, u32[]{:S(2)}) copy-start(f32[1024,128]{1,0:T(8,128)} %rest_2_.4) | copy-start | bytes 1572868
  0.0 13.5 %copy-start = (bf16[128,1024]{1,0:T(8,128)(2,1)S(1)}, bf16[128,1024]{1,0:T(8,128)(2,1)}, u32[]{:S(2)}) copy-start(bf16[128,1024]{1,0:T(8,128)(2,1)} %gate_ref.1) | copy-start | bytes 786436
  0.0 13.5 %copy-start.1 = (bf16[128,1024]{1,0:T(8,128)(2,1)S(1)}, bf16[128,1024]{1,0:T(8,128)(2,1)}, u32[]{:S(2)}) copy-start(bf16[128,1024]{1,0:T(8,128)(2,1)} %value_ref.1) | copy-start | bytes 786436
  0.0 13.5 %copy-start.5 = (bf16[512,256]{1,0:T(8,128)(2,1)S(1)}, bf16[512,256]{1,0:T(8,128)(2,1)}, u32[]{:S(2)}) copy-start(bf16[512,256]{1,0:T(8,128)(2,1)} %constant.4.clone.rest_3_) | copy-start | bytes 786436
  1.5 12.1 %copy-start.7 = (bf16[256,256]{1,0:T(8,128)(2,1)S(1)}, bf16[256,256]{1,0:T(8,128)(2,1)}, u32[]{:S(2)}) copy-start(bf16[256,256]{1,0:T(8,128)(2,1)} %constant.5.clone.rest_4_) | copy-start | bytes 393220
  1.5 6.4 %collective-permute-start = (bf16[640,256]{1,0:T(8,128)(2,1)S(1)}, bf16[640,256]{1,0:T(8,128)(2,1)S(1)}, u32[]{:S(2)}, u32[]{:S(2)}) collective-permute-start(bf16[640,256]{1,0:T(8,128)(2,1)S(1)} %get-tuple-element.25), channel_id=1, source_target_pairs={{0,4},{4,0},{8,12},{12,8},{1,5},{5,1},{9,13},{13,9},{2,6},{6,2},{1... | collective-permute-start | bytes 983048 | tf_op jit(solution)/shard_map/ppermute | solution.py:438
  2.0 4.5 %collective-permute-start.1 = (bf16[128,128]{1,0:T(8,128)(2,1)S(1)}, bf16[128,128]{1,0:T(8,128)(2,1)S(1)}, u32[]{:S(2)}, u32[]{:S(2)}) collective-permute-start(bf16[128,128]{1,0:T(8,128)(2,1)S(1)} %get-tuple-element.26), channel_id=1, source_target_pairs={{0,8},{4,12},{8,0},{12,4},{1,9},{5,13},{9,1},{13,5},{2,10},{6,14},... | collective-permute-start | bytes 98312 | tf_op jit(solution)/shard_map/ppermute | solution.py:438
  4.6 3.3 %collective-permute-start.2 = (bf16[128,128]{1,0:T(8,128)(2,1)S(1)}, bf16[128,128]{1,0:T(8,128)(2,1)S(1)}, u32[]{:S(2)}, u32[]{:S(2)}) collective-permute-start(bf16[128,128]{1,0:T(8,128)(2,1)S(1)} %get-tuple-element.27), channel_id=1, source_target_pairs={{0,12},{4,8},{8,4},{12,0},{1,13},{5,9},{9,5},{13,1},{2,14},{6,10},... | collective-permute-start | bytes 98312 | tf_op jit(solution)/shard_map/ppermute | solution.py:438
  4.6 6.8 %collective-permute-start.3 = (bf16[256,256]{1,0:T(8,128)(2,1)S(1)}, bf16[256,256]{1,0:T(8,128)(2,1)S(1)}, u32[]{:S(2)}, u32[]{:S(2)}) collective-permute-start(bf16[256,256]{1,0:T(8,128)(2,1)S(1)} %get-tuple-element.32), channel_id=1, source_target_pairs={{0,8},{4,12},{8,0},{12,4},{1,9},{5,13},{9,1},{13,5},{2,10},{6,14},... | collective-permute-start | bytes 393224 | tf_op jit(solution)/shard_map/ppermute | solution.py:438
  6.4 7.2 %collective-permute-start.4 = (bf16[256,256]{1,0:T(8,128)(2,1)S(1)}, bf16[256,256]{1,0:T(8,128)(2,1)S(1)}, u32[]{:S(2)}, u32[]{:S(2)}) collective-permute-start(bf16[256,256]{1,0:T(8,128)(2,1)S(1)} %get-tuple-element.33), channel_id=1, source_target_pairs={{0,12},{4,8},{8,4},{12,0},{1,13},{5,9},{9,5},{13,1},{2,14},{6,10},... | collective-permute-start | bytes 393224 | tf_op jit(solution)/shard_map/ppermute | solution.py:438
  7.9 9.8 %collective-permute-start.6 = (bf16[256,256]{1,0:T(8,128)(2,1)S(1)}, bf16[256,256]{1,0:T(8,128)(2,1)S(1)}, u32[]{:S(2)}, u32[]{:S(2)}) collective-permute-start(bf16[256,256]{1,0:T(8,128)(2,1)S(1)} %get-tuple-element.36), channel_id=1, source_target_pairs={{0,8},{4,12},{8,0},{12,4},{1,9},{5,13},{9,1},{13,5},{2,10},{6,14},... | collective-permute-start | bytes 393224 | tf_op jit(solution)/shard_map/ppermute | solution.py:438
  8.8 6.1 %copy-start.4 = (bf16[128,1024]{1,0:T(8,128)(2,1)S(1)}, bf16[128,1024]{1,0:T(8,128)(2,1)}, u32[]{:S(2)}) copy-start(bf16[128,1024]{1,0:T(8,128)(2,1)} %own_ref.3) | copy-start | bytes 786436
  8.8 6.2 %copy-start.8 = (bf16[8,128,128]{2,1,0:T(8,128)(2,1)S(1)}, bf16[8,128,128]{2,1,0:T(8,128)(2,1)}, u32[]{:S(2)}) copy-start(bf16[8,128,128]{2,1,0:T(8,128)(2,1)} %rest_2_.5) | copy-start | bytes 786436
  8.8 6.1 %collective-permute-start.5 = (bf16[256,128]{1,0:T(8,128)(2,1)S(1)}, bf16[256,128]{1,0:T(8,128)(2,1)S(1)}, u32[]{:S(2)}, u32[]{:S(2)}) collective-permute-start(bf16[256,128]{1,0:T(8,128)(2,1)S(1)} %constant_dynamic-update-slice_fusion.rest_0_), channel_id=1, source_target_pairs={{0,16},{16,0},{1,17},{17,1},{2,18},{18,2},{3,19},{19,3},{4,20},{20... | collective-permute-start | bytes 196616 | tf_op jit(solution)/shard_map/ppermute | solution.py:483
  10.5 7.3 %collective-permute-start.7 = (bf16[128,256]{1,0:T(8,128)(2,1)S(1)}, bf16[128,256]{1,0:T(8,128)(2,1)S(1)}, u32[]{:S(2)}, u32[]{:S(2)}) collective-permute-start(bf16[128,256]{1,0:T(8,128)(2,1)S(1)} %get-tuple-element.37), channel_id=1, source_target_pairs={{0,12},{4,8},{8,4},{12,0},{1,13},{5,9},{9,5},{13,1},{2,14},{6,10},... | collective-permute-start | bytes 196616 | tf_op jit(solution)/shard_map/ppermute | solution.py:438
  11.4 7.7 %collective-permute-start.8 = (bf16[128,256]{1,0:T(8,128)(2,1)S(1)}, bf16[128,256]{1,0:T(8,128)(2,1)S(1)}, u32[]{:S(2)}, u32[]{:S(2)}) collective-permute-start(bf16[128,256]{1,0:T(8,128)(2,1)S(1)} %get-tuple-element.40), channel_id=1, source_target_pairs={{0,12},{4,8},{8,4},{12,0},{1,13},{5,9},{9,5},{13,1},{2,14},{6,10},... | collective-permute-start | bytes 196616 | tf_op jit(solution)/shard_map/ppermute | solution.py:438
  14.9 2.9 %copy-start.3 = (bf16[128,1024]{1,0:T(8,128)(2,1)S(1)}, bf16[128,1024]{1,0:T(8,128)(2,1)}, u32[]{:S(2)}) copy-start(bf16[128,1024]{1,0:T(8,128)(2,1)} %own_ref.4) | copy-start | bytes 786436
  16.5 2.7 %copy-start.2 = (bf16[128,1024]{1,0:T(8,128)(2,1)S(1)}, bf16[128,1024]{1,0:T(8,128)(2,1)}, u32[]{:S(2)}) copy-start(bf16[128,1024]{1,0:T(8,128)(2,1)} %own_ref.5) | copy-start | bytes 786436
  19.5 1.9 %collective-permute-start.11 = (bf16[128,256]{1,0:T(8,128)(2,1)S(1)}, bf16[128,256]{1,0:T(8,128)(2,1)S(1)}, u32[]{:S(2)}, u32[]{:S(2)}) collective-permute-start(bf16[128,256]{1,0:T(8,128)(2,1)S(1)} %get-tuple-element.44), channel_id=1, source_target_pairs={{0,4},{4,0},{8,12},{12,8},{1,5},{5,1},{9,13},{13,9},{2,6},{6,2},{1... | collective-permute-start | bytes 196616 | tf_op jit(solution)/shard_map/ppermute | solution.py:438
  19.9 4.3 %collective-permute-start.9 = (bf16[128,256]{1,0:T(8,128)(2,1)S(1)}, bf16[128,256]{1,0:T(8,128)(2,1)S(1)}, u32[]{:S(2)}, u32[]{:S(2)}) collective-permute-start(bf16[128,256]{1,0:T(8,128)(2,1)S(1)} %get-tuple-element.41), channel_id=1, source_target_pairs={{0,8},{4,12},{8,0},{12,4},{1,9},{5,13},{9,1},{13,5},{2,10},{6,14},... | collective-permute-start | bytes 196616 | tf_op jit(solution)/shard_map/ppermute | solution.py:438
  21.2 4.4 %collective-permute-start.10 = (bf16[128,256]{1,0:T(8,128)(2,1)S(1)}, bf16[128,256]{1,0:T(8,128)(2,1)S(1)}, u32[]{:S(2)}, u32[]{:S(2)}) collective-permute-start(bf16[128,256]{1,0:T(8,128)(2,1)S(1)} %get-tuple-element.42), channel_id=1, source_target_pairs={{0,12},{4,8},{8,4},{12,0},{1,13},{5,9},{9,5},{13,1},{2,14},{6,10},... | collective-permute-start | bytes 196616 | tf_op jit(solution)/shard_map/ppermute | solution.py:438

commit v5 on v4

--- a/solution.py
+++ b/solution.py
@@ -200,10 +200,9 @@
 
 def block_tables(block):
     angle = np.pi / block * (np.arange(block) + 0.5)
-    window = angle[:, None] * (np.arange(2 * block) - block)[None]
-    ahead = np.concatenate([np.cos(window), -np.sin(window)], axis=0)
-    inner = np.arange(block)[:, None] * angle[None]
-    back = np.concatenate([np.cos(inner), -np.sin(inner)], axis=1) / block
+    turns = angle[:, None] * np.arange(block)[None]
+    ahead = np.concatenate([np.cos(turns), -np.sin(turns)], axis=0)
+    back = np.concatenate([np.cos(turns.T), -np.sin(turns.T)], axis=1) / block
 
     def pair(table):
         high = table.astype(ml_dtypes.bfloat16)
@@ -233,25 +232,25 @@
     return mxu(wide, jnp.concatenate([value, value], axis=0))
 
 
-def to_block(back, spec_re, spec_im, block):
-    high, rest = two_parts(jnp.concatenate([spec_re, spec_im], axis=0))
-    return folded_sum(mxu(back, high)) + mxu(back[:block], rest)
+def to_blocks(back, spectra, block):
+    parts = [two_parts(jnp.concatenate(spec, axis=0)) for spec in spectra]
+    main = [mxu(back, high) for high, _ in parts]
+    small = [mxu(back[:block], rest) for _, rest in parts]
+    return [folded_sum(large) + rest for large, rest in zip(main, small)]
 
 
 def pack_kernel(*rest, parts, width):
     outs, sem = rest[-len(parts) - 1 : -1], rest[-1]
     here, group = lax.axis_index("seq"), lax.axis_index("groups")
     copies = []
-    for (step, columns, shared, arrays), out in zip(parts, outs):
-        start = (here ^ step) * width
-        if shared:
-            start = start + group * columns
-        chosen = pl.ds(pl.multiple_of(start, HEAD_DIM), columns)
-        for n, source in enumerate(rest[i] for i in arrays):
+    for (step, columns, blocks), out in zip(parts, outs):
+        for n, (i, slot) in enumerate(blocks):
+            start = (here ^ step) * width + (group if slot is None else slot) * columns
+            source = rest[i].at[:, pl.ds(pl.multiple_of(start, HEAD_DIM), columns)]
             rows = source.shape[0]
             copies.append(
                 pltpu.make_async_copy(
-                    source.at[:, chosen], out.at[n * rows : (n + 1) * rows], sem.at[len(copies)]
+                    source, out.at[n * rows : (n + 1) * rows], sem.at[len(copies)]
                 )
             )
     for copy in copies:
@@ -264,77 +263,106 @@
     return ref[:, pl.ds(pl.multiple_of(here * width, width), width)]
 
 
-def smooth_kernel(gate_ref, value_ref, near_ref, *rest, count, block):
-    arrived = rest[: count - 2]
-    taps_ref, ahead_ref, back_ref, mixed_ref, gate_all, value_all = rest[count - 2 :]
+def with_block_before(spec, before, block):
+    odd = lax.broadcasted_iota(jnp.int32, (block, spec.shape[1]), 0) % 2
+    sign = 1.0 - 2.0 * odd.astype(jnp.float32)
+    return spec[:block] - sign * before[block:], spec[block:] + sign * before[:block]
+
+
+def local_kernel(gate_ref, filter_ref, near_ref, taps_ref, ahead_ref, *outs, block):
+    gate_spec_ref, filter_spec_ref, taps_spec_ref = outs
     here = lax.axis_index("seq")
-    gate_all[0] = jnp.zeros(gate_all.shape[1:], gate_all.dtype)
     width = near_ref.shape[1]
-    gate_all[here + 1] = own_columns(gate_ref, here, width)
-    value_all[here] = own_columns(value_ref, here, width)
-    for step, piece in enumerate((near_ref, *arrived), 1):
-        gate_all[(here ^ step) + 1] = piece[:block]
-        value_all[here ^ step] = piece[block : 2 * block]
     ahead = ahead_ref[...]
-    back = back_ref[...]
-    first = ahead[:, block:]
+    gate_spec_ref[0] = wide_mxu(ahead, own_columns(gate_ref, here, width))
+    gate_spec_ref[1] = wide_mxu(ahead, near_ref[:block])
+    filter_spec_ref[0] = wide_mxu(ahead, own_columns(filter_ref, here, width))
+    filter_spec_ref[1] = wide_mxu(ahead, near_ref[2 * block : 3 * block])
     turned = (((1,), (1,)), ((), ()))
     taps = taps_ref[pl.ds(pl.multiple_of(here * width, width), width)]
     taps_high, taps_rest = two_parts(taps)
-    taps_spec = folded_sum(
-        lax.dot_general(first, taps_high, turned, preferred_element_type=jnp.float32)
+    taps_spec_ref[...] = folded_sum(
+        lax.dot_general(ahead, taps_high, turned, preferred_element_type=jnp.float32)
     ) + lax.dot_general(
-        first[: 2 * block], taps_rest, turned, preferred_element_type=jnp.float32
-    )
-    taps_re, taps_im = taps_spec[:block], taps_spec[block:]
+        ahead[: 2 * block], taps_rest, turned, preferred_element_type=jnp.float32
+    )
+
+
+def smooth_kernel(gate_spec_ref, taps_spec_ref, value_ref, near_ref, *rest, count, block):
+    arrived = rest[: count - 2]
+    ahead_ref, back_ref, line_ref, gate_all, value_all = rest[count - 2 :]
+    here = lax.axis_index("seq")
+    width = near_ref.shape[1]
+    ahead = ahead_ref[...]
+    back = back_ref[...]
+    value_all[here] = own_columns(value_ref, here, width)
+    value_all[here ^ 1] = near_ref[block : 2 * block]
+    gate_all[here] = gate_spec_ref[0]
+    gate_all[here ^ 1] = gate_spec_ref[1]
+    for step, piece in enumerate(arrived, 2):
+        columns = piece.shape[1]
+        slots = width // columns
+
+        def joined(first):
+            return jnp.concatenate(
+                [piece[n * block : (n + 1) * block] for n in range(first, first + slots)], axis=1
+            )
+
+        gate_all[here ^ step] = wide_mxu(ahead, joined(0))
+        value_all[here ^ step] = joined(slots)
+    taps_re, taps_im = taps_spec_ref[:block], taps_spec_ref[block:]
+    spectra = []
     for b in range(count):
-        window = jnp.concatenate([gate_all[b], gate_all[b + 1]], axis=0)
-        gate_spec = wide_mxu(ahead, window)
-        gate_re, gate_im = gate_spec[:block], gate_spec[block:]
-        smoothed = to_block(
-            back,
-            gate_re * taps_re - gate_im * taps_im,
-            gate_re * taps_im + gate_im * taps_re,
-            block,
+        gate_spec = gate_all[b]
+        if b > 0:
+            gate_re, gate_im = with_block_before(gate_spec, gate_all[b - 1], block)
+        else:
+            gate_re, gate_im = gate_spec[:block], gate_spec[block:]
+        spectra.append(
+            (gate_re * taps_re - gate_im * taps_im, gate_re * taps_im + gate_im * taps_re)
         )
-        mixed_ref[b] = (smoothed * value_all[b].astype(jnp.float32)).astype(jnp.bfloat16)
-
-
-def conv_kernel(mixed_ref, own_ref, near_ref, *rest, count, groups, block, head_dim):
+    mixed = [
+        (smoothed * value_all[b].astype(jnp.float32)).astype(jnp.bfloat16)
+        for b, smoothed in enumerate(to_blocks(back, spectra, block))
+    ]
+    for b in range(count):
+        line_ref[b] = wide_mxu(ahead, mixed[b])
+
+
+def conv_kernel(line_ref, filter_spec_ref, *rest, count, groups, block, head_dim):
     far = count - 2
-    shares = rest[:groups]
-    weight_ref, ahead_ref, back_ref, query_ref, filter_all = rest[groups:]
+    shares = [rest[n * far : (n + 1) * far] for n in range(groups)]
+    weight_ref, ahead_ref, back_ref, query_ref, filter_all, spec_all = rest[groups * far :]
     here = lax.axis_index("seq")
     group = lax.axis_index("groups") if groups > 1 else 0
-    filter_all[0] = jnp.zeros(filter_all.shape[1:], filter_all.dtype)
-    filter_all[here + 1] = own_columns(own_ref, here, near_ref.shape[1])
-    filter_all[(here ^ 1) + 1] = near_ref[2 * block : 3 * block]
-    for shift, share in enumerate(shares):
-        columns = share.shape[1]
-        start = lax.rem(group + groups - shift, groups) * columns
-        chosen = pl.ds(pl.multiple_of(start, head_dim), columns)
-        for n in range(far):
-            filter_all[(here ^ (n + 2)) + 1, :, chosen] = share[n * block : (n + 1) * block]
+    for shift, pieces in enumerate(shares):
+        for n, piece in enumerate(pieces):
+            columns = piece.shape[1]
+            start = lax.rem(group + groups - shift, groups) * columns
+            chosen = pl.ds(pl.multiple_of(start, head_dim), columns)
+            filter_all[n, :, chosen] = piece[piece.shape[0] - block :]
     ahead = ahead_ref[...]
     back = back_ref[...]
-    first = ahead[:, block:]
-    heads = mixed_ref.shape[2] // head_dim
-    lines = []
-    kernels = []
-    for b in range(count):
-        lines.append(wide_mxu(first, mixed_ref[b]))
-        kernels.append(
-            wide_mxu(ahead, jnp.concatenate([filter_all[b], filter_all[b + 1]], axis=0))
-        )
+    heads = line_ref.shape[2] // head_dim
+    spec_all[here] = filter_spec_ref[0]
+    spec_all[here ^ 1] = filter_spec_ref[1]
+    for n in range(far):
+        spec_all[here ^ (n + 2)] = wide_mxu(ahead, filter_all[n])
+    lines = [(line_ref[b, :block], line_ref[b, block:]) for b in range(count)]
+    kernels = [(spec_all[0, :block], spec_all[0, block:])] + [
+        with_block_before(spec_all[b], spec_all[b - 1], block) for b in range(1, count)
+    ]
+    totals = []
     for b in range(count):
         total_re, total_im = 0.0, 0.0
         for j in range(b + 1):
-            line, kernel = lines[j], kernels[b - j]
-            line_re, line_im = line[:block], line[block:]
-            kernel_re, kernel_im = kernel[:block], kernel[block:]
+            line_re, line_im = lines[j]
+            kernel_re, kernel_im = kernels[b - j]
             total_re = total_re + (line_re * kernel_re - line_im * kernel_im)
             total_im = total_im + (line_re * kernel_im + line_im * kernel_re)
-        conv_out = to_block(back, total_re, total_im, block).astype(jnp.bfloat16)
+        totals.append((total_re, total_im))
+    for b, conv_out in enumerate(to_blocks(back, totals, block)):
+        conv_out = conv_out.astype(jnp.bfloat16)
         for h in range(heads):
             columns = slice(h * head_dim, (h + 1) * head_dim)
             query_ref[b, :, columns] = mxu(
@@ -356,32 +384,31 @@
     row = lax.broadcasted_iota(jnp.int32, (block, block), 0)
     column = lax.broadcasted_iota(jnp.int32, (block, block), 1)
     allowed = column <= row
-    for h in range(width // head_dim):
+    places = [(h, b) for h in range(width // head_dim) for b in range(count)]
+    scores = []
+    for h, b in places:
         columns = slice(h * head_dim, (h + 1) * head_dim)
-        for b in range(count):
-            query = query_ref[b, :, columns]
-            scores = []
-            for j in range(b + 1):
-                part = (
-                    lax.dot_general(
-                        query,
-                        key_all[j, :, columns],
-                        turned,
-                        preferred_element_type=jnp.float32,
-                    )
-                    * scale
-                )
-                scores.append(jnp.where(allowed, part, -1e30) if j == b else part)
-            peak = functools.reduce(jnp.maximum, scores)
-            peak = jnp.max(peak, axis=1, keepdims=True)
-            weights = [jnp.exp(part - peak) for part in scores]
-            weights[b] = jnp.where(allowed, weights[b], 0.0)
-            weight_sum = jnp.sum(functools.reduce(jnp.add, weights), axis=1, keepdims=True)
-            part_ref[h, b] = jnp.broadcast_to(1.0 / weight_sum, (block, head_dim))
-            for j in range(b + 1):
-                weight_ref[h, b, :, j * block : (j + 1) * block] = weights[j].astype(
-                    jnp.bfloat16
-                )
+        query = query_ref[b, :, columns]
+        parts = []
+        for j in range(b + 1):
+            part = lax.dot_general(
+                query, key_all[j, :, columns], turned, preferred_element_type=jnp.float32
+            )
+            part = part * scale
+            parts.append(jnp.where(allowed, part, -1e30) if j == b else part)
+        scores.append(parts)
+    peaks = [
+        jnp.max(functools.reduce(jnp.maximum, parts), axis=1, keepdims=True) for parts in scores
+    ]
+    sums = []
+    for (h, b), parts, peak in zip(places, scores, peaks):
+        weights = [jnp.exp(part - peak) for part in parts]
+        weights[b] = jnp.where(allowed, weights[b], 0.0)
+        sums.append(jnp.sum(functools.reduce(jnp.add, weights), axis=1, keepdims=True))
+        for j in range(b + 1):
+            weight_ref[h, b, :, j * block : (j + 1) * block] = weights[j].astype(jnp.bfloat16)
+    for (h, b), weight_sum in zip(places, sums):
+        part_ref[h, b] = jnp.broadcast_to(1.0 / weight_sum, (block, head_dim))
 
 
 def sum_kernel(
@@ -442,7 +469,7 @@
             functools.partial(pack_kernel, parts=parts, width=width),
             out_shape=[
                 pltpu.VMEM((len(chosen) * block, columns), jnp.bfloat16)
-                for _, columns, _, chosen in parts
+                for _, columns, chosen in parts
             ],
             in_specs=[pl.BlockSpec(memory_space=pl.ANY)] * (len(arrays) + len(after)),
             out_specs=[WHOLE] * len(parts),
@@ -457,55 +484,61 @@
     params = pltpu.CompilerParams(vmem_limit_bytes=32 * 1024 * 1024)
     far = range(2, count)
     share = width // groups
-    every = (0, 1, 2, 3, 4)
+    slots = range(groups)
+    streams = [(i, slot) for i in (0, 1) for slot in slots] + [(2, None)]
+    arrays = [gate_input, value_input, long_filter, key_matrix, value_matrix]
+    first, near = packed(
+        arrays, [(far[0], share, streams), (1, width, [(n, 0) for n in range(5)])]
+    )
+    near = swap(near, 1)
     pieces = packed(
-        [gate_input, value_input, long_filter, key_matrix, value_matrix],
-        [(step, share, True, (2,)) for step in far]
-        + [(step, width, False, (0, 1)) for step in far]
-        + [(1, width, False, every)]
-        + [(step, width, False, (3, 4)) for step in far[:-1]]
-        + [(far[-1], width, False, (n,)) for n in (3, 4)],
-    )
-    filters, streams, near, later = (
-        pieces[: len(far)],
-        pieces[len(far) : 2 * len(far)],
-        pieces[2 * len(far)],
-        pieces[2 * len(far) + 1 :],
-    )
-    near = swap(near, 1)
-    filters = [swap(piece, step) for step, piece in zip(far, filters)]
-    arrived = [swap(piece, step) for step, piece in zip(far, streams)]
-    near, *rest = lax.optimization_barrier((near, *filters, *later))
-    filters, later = rest[: len(far)], rest[len(far) :]
-    shares = [jnp.concatenate(filters)]
-    for shift in range(1, groups):
-        shares.append(
-            lax.ppermute(
-                shares[0], "groups", [(i, (i + shift) % groups) for i in range(groups)]
-            )
-        )
+        arrays,
+        [(step, share, streams) for step in far[1:]]
+        + [(step, width, [(3, 0), (4, 0)]) for step in far[:-1]]
+        + [(far[-1], width, [(n, 0)]) for n in (3, 4)],
+        after=[near],
+    )
+    arrived = [swap(piece, step) for step, piece in zip(far, [first, *pieces])]
+    later = pieces[len(far) - 1 :]
+    filters = [piece[-block:] for piece in arrived]
+    shares = arrived + [
+        lax.ppermute(piece, "groups", [(i, (i + shift) % groups) for i in range(groups)])
+        for shift in range(1, groups)
+        for piece in filters
+    ]
     later = [swap(piece, step) for step, piece in zip([*far, far[-1]], later)]
     arrived_keys, arrived_values = later[:-1], [*later[:-2], later[-1]]
     tables = jnp.asarray(ahead), jnp.asarray(back)
-    streamed = jax.ShapeDtypeStruct((count, block, width), jnp.bfloat16)
-    mixed = pl.pallas_call(
+    spectra = lambda n: (n, 2 * block, width)
+    gate_spec, filter_spec, taps_spec = pl.pallas_call(
+        functools.partial(local_kernel, block=block),
+        out_shape=[
+            jax.ShapeDtypeStruct(spectra(2), jnp.float32),
+            jax.ShapeDtypeStruct(spectra(2), jnp.float32),
+            jax.ShapeDtypeStruct((2 * block, width), jnp.float32),
+        ],
+        in_specs=[WHOLE] * 5,
+        out_specs=[WHOLE] * 3,
+        compiler_params=params,
+    )(gate_input, long_filter, near, short_filter, tables[0])
+    lines = pl.pallas_call(
         functools.partial(smooth_kernel, count=count, block=block),
-        out_shape=streamed,
+        out_shape=jax.ShapeDtypeStruct(spectra(count), jnp.float32),
         in_specs=[WHOLE] * (count + 4),
         out_specs=WHOLE,
-        scratch_shapes=[scratch(count + 1), scratch(count)],
+        scratch_shapes=[pltpu.VMEM(spectra(count), jnp.float32), scratch(count)],
         compiler_params=params,
-    )(gate_input, value_input, near, *arrived, short_filter, *tables)
+    )(gate_spec, taps_spec, value_input, near, *arrived, *tables)
     queries = pl.pallas_call(
         functools.partial(
             conv_kernel, count=count, groups=groups, block=block, head_dim=HEAD_DIM
         ),
-        out_shape=streamed,
-        in_specs=[WHOLE] * (groups + 6),
+        out_shape=jax.ShapeDtypeStruct((count, block, width), jnp.bfloat16),
+        in_specs=[WHOLE] * (groups * len(far) + 5),
         out_specs=WHOLE,
-        scratch_shapes=[scratch(count + 1)],
+        scratch_shapes=[scratch(len(far)), pltpu.VMEM(spectra(count), jnp.float32)],
         compiler_params=params,
-    )(mixed, long_filter, near, *shares, query_weight, *tables)
+    )(lines, filter_spec, *shares, query_weight, *tables)
     weights, parts = pl.pallas_call(
         functools.partial(weigh_kernel, count=count, block=block, head_dim=HEAD_DIM),
         out_shape=[

time: 26.4 us -> 25.6 us (0.970)
  waiting for transfers between devices: 8.36 us -> 5.36 us
  starting transfers between devices: 10.8 us -> 12.2 us
  Pallas kernels: 6.85 us -> 7.51 us
    ppermute x11 -> x9, waiting for transfers between devices: 8.36 us -> 4.53 us  [swap(): return lax.ppermute(value, 'seq', [(i, i ^ step) for i in range(count)])]
    ppermute x1 -> x2, starting transfers between devices: 1.72 us -> 3.62 us  [head_shards(): lax.ppermute(piece, 'groups', [(i, (i + shift) % groups) for i in range(g...]
    pallas_call x1 -> x2, Pallas kernels: 1.45 us -> 2.31 us  [packed(): pl.pallas_call(functools.partial(pack_kernel, parts=parts, width=width),...]
    ppermute x1 -> x2, waiting for transfers between devices: 0.01 us -> 0.83 us  [head_shards(): lax.ppermute(piece, 'groups', [(i, (i + shift) % groups) for i in range(g...]
    ppermute x11 -> x9, starting transfers between devices: 9.1 us -> 8.62 us  [swap(): return lax.ppermute(value, 'seq', [(i, i ^ step) for i in range(count)])]
    pallas_call x0 -> x1, Pallas kernels: none -> 0.41 us  [head_shards(): pl.pallas_call(functools.partial(local_kernel, block=block), out_shape=[j...]
    pallas_call x1, Pallas kernels: 1.56 us -> 1.19 us  [head_shards(): pl.pallas_call(functools.partial(conv_kernel, count=count, groups=groups,...]
  transfers between devices with their start and end apart: 12 -> 11, of which waited for: 8 -> 5; matrix products, arithmetic and copies ran while one was open for 0% -> 0% of each run, Pallas kernels for 17% -> 21%
where the time goes in v5:
time: 25.6 us; the launch traced here: 25.4 us
  starting transfers between devices  12.2 us (48%)
  Pallas kernels  7.51 us (29%)
  waiting for transfers between devices  5.36 us (21%)
    ppermute x9, starting transfers between devices, swap(): return lax.ppermute(value, 'seq', [(i, i ^ step) for i in range(count)])  8.62 us
    ppermute x9, waiting for transfers between devices, swap(): return lax.ppermute(value, 'seq', [(i, i ^ step) for i in range(count)])  4.53 us
    ppermute x2, starting transfers between devices, head_shards(): lax.ppermute(piece, 'groups', [(i, (i + shift) % groups) for i in range(g...  3.62 us
    pallas_call x2, Pallas kernels, packed(): pl.pallas_call(functools.partial(pack_kernel, parts=parts, width=width),...  2.31 us
    pallas_call x2, Pallas kernels, joined(): pl.pallas_call(functools.partial(join_kernel, steps=steps, width=width),...  1.33 us
    pallas_call x1, Pallas kernels, head_shards(): pl.pallas_call(functools.partial(conv_kernel, count=count, groups=groups,...  1.19 us
    pallas_call x1, Pallas kernels, head_shards(): pl.pallas_call(functools.partial(smooth_kernel, count=count, block=block)...  1.05 us
    pallas_call x1, Pallas kernels, head_shards(): pl.pallas_call(functools.partial(weigh_kernel, count=count, block=block,...  0.84 us
  transfers between devices with their start and end apart: 11, of which 5 were waited for; matrix products, arithmetic and copies ran while one was open for 0% of the time, Pallas kernels for 21%

profile of v5, /device:TPU:0, one launch (start us, length us, event | category | flops | bytes accessed | tf_op | source)
XLA Modules:
  0.0 25.4 jit_solution(11140459381939850421)
XLA Ops:
  0.0 1.2 %shard_map.91 = (bf16[640,128]{1,0:T(8,128)(2,1)S(1)}, bf16[640,256]{1,0:T(8,128)(2,1)S(1)}) custom-call(bf16[128,1024]{1,0:T(8,128)(2,1)} %rest_0_.3, bf16[128,1024]{1,0:T(8,128)(2,1)} %value_ref.1, bf16[128,1024]{1,0:T(8,128)(2,1)} %rest_2_.4, bf16[128,1024]{1,0:T(8,128)(2,1)} %own_ref.2, bf16[128,1024]{1,0:T(8,128)(2,1)} %own_ref.3), custom_call_target="tpu_custom_call" | custom-call | tf_op jit(solution)/shard_map/pallas_call | solution.py:468
  1.2 0.5 %collective-permute-start = (bf16[640,256]{1,0:T(8,128)(2,1)S(1)}, bf16[640,256]{1,0:T(8,128)(2,1)S(1)}, u32[]{:S(2)}, u32[]{:S(2)}) collective-permute-start(bf16[640,256]{1,0:T(8,128)(2,1)S(1)} %get-tuple-element.20), channel_id=1, source_target_pairs={{0,4},{4,0},{8,12},{12,8},{1,5},{5,1},{9,13},{13,9},{2,6},{6,2},{1... | collective-permute-start | bytes 983048 | tf_op jit(solution)/shard_map/ppermute | solution.py:465
  1.7 2.6 %collective-permute-start.1 = (bf16[640,128]{1,0:T(8,128)(2,1)S(1)}, bf16[640,128]{1,0:T(8,128)(2,1)S(1)}, u32[]{:S(2)}, u32[]{:S(2)}) collective-permute-start(bf16[640,128]{1,0:T(8,128)(2,1)S(1)} %get-tuple-element.23), channel_id=1, source_target_pairs={{0,8},{4,12},{8,0},{12,4},{1,9},{5,13},{9,1},{13,5},{2,10},{6,14},... | collective-permute-start | bytes 491528 | tf_op jit(solution)/shard_map/ppermute | solution.py:465
  4.3 1.2 %shard_map.93 = (bf16[640,128]{1,0:T(8,128)(2,1)S(1)}, bf16[256,256]{1,0:T(8,128)(2,1)S(1)}, bf16[128,256]{1,0:T(8,128)(2,1)S(1)}, bf16[128,256]{1,0:T(8,128)(2,1)S(1)}) custom-call(bf16[128,1024]{1,0:T(8,128)(2,1)} %rest_0_.3, bf16[128,1024]{1,0:T(8,128)(2,1)} %value_ref.1, bf16[128,1024]{1,0:T(8,128)(2,1)} %rest_2_.4, bf16[128,1024]{1,0:T(8,128)(2,1)} %own_ref.2, ...), custom_call_target="tpu_custom_call" | custom-call | tf_op jit(solution)/shard_map/pallas_call | solution.py:468
  5.4 1.3 %collective-permute-start.2 = (bf16[640,128]{1,0:T(8,128)(2,1)S(1)}, bf16[640,128]{1,0:T(8,128)(2,1)S(1)}, u32[]{:S(2)}, u32[]{:S(2)}) collective-permute-start(bf16[640,128]{1,0:T(8,128)(2,1)S(1)} %get-tuple-element.24), channel_id=1, source_target_pairs={{0,12},{4,8},{8,4},{12,0},{1,13},{5,9},{9,5},{13,1},{2,14},{6,10},... | collective-permute-start | bytes 491528 | tf_op jit(solution)/shard_map/ppermute | solution.py:465
  6.8 0.5 %collective-permute-start.5 = (bf16[256,256]{1,0:T(8,128)(2,1)S(1)}, bf16[256,256]{1,0:T(8,128)(2,1)S(1)}, u32[]{:S(2)}, u32[]{:S(2)}) collective-permute-start(bf16[256,256]{1,0:T(8,128)(2,1)S(1)} %get-tuple-element.26), channel_id=1, source_target_pairs={{0,8},{4,12},{8,0},{12,4},{1,9},{5,13},{9,1},{13,5},{2,10},{6,14},... | collective-permute-start | bytes 393224 | tf_op jit(solution)/shard_map/ppermute | solution.py:465
  7.3 1.2 %collective-permute-start.6 = (bf16[128,256]{1,0:T(8,128)(2,1)S(1)}, bf16[128,256]{1,0:T(8,128)(2,1)S(1)}, u32[]{:S(2)}, u32[]{:S(2)}) collective-permute-start(bf16[128,256]{1,0:T(8,128)(2,1)S(1)} %get-tuple-element.27), channel_id=1, source_target_pairs={{0,12},{4,8},{8,4},{12,0},{1,13},{5,9},{9,5},{13,1},{2,14},{6,10},... | collective-permute-start | bytes 196616 | tf_op jit(solution)/shard_map/ppermute | solution.py:465
  8.5 0.5 %collective-permute-start.7 = (bf16[128,256]{1,0:T(8,128)(2,1)S(1)}, bf16[128,256]{1,0:T(8,128)(2,1)S(1)}, u32[]{:S(2)}, u32[]{:S(2)}) collective-permute-start(bf16[128,256]{1,0:T(8,128)(2,1)S(1)} %get-tuple-element.30), channel_id=1, source_target_pairs={{0,12},{4,8},{8,4},{12,0},{1,13},{5,9},{9,5},{13,1},{2,14},{6,10},... | collective-permute-start | bytes 196616 | tf_op jit(solution)/shard_map/ppermute | solution.py:465
  9.0 0.3 %collective-permute-done.1.rest_0_ = bf16[640,128]{1,0:T(8,128)(2,1)S(1)} collective-permute-done((bf16[640,128]{1,0:T(8,128)(2,1)S(1)}, bf16[640,128]{1,0:T(8,128)(2,1)S(1)}, u32[]{:S(2)}, u32[]{:S(2)}) %collective-permute-start.1) | collective-permute-done | bytes 163872 | tf_op jit(solution)/shard_map/ppermute | solution.py:465
  9.3 2.0 %collective-permute-start.3 = (bf16[128,128]{1,0:T(8,128)(2,1)S(1)}, bf16[128,128]{1,0:T(8,128)(2,1)S(1)}, u32[]{:S(2)}, u32[]{:S(2)}) collective-permute-start(bf16[128,128]{1,0:T(8,128)(2,1)S(1)} %slice.8), channel_id=1, source_target_pairs={{0,16},{16,0},{1,17},{17,1},{2,18},{18,2},{3,19},{19,3},{4,20},{20... | collective-permute-start | bytes 98312 | tf_op jit(solution)/shard_map/ppermute | solution.py:505
  11.3 1.0 %collective-permute-done.2.rest_1_ = bf16[640,128]{1,0:T(8,128)(2,1)S(1)} collective-permute-done((bf16[640,128]{1,0:T(8,128)(2,1)S(1)}, bf16[640,128]{1,0:T(8,128)(2,1)S(1)}, u32[]{:S(2)}, u32[]{:S(2)}) %collective-permute-start.2) | collective-permute-done | bytes 163872 | tf_op jit(solution)/shard_map/ppermute | solution.py:465
  12.3 1.6 %collective-permute-start.4 = (bf16[128,128]{1,0:T(8,128)(2,1)S(1)}, bf16[128,128]{1,0:T(8,128)(2,1)S(1)}, u32[]{:S(2)}, u32[]{:S(2)}) collective-permute-start(bf16[128,128]{1,0:T(8,128)(2,1)S(1)} %slice.9), channel_id=1, source_target_pairs={{0,16},{16,0},{1,17},{17,1},{2,18},{18,2},{3,19},{19,3},{4,20},{20... | collective-permute-start | bytes 98312 | tf_op jit(solution)/shard_map/ppermute | solution.py:505
  14.0 0.4 %shard_map.92 = (f32[2,256,256]{2,1,0:T(8,128)S(1)}, f32[2,256,256]{2,1,0:T(8,128)S(1)}, f32[256,256]{1,0:T(8,128)S(1)}) custom-call(bf16[128,1024]{1,0:T(8,128)(2,1)S(1)} %copy-done.2, bf16[128,1024]{1,0:T(8,128)(2,1)S(1)} %copy-done.3, bf16[640,256]{1,0:T(8,128)(2,1)S(1)} %collective-permute-done.near_ref.rest_5_, f32[1024,128]{1,0:T(8,128)S(1)} %copy-done.6, ...), custom_call_target="tpu_custom_call" | custom-call | tf_op jit(solution)/shard_map/pallas_call | solution.py:513
  14.4 1.0 %shard_map.94.line_ref = f32[4,256,256]{2,1,0:T(8,128)S(1)} custom-call(f32[2,256,256]{2,1,0:T(8,128)S(1)} %get-tuple-element.21.gate_spec_ref, f32[256,256]{1,0:T(8,128)S(1)} %get-tuple-element.22.taps_spec_ref, bf16[128,1024]{1,0:T(8,128)(2,1)S(1)} %copy-done, bf16[640,256]{1,0:T(8,128)(2,1)S(1)} %collective-permute-done.near_ref.rest_5_, ...), custom_call_target="tpu_custom_call" | custom-call | tf_op jit(solution)/shard_map/pallas_call | solution.py:524
  15.5 0.8 %collective-permute-done.4.rest_3_ = bf16[128,128]{1,0:T(8,128)(2,1)S(1)} collective-permute-done((bf16[128,128]{1,0:T(8,128)(2,1)S(1)}, bf16[128,128]{1,0:T(8,128)(2,1)S(1)}, u32[]{:S(2)}, u32[]{:S(2)}) %collective-permute-start.4) | collective-permute-done | bytes 32800 | tf_op jit(solution)/shard_map/ppermute | solution.py:505
  16.3 1.2 %shard_map.95.query_ref = bf16[4,128,256]{2,1,0:T(8,128)(2,1)S(1)} custom-call(f32[4,256,256]{2,1,0:T(8,128)S(1)} %shard_map.94.line_ref, f32[2,256,256]{2,1,0:T(8,128)S(1)} %get-tuple-element.25.filter_spec_ref, bf16[640,128]{1,0:T(8,128)(2,1)S(1)} %collective-permute-done.1.rest_0_, bf16[640,128]{1,0:T(8,128)(2,1)S(1)} %collective-permute-done.2.rest_1_, ...), custom_call_target="tpu_custom_call" | custom-call | tf_op jit(solution)/shard_map/pallas_call | solution.py:532
  17.5 0.8 %shard_map.96 = (bf16[2,4,128,512]{3,2,1,0:T(8,128)(2,1)S(1)}, f32[2,4,128,128]{3,2,1,0:T(8,128)S(1)}) custom-call(bf16[4,128,256]{2,1,0:T(8,128)(2,1)S(1)} %shard_map.95.query_ref, bf16[128,1024]{1,0:T(8,128)(2,1)S(1)} %copy-done.4, bf16[640,256]{1,0:T(8,128)(2,1)S(1)} %collective-permute-done.near_ref.rest_5_, ...), custom_call_target="tpu_custom_call" | custom-call | tf_op jit(solution)/shard_map/pallas_call | solution.py:542
  18.4 0.4 %shard_map.97 = (bf16[128,256]{1,0:T(8,128)(2,1)S(1)}, bf16[128,256]{1,0:T(8,128)(2,1)S(1)}, bf16[128,256]{1,0:T(8,128)(2,1)S(1)}, bf16[128,256]{1,0:T(8,128)(2,1)S(1)}) custom-call(bf16[2,4,128,512]{3,2,1,0:T(8,128)(2,1)S(1)} %get-tuple-element.28.weight_ref, f32[2,4,128,128]{3,2,1,0:T(8,128)S(1)} %get-tuple-element.29.part_ref, ...), custom_call_target="tpu_custom_call" | custom-call | tf_op jit(solution)/shard_map/pallas_call | solution.py:553
  18.9 1.7 %collective-permute-start.8 = (bf16[128,256]{1,0:T(8,128)(2,1)S(1)}, bf16[128,256]{1,0:T(8,128)(2,1)S(1)}, u32[]{:S(2)}, u32[]{:S(2)}) collective-permute-start(bf16[128,256]{1,0:T(8,128)(2,1)S(1)} %get-tuple-element.31), channel_id=1, source_target_pairs={{0,8},{4,12},{8,0},{12,4},{1,9},{5,13},{9,1},{13,5},{2,10},{6,14},... | collective-permute-start | bytes 196616 | tf_op jit(solution)/shard_map/ppermute | solution.py:465
  20.7 0.1 collective-permute-start.9
  20.8 0.7 %shard_map.98.rest_2_ = bf16[128,1024]{1,0:T(8,128)(2,1)} custom-call(bf16[128,256]{1,0:T(8,128)(2,1)S(1)} %get-tuple-element.33.rest_0_, bf16[128,256]{1,0:T(8,128)(2,1)S(1)} %collective-permute-done.10.rest_1_), custom_call_target="tpu_custom_call" | custom-call | tf_op jit(solution)/shard_map/pallas_call | solution.py:568
  21.5 2.0 %collective-permute-done.8.rest_0_ = bf16[128,256]{1,0:T(8,128)(2,1)S(1)} collective-permute-done((bf16[128,256]{1,0:T(8,128)(2,1)S(1)}, bf16[128,256]{1,0:T(8,128)(2,1)S(1)}, u32[]{:S(2)}, u32[]{:S(2)}) %collective-permute-start.8) | collective-permute-done | bytes 65568 | tf_op jit(solution)/shard_map/ppermute | solution.py:465
  23.4 1.3 %collective-permute-done.9.rest_1_ = bf16[128,256]{1,0:T(8,128)(2,1)S(1)} collective-permute-done((bf16[128,256]{1,0:T(8,128)(2,1)S(1)}, bf16[128,256]{1,0:T(8,128)(2,1)S(1)}, u32[]{:S(2)}, u32[]{:S(2)}) %collective-permute-start.9) | collective-permute-done | bytes 65568 | tf_op jit(solution)/shard_map/ppermute | solution.py:465
  24.7 0.7 %shard_map.99 = bf16[128,1024]{1,0:T(8,128)(2,1)} custom-call(bf16[128,256]{1,0:T(8,128)(2,1)S(1)} %collective-permute-done.8.rest_0_, bf16[128,256]{1,0:T(8,128)(2,1)S(1)} %collective-permute-done.9.rest_1_, bf16[128,1024]{1,0:T(8,128)(2,1)} %shard_map.98.rest_2_), custom_call_target="tpu_custom_call", output_to_operand_aliasing={{}: (2, {})} | custom-call | tf_op jit(solution)/shard_map/pallas_call | solution.py:568
  (27 shorter events, 0.2 us)
Async XLA Ops:
  1.2 3.1 %collective-permute-start = (bf16[640,256]{1,0:T(8,128)(2,1)S(1)}, bf16[640,256]{1,0:T(8,128)(2,1)S(1)}, u32[]{:S(2)}, u32[]{:S(2)}) collective-permute-start(bf16[640,256]{1,0:T(8,128)(2,1)S(1)} %get-tuple-element.20), channel_id=1, source_target_pairs={{0,4},{4,0},{8,12},{12,8},{1,5},{5,1},{9,13},{13,9},{2,6},{6,2},{1... | collective-permute-start | bytes 983048 | tf_op jit(solution)/shard_map/ppermute | solution.py:465
  1.7 12.3 %copy-start.6 = (f32[1024,128]{1,0:T(8,128)S(1)}, f32[1024,128]{1,0:T(8,128)}, u32[]{:S(2)}) copy-start(f32[1024,128]{1,0:T(8,128)} %taps_ref.1) | copy-start | bytes 1572868
  1.7 7.6 %collective-permute-start.1 = (bf16[640,128]{1,0:T(8,128)(2,1)S(1)}, bf16[640,128]{1,0:T(8,128)(2,1)S(1)}, u32[]{:S(2)}, u32[]{:S(2)}) collective-permute-start(bf16[640,128]{1,0:T(8,128)(2,1)S(1)} %get-tuple-element.23), channel_id=1, source_target_pairs={{0,8},{4,12},{8,0},{12,4},{1,9},{5,13},{9,1},{13,5},{2,10},{6,14},... | collective-permute-start | bytes 491528 | tf_op jit(solution)/shard_map/ppermute | solution.py:465
  4.3 9.7 %copy-start.2 = (bf16[128,1024]{1,0:T(8,128)(2,1)S(1)}, bf16[128,1024]{1,0:T(8,128)(2,1)}, u32[]{:S(2)}) copy-start(bf16[128,1024]{1,0:T(8,128)(2,1)} %rest_0_.3) | copy-start | bytes 786436
  4.3 9.7 %copy-start.3 = (bf16[128,1024]{1,0:T(8,128)(2,1)S(1)}, bf16[128,1024]{1,0:T(8,128)(2,1)}, u32[]{:S(2)}) copy-start(bf16[128,1024]{1,0:T(8,128)(2,1)} %rest_2_.4) | copy-start | bytes 786436
  5.4 8.5 %copy-start.5 = (bf16[512,128]{1,0:T(8,128)(2,1)S(1)}, bf16[512,128]{1,0:T(8,128)(2,1)}, u32[]{:S(2)}) copy-start(bf16[512,128]{1,0:T(8,128)(2,1)} %constant.4.clone.ahead_ref.rest_2_.rest_5_) | copy-start | bytes 393220
  5.4 6.9 %collective-permute-start.2 = (bf16[640,128]{1,0:T(8,128)(2,1)S(1)}, bf16[640,128]{1,0:T(8,128)(2,1)S(1)}, u32[]{:S(2)}, u32[]{:S(2)}) collective-permute-start(bf16[640,128]{1,0:T(8,128)(2,1)S(1)} %get-tuple-element.24), channel_id=1, source_target_pairs={{0,12},{4,8},{8,4},{12,0},{1,13},{5,9},{9,5},{13,1},{2,14},{6,10},... | collective-permute-start | bytes 491528 | tf_op jit(solution)/shard_map/ppermute | solution.py:465
  6.8 10.7 %collective-permute-start.5 = (bf16[256,256]{1,0:T(8,128)(2,1)S(1)}, bf16[256,256]{1,0:T(8,128)(2,1)S(1)}, u32[]{:S(2)}, u32[]{:S(2)}) collective-permute-start(bf16[256,256]{1,0:T(8,128)(2,1)S(1)} %get-tuple-element.26), channel_id=1, source_target_pairs={{0,8},{4,12},{8,0},{12,4},{1,9},{5,13},{9,1},{13,5},{2,10},{6,14},... | collective-permute-start | bytes 393224 | tf_op jit(solution)/shard_map/ppermute | solution.py:465
  7.3 10.2 %collective-permute-start.6 = (bf16[128,256]{1,0:T(8,128)(2,1)S(1)}, bf16[128,256]{1,0:T(8,128)(2,1)S(1)}, u32[]{:S(2)}, u32[]{:S(2)}) collective-permute-start(bf16[128,256]{1,0:T(8,128)(2,1)S(1)} %get-tuple-element.27), channel_id=1, source_target_pairs={{0,12},{4,8},{8,4},{12,0},{1,13},{5,9},{9,5},{13,1},{2,14},{6,10},... | collective-permute-start | bytes 196616 | tf_op jit(solution)/shard_map/ppermute | solution.py:465
  8.5 9.9 %collective-permute-start.7 = (bf16[128,256]{1,0:T(8,128)(2,1)S(1)}, bf16[128,256]{1,0:T(8,128)(2,1)S(1)}, u32[]{:S(2)}, u32[]{:S(2)}) collective-permute-start(bf16[128,256]{1,0:T(8,128)(2,1)S(1)} %get-tuple-element.30), channel_id=1, source_target_pairs={{0,12},{4,8},{8,4},{12,0},{1,13},{5,9},{9,5},{13,1},{2,14},{6,10},... | collective-permute-start | bytes 196616 | tf_op jit(solution)/shard_map/ppermute | solution.py:465
  9.3 6.1 %collective-permute-start.3 = (bf16[128,128]{1,0:T(8,128)(2,1)S(1)}, bf16[128,128]{1,0:T(8,128)(2,1)S(1)}, u32[]{:S(2)}, u32[]{:S(2)}) collective-permute-start(bf16[128,128]{1,0:T(8,128)(2,1)S(1)} %slice.8), channel_id=1, source_target_pairs={{0,16},{16,0},{1,17},{17,1},{2,18},{18,2},{3,19},{19,3},{4,20},{20... | collective-permute-start | bytes 98312 | tf_op jit(solution)/shard_map/ppermute | solution.py:505
  12.3 2.1 %copy-start = (bf16[128,1024]{1,0:T(8,128)(2,1)S(1)}, bf16[128,1024]{1,0:T(8,128)(2,1)}, u32[]{:S(2)}) copy-start(bf16[128,1024]{1,0:T(8,128)(2,1)} %value_ref.1) | copy-start | bytes 786436
  12.3 2.1 %copy-start.7 = (bf16[256,256]{1,0:T(8,128)(2,1)S(1)}, bf16[256,256]{1,0:T(8,128)(2,1)}, u32[]{:S(2)}) copy-start(bf16[256,256]{1,0:T(8,128)(2,1)} %constant.5.clone.rest_3_.rest_6_) | copy-start | bytes 393220
  12.3 4.0 %collective-permute-start.4 = (bf16[128,128]{1,0:T(8,128)(2,1)S(1)}, bf16[128,128]{1,0:T(8,128)(2,1)S(1)}, u32[]{:S(2)}, u32[]{:S(2)}) collective-permute-start(bf16[128,128]{1,0:T(8,128)(2,1)S(1)} %slice.9), channel_id=1, source_target_pairs={{0,16},{16,0},{1,17},{17,1},{2,18},{18,2},{3,19},{19,3},{4,20},{20... | collective-permute-start | bytes 98312 | tf_op jit(solution)/shard_map/ppermute | solution.py:505
  14.4 1.9 %copy-start.8 = (bf16[8,128,128]{2,1,0:T(8,128)(2,1)S(1)}, bf16[8,128,128]{2,1,0:T(8,128)(2,1)}, u32[]{:S(2)}) copy-start(bf16[8,128,128]{2,1,0:T(8,128)(2,1)} %rest_4_.5) | copy-start | bytes 786436
  16.3 1.2 %copy-start.4 = (bf16[128,1024]{1,0:T(8,128)(2,1)S(1)}, bf16[128,1024]{1,0:T(8,128)(2,1)}, u32[]{:S(2)}) copy-start(bf16[128,1024]{1,0:T(8,128)(2,1)} %own_ref.2) | copy-start | bytes 786436
  17.5 1.0 %copy-start.1 = (bf16[128,1024]{1,0:T(8,128)(2,1)S(1)}, bf16[128,1024]{1,0:T(8,128)(2,1)}, u32[]{:S(2)}) copy-start(bf16[128,1024]{1,0:T(8,128)(2,1)} %own_ref.3) | copy-start | bytes 786436
  18.8 1.9 %collective-permute-start.10 = (bf16[128,256]{1,0:T(8,128)(2,1)S(1)}, bf16[128,256]{1,0:T(8,128)(2,1)S(1)}, u32[]{:S(2)}, u32[]{:S(2)}) collective-permute-start(bf16[128,256]{1,0:T(8,128)(2,1)S(1)} %get-tuple-element.34), channel_id=1, source_target_pairs={{0,4},{4,0},{8,12},{12,8},{1,5},{5,1},{9,13},{13,9},{2,6},{6,2},{1... | collective-permute-start | bytes 196616 | tf_op jit(solution)/shard_map/ppermute | solution.py:465
  18.9 4.5 %collective-permute-start.8 = (bf16[128,256]{1,0:T(8,128)(2,1)S(1)}, bf16[128,256]{1,0:T(8,128)(2,1)S(1)}, u32[]{:S(2)}, u32[]{:S(2)}) collective-permute-start(bf16[128,256]{1,0:T(8,128)(2,1)S(1)} %get-tuple-element.31), channel_id=1, source_target_pairs={{0,8},{4,12},{8,0},{12,4},{1,9},{5,13},{9,1},{13,5},{2,10},{6,14},... | collective-permute-start | bytes 196616 | tf_op jit(solution)/shard_map/ppermute | solution.py:465
  20.7 4.0 %collective-permute-start.9 = (bf16[128,256]{1,0:T(8,128)(2,1)S(1)}, bf16[128,256]{1,0:T(8,128)(2,1)S(1)}, u32[]{:S(2)}, u32[]{:S(2)}) collective-permute-start(bf16[128,256]{1,0:T(8,128)(2,1)S(1)} %get-tuple-element.32), channel_id=1, source_target_pairs={{0,12},{4,8},{8,4},{12,0},{1,13},{5,9},{9,5},{13,1},{2,14},{6,10},... | collective-permute-start | bytes 196616 | tf_op jit(solution)/shard_map/ppermute | solution.py:465

commit v6 on v5

--- a/solution.py
+++ b/solution.py
@@ -329,26 +329,28 @@
         line_ref[b] = wide_mxu(ahead, mixed[b])
 
 
-def conv_kernel(line_ref, filter_spec_ref, *rest, count, groups, block, head_dim):
+def share_start(shift, columns, groups):
+    group = lax.axis_index("groups") if groups > 1 else 0
+    return pl.multiple_of(lax.rem(group + groups - shift, groups) * columns, HEAD_DIM)
+
+
+def conv_kernel(line_ref, filter_spec_ref, *rest, count, groups, shift, block, head_dim):
     far = count - 2
-    shares = [rest[n * far : (n + 1) * far] for n in range(groups)]
-    weight_ref, ahead_ref, back_ref, query_ref, filter_all, spec_all = rest[groups * far :]
+    arrived = rest[:far]
+    weight_ref, ahead_ref, back_ref, query_ref, spec_all = rest[far:]
     here = lax.axis_index("seq")
-    group = lax.axis_index("groups") if groups > 1 else 0
-    for shift, pieces in enumerate(shares):
-        for n, piece in enumerate(pieces):
-            columns = piece.shape[1]
-            start = lax.rem(group + groups - shift, groups) * columns
-            chosen = pl.ds(pl.multiple_of(start, head_dim), columns)
-            filter_all[n, :, chosen] = piece[piece.shape[0] - block :]
+    width = line_ref.shape[2]
+    columns = width // groups
+    start = share_start(shift, columns, groups)
+    chosen = pl.ds(start, columns)
     ahead = ahead_ref[...]
     back = back_ref[...]
-    heads = line_ref.shape[2] // head_dim
-    spec_all[here] = filter_spec_ref[0]
-    spec_all[here ^ 1] = filter_spec_ref[1]
-    for n in range(far):
-        spec_all[here ^ (n + 2)] = wide_mxu(ahead, filter_all[n])
-    lines = [(line_ref[b, :block], line_ref[b, block:]) for b in range(count)]
+    first_head = here * (width // head_dim) + start // head_dim
+    spec_all[here] = filter_spec_ref[0, :, chosen]
+    spec_all[here ^ 1] = filter_spec_ref[1, :, chosen]
+    for step, piece in enumerate(arrived, 2):
+        spec_all[here ^ step] = wide_mxu(ahead, piece[piece.shape[0] - block :])
+    lines = [(line_ref[b, :block, chosen], line_ref[b, block:, chosen]) for b in range(count)]
     kernels = [(spec_all[0, :block], spec_all[0, block:])] + [
         with_block_before(spec_all[b], spec_all[b - 1], block) for b in range(1, count)
     ]
@@ -363,57 +365,63 @@
         totals.append((total_re, total_im))
     for b, conv_out in enumerate(to_blocks(back, totals, block)):
         conv_out = conv_out.astype(jnp.bfloat16)
-        for h in range(heads):
-            columns = slice(h * head_dim, (h + 1) * head_dim)
-            query_ref[b, :, columns] = mxu(
-                conv_out[:, columns], weight_ref[here * heads + h]
-            ).astype(jnp.bfloat16)
-
-
-def weigh_kernel(query_ref, own_ref, near_ref, *rest, count, block, head_dim):
-    arrived = rest[: count - 2]
-    weight_ref, part_ref, key_all = rest[count - 2 :]
+        for h in range(columns // head_dim):
+            part = slice(h * head_dim, (h + 1) * head_dim)
+            query_ref[b, :, part] = mxu(conv_out[:, part], weight_ref[first_head + h]).astype(
+                jnp.bfloat16
+            )
+
+
+def weigh_kernel(own_ref, near_ref, *rest, count, groups, block, head_dim):
+    arrived, queries = rest[: count - 2], rest[count - 2 : count - 2 + groups]
+    weight_ref, part_ref, key_all = rest[count - 2 + groups :]
     here = lax.axis_index("seq")
     key_all[here] = own_columns(own_ref, here, near_ref.shape[1])
     for step, piece in enumerate((near_ref, *arrived), 1):
         first = max(piece.shape[0] - 2 * block, 0)
         key_all[here ^ step] = piece[first : first + block]
-    width = query_ref.shape[2]
     turned = (((1,), (1,)), ((), ()))
-    scale = 1.0 / math.sqrt(head_dim)
+    scale = math.log2(math.e) / math.sqrt(head_dim)
     row = lax.broadcasted_iota(jnp.int32, (block, block), 0)
     column = lax.broadcasted_iota(jnp.int32, (block, block), 1)
     allowed = column <= row
-    places = [(h, b) for h in range(width // head_dim) for b in range(count)]
-    scores = []
+    share = queries[0].shape[2]
+    heads = share // head_dim
+    places = [(h, b) for h in range(groups * heads) for b in range(count)]
+    scores = {place: [] for place in places}
+    for h in range(groups * heads):
+        shift, part = divmod(h, heads)
+        query = jnp.concatenate(
+            [queries[shift][b, :, part * head_dim : (part + 1) * head_dim] for b in range(count)],
+            axis=0,
+        )
+        columns = pl.ds(share_start(shift, share, groups) + part * head_dim, head_dim)
+        for j in range(count):
+            later = lax.dot_general(
+                query[j * block :],
+                key_all[j, :, columns],
+                turned,
+                preferred_element_type=jnp.float32,
+            )
+            for b in range(j, count):
+                score = later[(b - j) * block : (b - j + 1) * block]
+                scores[h, b].append(jnp.where(allowed, score, -1e30) if j == b else score)
+    peaks = {
+        place: jnp.max(functools.reduce(jnp.maximum, parts), axis=1, keepdims=True)
+        for place, parts in scores.items()
+    }
+    sums = {}
     for h, b in places:
-        columns = slice(h * head_dim, (h + 1) * head_dim)
-        query = query_ref[b, :, columns]
-        parts = []
-        for j in range(b + 1):
-            part = lax.dot_general(
-                query, key_all[j, :, columns], turned, preferred_element_type=jnp.float32
-            )
-            part = part * scale
-            parts.append(jnp.where(allowed, part, -1e30) if j == b else part)
-        scores.append(parts)
-    peaks = [
-        jnp.max(functools.reduce(jnp.maximum, parts), axis=1, keepdims=True) for parts in scores
-    ]
-    sums = []
-    for (h, b), parts, peak in zip(places, scores, peaks):
-        weights = [jnp.exp(part - peak) for part in parts]
+        weights = [jnp.exp2((score - peaks[h, b]) * scale) for score in scores[h, b]]
         weights[b] = jnp.where(allowed, weights[b], 0.0)
-        sums.append(jnp.sum(functools.reduce(jnp.add, weights), axis=1, keepdims=True))
+        sums[h, b] = jnp.sum(functools.reduce(jnp.add, weights), axis=1, keepdims=True)
         for j in range(b + 1):
             weight_ref[h, b, :, j * block : (j + 1) * block] = weights[j].astype(jnp.bfloat16)
-    for (h, b), weight_sum in zip(places, sums):
-        part_ref[h, b] = jnp.broadcast_to(1.0 / weight_sum, (block, head_dim))
-
-
-def sum_kernel(
-    weight_ref, part_ref, own_ref, near_ref, *rest, count, block, head_dim
-):
+    for h, b in places:
+        part_ref[h, b] = jnp.broadcast_to(1.0 / sums[h, b], (block, head_dim))
+
+
+def sum_kernel(weight_ref, part_ref, own_ref, near_ref, *rest, count, groups, block, head_dim):
     arrived = rest[: count - 2]
     outs = rest[count - 2 : 2 * count - 2]
     value_all, out_all = rest[2 * count - 2 :]
@@ -425,8 +433,10 @@
     value_all[rows_of(here)] = own_columns(own_ref, here, near_ref.shape[1])
     for step, piece in enumerate((near_ref, *arrived), 1):
         value_all[rows_of(here ^ step)] = piece[-block:]
-    for h in range(value_all.shape[1] // head_dim):
-        columns = slice(h * head_dim, (h + 1) * head_dim)
+    share = value_all.shape[1] // groups
+    for h in range(weight_ref.shape[0]):
+        shift, part = divmod(h, share // head_dim)
+        columns = pl.ds(share_start(shift, share, groups) + part * head_dim, head_dim)
         for b in range(count):
             seen = (b + 1) * block
             total = mxu(weight_ref[h, b, :, :seen], value_all[:seen, columns])
@@ -500,14 +510,6 @@
     )
     arrived = [swap(piece, step) for step, piece in zip(far, [first, *pieces])]
     later = pieces[len(far) - 1 :]
-    filters = [piece[-block:] for piece in arrived]
-    shares = arrived + [
-        lax.ppermute(piece, "groups", [(i, (i + shift) % groups) for i in range(groups)])
-        for shift in range(1, groups)
-        for piece in filters
-    ]
-    later = [swap(piece, step) for step, piece in zip([*far, far[-1]], later)]
-    arrived_keys, arrived_values = later[:-1], [*later[:-2], later[-1]]
     tables = jnp.asarray(ahead), jnp.asarray(back)
     spectra = lambda n: (n, 2 * block, width)
     gate_spec, filter_spec, taps_spec = pl.pallas_call(
@@ -521,6 +523,17 @@
         out_specs=[WHOLE] * 3,
         compiler_params=params,
     )(gate_input, long_filter, near, short_filter, tables[0])
+    filters = [piece[-block:] for piece in arrived]
+    filters[0], taps_spec = lax.optimization_barrier((filters[0], taps_spec))
+    shares = [arrived] + [
+        [
+            lax.ppermute(piece, "groups", [(i, (i + shift) % groups) for i in range(groups)])
+            for piece in filters
+        ]
+        for shift in range(1, groups)
+    ]
+    later = [swap(piece, step) for step, piece in zip([*far, far[-1]], later)]
+    arrived_keys, arrived_values = later[:-1], [*later[:-2], later[-1]]
     lines = pl.pallas_call(
         functools.partial(smooth_kernel, count=count, block=block),
         out_shape=jax.ShapeDtypeStruct(spectra(count), jnp.float32),
@@ -529,29 +542,41 @@
         scratch_shapes=[pltpu.VMEM(spectra(count), jnp.float32), scratch(count)],
         compiler_params=params,
     )(gate_spec, taps_spec, value_input, near, *arrived, *tables)
-    queries = pl.pallas_call(
+    queries = [
+        pl.pallas_call(
+            functools.partial(
+                conv_kernel,
+                count=count,
+                groups=groups,
+                shift=shift,
+                block=block,
+                head_dim=HEAD_DIM,
+            ),
+            out_shape=jax.ShapeDtypeStruct((count, block, share), jnp.bfloat16),
+            in_specs=[WHOLE] * (len(far) + 5),
+            out_specs=WHOLE,
+            scratch_shapes=[pltpu.VMEM((count, 2 * block, share), jnp.float32)],
+            compiler_params=params,
+        )(lines, filter_spec, *pieces, query_weight, *tables)
+        for shift, pieces in enumerate(shares)
+    ]
+    weights, parts = pl.pallas_call(
         functools.partial(
-            conv_kernel, count=count, groups=groups, block=block, head_dim=HEAD_DIM
+            weigh_kernel, count=count, groups=groups, block=block, head_dim=HEAD_DIM
         ),
-        out_shape=jax.ShapeDtypeStruct((count, block, width), jnp.bfloat16),
-        in_specs=[WHOLE] * (groups * len(far) + 5),
-        out_specs=WHOLE,
-        scratch_shapes=[scratch(len(far)), pltpu.VMEM(spectra(count), jnp.float32)],
-        compiler_params=params,
-    )(lines, filter_spec, *shares, query_weight, *tables)
-    weights, parts = pl.pallas_call(
-        functools.partial(weigh_kernel, count=count, block=block, head_dim=HEAD_DIM),
         out_shape=[
             jax.ShapeDtypeStruct((heads, count, block, count * block), jnp.bfloat16),
             jax.ShapeDtypeStruct((heads, count, block, HEAD_DIM), jnp.float32),
         ],
-        in_specs=[WHOLE] * (count + 1),
+        in_specs=[WHOLE] * (count + groups),
         out_specs=[WHOLE] * 2,
         scratch_shapes=[scratch(count)],
         compiler_params=params,
-    )(queries, key_matrix, near, *arrived_keys)
+    )(key_matrix, near, *arrived_keys, *queries)
     pieces = pl.pallas_call(
-        functools.partial(sum_kernel, count=count, block=block, head_dim=HEAD_DIM),
+        functools.partial(
+            sum_kernel, count=count, groups=groups, block=block, head_dim=HEAD_DIM
+        ),
         out_shape=[jax.ShapeDtypeStruct((block, width), jnp.bfloat16)] * count,
         in_specs=[WHOLE] * (count + 2),
         out_specs=[WHOLE] * count,

time: 25.6 us -> 25.3 us (0.988)
  waiting for transfers between devices: 5.36 us -> 4.66 us
  Pallas kernels: 7.51 us -> 7.82 us
    pallas_call x1 -> x2, Pallas kernels: 1.19 us -> 1.68 us  [head_shards(): pl.pallas_call(functools.partial(conv_kernel, count=count, groups=groups,...]
    ppermute x2, waiting for transfers between devices: 0.83 us -> 0.44 us  [head_shards(): lax.ppermute(piece, 'groups', [(i, (i + shift) % groups) for i in range(g...]
    ppermute x9, waiting for transfers between devices: 4.53 us -> 4.22 us  [swap(): return lax.ppermute(value, 'seq', [(i, i ^ step) for i in range(count)])]
  transfers between devices with their start and end apart: 11 -> 11, of which waited for: 5 -> 5; matrix products, arithmetic and copies ran while one was open for 0% -> 0% of each run, Pallas kernels for 21% -> 22%
where the time goes in v6:
time: 25.3 us; the launch traced here: 25.1 us
  starting transfers between devices  12.3 us (49%)
  Pallas kernels  7.82 us (31%)
  waiting for transfers between devices  4.66 us (18%)
    ppermute x9, starting transfers between devices, swap(): return lax.ppermute(value, 'seq', [(i, i ^ step) for i in range(count)])  8.66 us
    ppermute x9, waiting for transfers between devices, swap(): return lax.ppermute(value, 'seq', [(i, i ^ step) for i in range(count)])  4.22 us
    ppermute x2, starting transfers between devices, head_shards(): lax.ppermute(piece, 'groups', [(i, (i + shift) % groups) for i in range(g...  3.61 us
    pallas_call x2, Pallas kernels, packed(): pl.pallas_call(functools.partial(pack_kernel, parts=parts, width=width),...  2.29 us
    pallas_call x2, Pallas kernels, head_shards(): pl.pallas_call(functools.partial(conv_kernel, count=count, groups=groups,...  1.68 us
    pallas_call x2, Pallas kernels, joined(): pl.pallas_call(functools.partial(join_kernel, steps=steps, width=width),...  1.33 us
    pallas_call x1, Pallas kernels, head_shards(): pl.pallas_call(functools.partial(smooth_kernel, count=count, block=block)...  1.04 us
    pallas_call x1, Pallas kernels, head_shards(): pl.pallas_call(functools.partial(weigh_kernel, count=count, groups=groups...  0.68 us
  transfers between devices with their start and end apart: 11, of which 5 were waited for; matrix products, arithmetic and copies ran while one was open for 0% of the time, Pallas kernels for 22%

profile of v6, /device:TPU:0, one launch (start us, length us, event | category | flops | bytes accessed | tf_op | source)
XLA Modules:
  0.0 25.1 jit_solution(14876532723258186421)
XLA Ops:
  0.0 1.2 %shard_map.91 = (bf16[640,128]{1,0:T(8,128)(2,1)S(1)}, bf16[640,256]{1,0:T(8,128)(2,1)S(1)}) custom-call(bf16[128,1024]{1,0:T(8,128)(2,1)} %gate_ref.1, bf16[128,1024]{1,0:T(8,128)(2,1)} %value_ref.1, bf16[128,1024]{1,0:T(8,128)(2,1)} %filter_ref.1, bf16[128,1024]{1,0:T(8,128)(2,1)} %own_ref.2, bf16[128,1024]{1,0:T(8,128)(2,1)} %own_ref.3), custom_call_target="tpu_custom_call" | custom-call | tf_op jit(solution)/shard_map/pallas_call | solution.py:478
  1.2 0.5 %collective-permute-start = (bf16[640,256]{1,0:T(8,128)(2,1)S(1)}, bf16[640,256]{1,0:T(8,128)(2,1)S(1)}, u32[]{:S(2)}, u32[]{:S(2)}) collective-permute-start(bf16[640,256]{1,0:T(8,128)(2,1)S(1)} %get-tuple-element.22), channel_id=1, source_target_pairs={{0,4},{4,0},{8,12},{12,8},{1,5},{5,1},{9,13},{13,9},{2,6},{6,2},{1... | collective-permute-start | bytes 983048 | tf_op jit(solution)/shard_map/ppermute | solution.py:475
  1.7 2.6 %collective-permute-start.3 = (bf16[640,128]{1,0:T(8,128)(2,1)S(1)}, bf16[640,128]{1,0:T(8,128)(2,1)S(1)}, u32[]{:S(2)}, u32[]{:S(2)}) collective-permute-start(bf16[640,128]{1,0:T(8,128)(2,1)S(1)} %get-tuple-element.26), channel_id=1, source_target_pairs={{0,8},{4,12},{8,0},{12,4},{1,9},{5,13},{9,1},{13,5},{2,10},{6,14},... | collective-permute-start | bytes 491528 | tf_op jit(solution)/shard_map/ppermute | solution.py:475
  4.3 1.1 %shard_map.92 = (bf16[640,128]{1,0:T(8,128)(2,1)S(1)}, bf16[256,256]{1,0:T(8,128)(2,1)S(1)}, bf16[128,256]{1,0:T(8,128)(2,1)S(1)}, bf16[128,256]{1,0:T(8,128)(2,1)S(1)}) custom-call(bf16[128,1024]{1,0:T(8,128)(2,1)} %gate_ref.1, bf16[128,1024]{1,0:T(8,128)(2,1)} %value_ref.1, bf16[128,1024]{1,0:T(8,128)(2,1)} %filter_ref.1, bf16[128,1024]{1,0:T(8,128)(2,1)} %own_ref.2, ...), custom_call_target="tpu_custom_call" | custom-call | tf_op jit(solution)/shard_map/pallas_call | solution.py:478
  5.4 1.3 %collective-permute-start.4 = (bf16[640,128]{1,0:T(8,128)(2,1)S(1)}, bf16[640,128]{1,0:T(8,128)(2,1)S(1)}, u32[]{:S(2)}, u32[]{:S(2)}) collective-permute-start(bf16[640,128]{1,0:T(8,128)(2,1)S(1)} %get-tuple-element.29), channel_id=1, source_target_pairs={{0,12},{4,8},{8,4},{12,0},{1,13},{5,9},{9,5},{13,1},{2,14},{6,10},... | collective-permute-start | bytes 491528 | tf_op jit(solution)/shard_map/ppermute | solution.py:475
  6.8 0.5 %collective-permute-start.1 = (bf16[256,256]{1,0:T(8,128)(2,1)S(1)}, bf16[256,256]{1,0:T(8,128)(2,1)S(1)}, u32[]{:S(2)}, u32[]{:S(2)}) collective-permute-start(bf16[256,256]{1,0:T(8,128)(2,1)S(1)} %get-tuple-element.23), channel_id=1, source_target_pairs={{0,8},{4,12},{8,0},{12,4},{1,9},{5,13},{9,1},{13,5},{2,10},{6,14},... | collective-permute-start | bytes 393224 | tf_op jit(solution)/shard_map/ppermute | solution.py:475
  7.3 1.2 %collective-permute-start.2 = (bf16[128,256]{1,0:T(8,128)(2,1)S(1)}, bf16[128,256]{1,0:T(8,128)(2,1)S(1)}, u32[]{:S(2)}, u32[]{:S(2)}) collective-permute-start(bf16[128,256]{1,0:T(8,128)(2,1)S(1)} %get-tuple-element.24), channel_id=1, source_target_pairs={{0,12},{4,8},{8,4},{12,0},{1,13},{5,9},{9,5},{13,1},{2,14},{6,10},... | collective-permute-start | bytes 196616 | tf_op jit(solution)/shard_map/ppermute | solution.py:475
  8.5 0.6 %collective-permute-start.7 = (bf16[128,256]{1,0:T(8,128)(2,1)S(1)}, bf16[128,256]{1,0:T(8,128)(2,1)S(1)}, u32[]{:S(2)}, u32[]{:S(2)}) collective-permute-start(bf16[128,256]{1,0:T(8,128)(2,1)S(1)} %get-tuple-element.34), channel_id=1, source_target_pairs={{0,12},{4,8},{8,4},{12,0},{1,13},{5,9},{9,5},{13,1},{2,14},{6,10},... | collective-permute-start | bytes 196616 | tf_op jit(solution)/shard_map/ppermute | solution.py:475
  9.0 0.3 %collective-permute-done.3.rest_0_ = bf16[640,128]{1,0:T(8,128)(2,1)S(1)} collective-permute-done((bf16[640,128]{1,0:T(8,128)(2,1)S(1)}, bf16[640,128]{1,0:T(8,128)(2,1)S(1)}, u32[]{:S(2)}, u32[]{:S(2)}) %collective-permute-start.3) | collective-permute-done | bytes 163872 | tf_op jit(solution)/shard_map/ppermute | solution.py:475
  9.4 0.4 %shard_map.93 = (f32[2,256,256]{2,1,0:T(8,128)S(1)}, f32[2,256,256]{2,1,0:T(8,128)S(1)}, f32[256,256]{1,0:T(8,128)S(1)}) custom-call(bf16[128,1024]{1,0:T(8,128)(2,1)S(1)} %copy-done.2, bf16[128,1024]{1,0:T(8,128)(2,1)S(1)} %copy-done.3, bf16[640,256]{1,0:T(8,128)(2,1)S(1)} %collective-permute-done.rest_5_.near_ref, f32[1024,128]{1,0:T(8,128)S(1)} %copy-done.8, ...), custom_call_target="tpu_custom_call" | custom-call | tf_op jit(solution)/shard_map/pallas_call | solution.py:515
  9.8 2.0 %collective-permute-start.5 = (bf16[128,128]{1,0:T(8,128)(2,1)S(1)}, bf16[128,128]{1,0:T(8,128)(2,1)S(1)}, u32[]{:S(2)}, u32[]{:S(2)}) collective-permute-start(bf16[128,128]{1,0:T(8,128)(2,1)S(1)} %slice.8), channel_id=1, source_target_pairs={{0,16},{16,0},{1,17},{17,1},{2,18},{18,2},{3,19},{19,3},{4,20},{20... | collective-permute-start | bytes 98312 | tf_op jit(solution)/shard_map/ppermute | solution.py:530
  11.9 0.5 %collective-permute-done.4.rest_1_ = bf16[640,128]{1,0:T(8,128)(2,1)S(1)} collective-permute-done((bf16[640,128]{1,0:T(8,128)(2,1)S(1)}, bf16[640,128]{1,0:T(8,128)(2,1)S(1)}, u32[]{:S(2)}, u32[]{:S(2)}) %collective-permute-start.4) | collective-permute-done | bytes 163872 | tf_op jit(solution)/shard_map/ppermute | solution.py:475
  12.3 1.6 %collective-permute-start.6 = (bf16[128,128]{1,0:T(8,128)(2,1)S(1)}, bf16[128,128]{1,0:T(8,128)(2,1)S(1)}, u32[]{:S(2)}, u32[]{:S(2)}) collective-permute-start(bf16[128,128]{1,0:T(8,128)(2,1)S(1)} %slice.9), channel_id=1, source_target_pairs={{0,16},{16,0},{1,17},{17,1},{2,18},{18,2},{3,19},{19,3},{4,20},{20... | collective-permute-start | bytes 98312 | tf_op jit(solution)/shard_map/ppermute | solution.py:530
  13.9 1.0 %shard_map.94.line_ref = f32[4,256,256]{2,1,0:T(8,128)S(1)} custom-call(f32[2,256,256]{2,1,0:T(8,128)S(1)} %get-tuple-element.25.gate_spec_ref, f32[256,256]{1,0:T(8,128)S(1)} %get-tuple-element.28.taps_spec_ref, bf16[128,1024]{1,0:T(8,128)(2,1)S(1)} %copy-done, bf16[640,256]{1,0:T(8,128)(2,1)S(1)} %collective-permute-done.rest_5_.near_ref, ...), custom_call_target="tpu_custom_call" | custom-call | tf_op jit(solution)/shard_map/pallas_call | solution.py:537
  14.9 0.8 %shard_map.95.rest_2_ = bf16[4,128,128]{2,1,0:T(8,128)(2,1)S(1)} custom-call(f32[4,256,256]{2,1,0:T(8,128)S(1)} %shard_map.94.line_ref, f32[2,256,256]{2,1,0:T(8,128)S(1)} %get-tuple-element.30.filter_spec_ref, bf16[640,128]{1,0:T(8,128)(2,1)S(1)} %collective-permute-done.3.rest_0_, bf16[640,128]{1,0:T(8,128)(2,1)S(1)} %collective-permute-done.4.rest_1_, ...), custom_call_target="tpu_custom_call" | custom-call | tf_op jit(solution)/shard_map/pallas_call | solution.py:546
  15.8 0.4 %collective-permute-done.6.rest_1_ = bf16[128,128]{1,0:T(8,128)(2,1)S(1)} collective-permute-done((bf16[128,128]{1,0:T(8,128)(2,1)S(1)}, bf16[128,128]{1,0:T(8,128)(2,1)S(1)}, u32[]{:S(2)}, u32[]{:S(2)}) %collective-permute-start.6) | collective-permute-done | bytes 32800 | tf_op jit(solution)/shard_map/ppermute | solution.py:530
  16.2 0.9 %shard_map.96.rest_3_ = bf16[4,128,128]{2,1,0:T(8,128)(2,1)S(1)} custom-call(f32[4,256,256]{2,1,0:T(8,128)S(1)} %shard_map.94.line_ref, f32[2,256,256]{2,1,0:T(8,128)S(1)} %get-tuple-element.30.filter_spec_ref, bf16[128,128]{1,0:T(8,128)(2,1)S(1)} %collective-permute-done.5.rest_0_, bf16[128,128]{1,0:T(8,128)(2,1)S(1)} %collective-permute-done.6.rest_1_, ...), custom_call_target="tpu_custom_call" | custom-call | tf_op jit(solution)/shard_map/pallas_call | solution.py:546
  17.1 0.7 %shard_map.97 = (bf16[2,4,128,512]{3,2,1,0:T(8,128)(2,1)S(1)}, f32[2,4,128,128]{3,2,1,0:T(8,128)S(1)}) custom-call(bf16[128,1024]{1,0:T(8,128)(2,1)S(1)} %copy-done.4, bf16[640,256]{1,0:T(8,128)(2,1)S(1)} %collective-permute-done.rest_5_.near_ref, bf16[256,256]{1,0:T(8,128)(2,1)S(1)} %collective-permute-done.1.rest_0_, ...), custom_call_target="tpu_custom_call" | custom-call | tf_op jit(solution)/shard_map/pallas_call | solution.py:563
  18.0 0.4 %shard_map.98 = (bf16[128,256]{1,0:T(8,128)(2,1)S(1)}, bf16[128,256]{1,0:T(8,128)(2,1)S(1)}, bf16[128,256]{1,0:T(8,128)(2,1)S(1)}, bf16[128,256]{1,0:T(8,128)(2,1)S(1)}) custom-call(bf16[2,4,128,512]{3,2,1,0:T(8,128)(2,1)S(1)} %get-tuple-element.32.weight_ref, f32[2,4,128,128]{3,2,1,0:T(8,128)S(1)} %get-tuple-element.33.part_ref, ...), custom_call_target="tpu_custom_call" | custom-call | tf_op jit(solution)/shard_map/pallas_call | solution.py:576
  18.6 1.7 %collective-permute-start.8 = (bf16[128,256]{1,0:T(8,128)(2,1)S(1)}, bf16[128,256]{1,0:T(8,128)(2,1)S(1)}, u32[]{:S(2)}, u32[]{:S(2)}) collective-permute-start(bf16[128,256]{1,0:T(8,128)(2,1)S(1)} %get-tuple-element.35), channel_id=1, source_target_pairs={{0,8},{4,12},{8,0},{12,4},{1,9},{5,13},{9,1},{13,5},{2,10},{6,14},... | collective-permute-start | bytes 196616 | tf_op jit(solution)/shard_map/ppermute | solution.py:475
  20.4 0.7 %shard_map.99.rest_2_ = bf16[128,1024]{1,0:T(8,128)(2,1)} custom-call(bf16[128,256]{1,0:T(8,128)(2,1)S(1)} %get-tuple-element.37.rest_0_, bf16[128,256]{1,0:T(8,128)(2,1)S(1)} %collective-permute-done.10.rest_1_), custom_call_target="tpu_custom_call" | custom-call | tf_op jit(solution)/shard_map/pallas_call | solution.py:593
  21.1 2.0 %collective-permute-done.8.rest_0_ = bf16[128,256]{1,0:T(8,128)(2,1)S(1)} collective-permute-done((bf16[128,256]{1,0:T(8,128)(2,1)S(1)}, bf16[128,256]{1,0:T(8,128)(2,1)S(1)}, u32[]{:S(2)}, u32[]{:S(2)}) %collective-permute-start.8) | collective-permute-done | bytes 65568 | tf_op jit(solution)/shard_map/ppermute | solution.py:475
  23.0 1.4 %collective-permute-done.9.rest_1_ = bf16[128,256]{1,0:T(8,128)(2,1)S(1)} collective-permute-done((bf16[128,256]{1,0:T(8,128)(2,1)S(1)}, bf16[128,256]{1,0:T(8,128)(2,1)S(1)}, u32[]{:S(2)}, u32[]{:S(2)}) %collective-permute-start.9) | collective-permute-done | bytes 65568 | tf_op jit(solution)/shard_map/ppermute | solution.py:475
  24.5 0.7 %shard_map.100 = bf16[128,1024]{1,0:T(8,128)(2,1)} custom-call(bf16[128,256]{1,0:T(8,128)(2,1)S(1)} %collective-permute-done.8.rest_0_, bf16[128,256]{1,0:T(8,128)(2,1)S(1)} %collective-permute-done.9.rest_1_, bf16[128,1024]{1,0:T(8,128)(2,1)} %shard_map.99.rest_2_), custom_call_target="tpu_custom_call", output_to_operand_aliasing={{}: (2, {})} | custom-call | tf_op jit(solution)/shard_map/pallas_call | solution.py:593
  (28 shorter events, 0.5 us)
Async XLA Ops:
  1.2 3.1 %collective-permute-start = (bf16[640,256]{1,0:T(8,128)(2,1)S(1)}, bf16[640,256]{1,0:T(8,128)(2,1)S(1)}, u32[]{:S(2)}, u32[]{:S(2)}) collective-permute-start(bf16[640,256]{1,0:T(8,128)(2,1)S(1)} %get-tuple-element.22), channel_id=1, source_target_pairs={{0,4},{4,0},{8,12},{12,8},{1,5},{5,1},{9,13},{13,9},{2,6},{6,2},{1... | collective-permute-start | bytes 983048 | tf_op jit(solution)/shard_map/ppermute | solution.py:475
  1.7 7.7 %copy-start.2 = (bf16[128,1024]{1,0:T(8,128)(2,1)S(1)}, bf16[128,1024]{1,0:T(8,128)(2,1)}, u32[]{:S(2)}) copy-start(bf16[128,1024]{1,0:T(8,128)(2,1)} %gate_ref.1) | copy-start | bytes 786436
  1.7 7.7 %copy-start.3 = (bf16[128,1024]{1,0:T(8,128)(2,1)S(1)}, bf16[128,1024]{1,0:T(8,128)(2,1)}, u32[]{:S(2)}) copy-start(bf16[128,1024]{1,0:T(8,128)(2,1)} %filter_ref.1) | copy-start | bytes 786436
  1.7 7.7 %copy-start.8 = (f32[1024,128]{1,0:T(8,128)S(1)}, f32[1024,128]{1,0:T(8,128)}, u32[]{:S(2)}) copy-start(f32[1024,128]{1,0:T(8,128)} %taps_ref.1) | copy-start | bytes 1572868
  1.7 7.7 %collective-permute-start.3 = (bf16[640,128]{1,0:T(8,128)(2,1)S(1)}, bf16[640,128]{1,0:T(8,128)(2,1)S(1)}, u32[]{:S(2)}, u32[]{:S(2)}) collective-permute-start(bf16[640,128]{1,0:T(8,128)(2,1)S(1)} %get-tuple-element.26), channel_id=1, source_target_pairs={{0,8},{4,12},{8,0},{12,4},{1,9},{5,13},{9,1},{13,5},{2,10},{6,14},... | collective-permute-start | bytes 491528 | tf_op jit(solution)/shard_map/ppermute | solution.py:475
  4.3 5.1 %copy-start.5 = (bf16[512,128]{1,0:T(8,128)(2,1)S(1)}, bf16[512,128]{1,0:T(8,128)(2,1)}, u32[]{:S(2)}) copy-start(bf16[512,128]{1,0:T(8,128)(2,1)} %constant.4.clone.ahead_ref.rest_2_.rest_3_) | copy-start | bytes 393220
  5.4 6.9 %collective-permute-start.4 = (bf16[640,128]{1,0:T(8,128)(2,1)S(1)}, bf16[640,128]{1,0:T(8,128)(2,1)S(1)}, u32[]{:S(2)}, u32[]{:S(2)}) collective-permute-start(bf16[640,128]{1,0:T(8,128)(2,1)S(1)} %get-tuple-element.29), channel_id=1, source_target_pairs={{0,12},{4,8},{8,4},{12,0},{1,13},{5,9},{9,5},{13,1},{2,14},{6,10},... | collective-permute-start | bytes 491528 | tf_op jit(solution)/shard_map/ppermute | solution.py:475
  6.8 10.4 %collective-permute-start.1 = (bf16[256,256]{1,0:T(8,128)(2,1)S(1)}, bf16[256,256]{1,0:T(8,128)(2,1)S(1)}, u32[]{:S(2)}, u32[]{:S(2)}) collective-permute-start(bf16[256,256]{1,0:T(8,128)(2,1)S(1)} %get-tuple-element.23), channel_id=1, source_target_pairs={{0,8},{4,12},{8,0},{12,4},{1,9},{5,13},{9,1},{13,5},{2,10},{6,14},... | collective-permute-start | bytes 393224 | tf_op jit(solution)/shard_map/ppermute | solution.py:475
  7.3 9.8 %collective-permute-start.2 = (bf16[128,256]{1,0:T(8,128)(2,1)S(1)}, bf16[128,256]{1,0:T(8,128)(2,1)S(1)}, u32[]{:S(2)}, u32[]{:S(2)}) collective-permute-start(bf16[128,256]{1,0:T(8,128)(2,1)S(1)} %get-tuple-element.24), channel_id=1, source_target_pairs={{0,12},{4,8},{8,4},{12,0},{1,13},{5,9},{9,5},{13,1},{2,14},{6,10},... | collective-permute-start | bytes 196616 | tf_op jit(solution)/shard_map/ppermute | solution.py:475
  8.5 9.4 %collective-permute-start.7 = (bf16[128,256]{1,0:T(8,128)(2,1)S(1)}, bf16[128,256]{1,0:T(8,128)(2,1)S(1)}, u32[]{:S(2)}, u32[]{:S(2)}) collective-permute-start(bf16[128,256]{1,0:T(8,128)(2,1)S(1)} %get-tuple-element.34), channel_id=1, source_target_pairs={{0,12},{4,8},{8,4},{12,0},{1,13},{5,9},{9,5},{13,1},{2,14},{6,10},... | collective-permute-start | bytes 196616 | tf_op jit(solution)/shard_map/ppermute | solution.py:475
  9.4 4.5 %copy-start = (bf16[128,1024]{1,0:T(8,128)(2,1)S(1)}, bf16[128,1024]{1,0:T(8,128)(2,1)}, u32[]{:S(2)}) copy-start(bf16[128,1024]{1,0:T(8,128)(2,1)} %value_ref.1) | copy-start | bytes 786436
  9.4 4.5 %copy-start.6 = (bf16[256,256]{1,0:T(8,128)(2,1)S(1)}, bf16[256,256]{1,0:T(8,128)(2,1)}, u32[]{:S(2)}) copy-start(bf16[256,256]{1,0:T(8,128)(2,1)} %constant.5.clone.rest_3_.rest_4_) | copy-start | bytes 393220
  9.8 6.0 %collective-permute-start.5 = (bf16[128,128]{1,0:T(8,128)(2,1)S(1)}, bf16[128,128]{1,0:T(8,128)(2,1)S(1)}, u32[]{:S(2)}, u32[]{:S(2)}) collective-permute-start(bf16[128,128]{1,0:T(8,128)(2,1)S(1)} %slice.8), channel_id=1, source_target_pairs={{0,16},{16,0},{1,17},{17,1},{2,18},{18,2},{3,19},{19,3},{4,20},{20... | collective-permute-start | bytes 98312 | tf_op jit(solution)/shard_map/ppermute | solution.py:530
  12.3 3.9 %collective-permute-start.6 = (bf16[128,128]{1,0:T(8,128)(2,1)S(1)}, bf16[128,128]{1,0:T(8,128)(2,1)S(1)}, u32[]{:S(2)}, u32[]{:S(2)}) collective-permute-start(bf16[128,128]{1,0:T(8,128)(2,1)S(1)} %slice.9), channel_id=1, source_target_pairs={{0,16},{16,0},{1,17},{17,1},{2,18},{18,2},{3,19},{19,3},{4,20},{20... | collective-permute-start | bytes 98312 | tf_op jit(solution)/shard_map/ppermute | solution.py:530
  13.9 1.0 %copy-start.7 = (bf16[8,128,128]{2,1,0:T(8,128)(2,1)S(1)}, bf16[8,128,128]{2,1,0:T(8,128)(2,1)}, u32[]{:S(2)}) copy-start(bf16[8,128,128]{2,1,0:T(8,128)(2,1)} %rest_2_.8) | copy-start | bytes 786436
  15.8 1.4 %copy-start.4 = (bf16[128,1024]{1,0:T(8,128)(2,1)S(1)}, bf16[128,1024]{1,0:T(8,128)(2,1)}, u32[]{:S(2)}) copy-start(bf16[128,1024]{1,0:T(8,128)(2,1)} %own_ref.2) | copy-start | bytes 786436
  17.1 1.0 %copy-start.1 = (bf16[128,1024]{1,0:T(8,128)(2,1)S(1)}, bf16[128,1024]{1,0:T(8,128)(2,1)}, u32[]{:S(2)}) copy-start(bf16[128,1024]{1,0:T(8,128)(2,1)} %own_ref.3) | copy-start | bytes 786436
  18.4 1.9 %collective-permute-start.10 = (bf16[128,256]{1,0:T(8,128)(2,1)S(1)}, bf16[128,256]{1,0:T(8,128)(2,1)S(1)}, u32[]{:S(2)}, u32[]{:S(2)}) collective-permute-start(bf16[128,256]{1,0:T(8,128)(2,1)S(1)} %get-tuple-element.38), channel_id=1, source_target_pairs={{0,4},{4,0},{8,12},{12,8},{1,5},{5,1},{9,13},{13,9},{2,6},{6,2},{1... | collective-permute-start | bytes 196616 | tf_op jit(solution)/shard_map/ppermute | solution.py:475
  18.6 4.4 %collective-permute-start.8 = (bf16[128,256]{1,0:T(8,128)(2,1)S(1)}, bf16[128,256]{1,0:T(8,128)(2,1)S(1)}, u32[]{:S(2)}, u32[]{:S(2)}) collective-permute-start(bf16[128,256]{1,0:T(8,128)(2,1)S(1)} %get-tuple-element.35), channel_id=1, source_target_pairs={{0,8},{4,12},{8,0},{12,4},{1,9},{5,13},{9,1},{13,5},{2,10},{6,14},... | collective-permute-start | bytes 196616 | tf_op jit(solution)/shard_map/ppermute | solution.py:475
  20.3 4.1 %collective-permute-start.9 = (bf16[128,256]{1,0:T(8,128)(2,1)S(1)}, bf16[128,256]{1,0:T(8,128)(2,1)S(1)}, u32[]{:S(2)}, u32[]{:S(2)}) collective-permute-start(bf16[128,256]{1,0:T(8,128)(2,1)S(1)} %get-tuple-element.36), channel_id=1, source_target_pairs={{0,12},{4,8},{8,4},{12,0},{1,13},{5,9},{9,5},{13,1},{2,14},{6,10},... | collective-permute-start | bytes 196616 | tf_op jit(solution)/shard_map/ppermute | solution.py:475

commit v7 on v6

--- a/solution.py
+++ b/solution.py
@@ -434,13 +434,16 @@
     for step, piece in enumerate((near_ref, *arrived), 1):
         value_all[rows_of(here ^ step)] = piece[-block:]
     share = value_all.shape[1] // groups
+    totals = []
     for h in range(weight_ref.shape[0]):
         shift, part = divmod(h, share // head_dim)
         columns = pl.ds(share_start(shift, share, groups) + part * head_dim, head_dim)
         for b in range(count):
             seen = (b + 1) * block
             total = mxu(weight_ref[h, b, :, :seen], value_all[:seen, columns])
-            out_all[b, :, columns] = (total * part_ref[h, b]).astype(jnp.bfloat16)
+            totals.append((h, b, columns, total))
+    for h, b, columns, total in totals:
+        out_all[b, :, columns] = (total * part_ref[h, b]).astype(jnp.bfloat16)
     for step, out in enumerate(outs):
         out[...] = out_all[here ^ step]
 
@@ -600,7 +603,10 @@
             compiler_params=params,
         )(*[pieces[step] for step in steps], *before)
 
-    return joined(tuple(far), joined((0, 1)))
+    result = joined((0, 1))
+    for step in far:
+        result = joined((step,), result)
+    return result
 
 
 def shards(*arrays):

time: 25.3 us -> 25.3 us (level)
  waiting for transfers between devices: 4.66 us -> 4.02 us
  Pallas kernels: 7.82 us -> 8.42 us
    ppermute x9, waiting for transfers between devices: 4.22 us -> 3.58 us  [swap(): return lax.ppermute(value, 'seq', [(i, i ^ step) for i in range(count)])]
    pallas_call x2 -> x3, Pallas kernels: 1.33 us -> 1.94 us  [joined(): pl.pallas_call(functools.partial(join_kernel, steps=steps, width=width),...]
  transfers between devices with their start and end apart: 11 -> 11, of which waited for: 5 -> 5; matrix products, arithmetic and copies ran while one was open for 0% -> 0% of each run, Pallas kernels for 22% -> 25%
where the time goes in v7:
time: 25.3 us; the launch traced here: 25.1 us
  starting transfers between devices  12.3 us (49%)
  Pallas kernels  8.42 us (33%)
  waiting for transfers between devices  4.02 us (16%)
    ppermute x9, starting transfers between devices, swap(): return lax.ppermute(value, 'seq', [(i, i ^ step) for i in range(count)])  8.66 us
    ppermute x2, starting transfers between devices, head_shards(): lax.ppermute(piece, 'groups', [(i, (i + shift) % groups) for i in range(g...  3.61 us
    ppermute x9, waiting for transfers between devices, swap(): return lax.ppermute(value, 'seq', [(i, i ^ step) for i in range(count)])  3.58 us
    pallas_call x2, Pallas kernels, packed(): pl.pallas_call(functools.partial(pack_kernel, parts=parts, width=width),...  2.29 us
    pallas_call x3, Pallas kernels, joined(): pl.pallas_call(functools.partial(join_kernel, steps=steps, width=width),...  1.94 us
    pallas_call x2, Pallas kernels, head_shards(): pl.pallas_call(functools.partial(conv_kernel, count=count, groups=groups,...  1.68 us
    pallas_call x1, Pallas kernels, head_shards(): pl.pallas_call(functools.partial(smooth_kernel, count=count, block=block)...  1.04 us
    pallas_call x1, Pallas kernels, head_shards(): pl.pallas_call(functools.partial(weigh_kernel, count=count, groups=groups...  0.68 us
  transfers between devices with their start and end apart: 11, of which 5 were waited for; matrix products, arithmetic and copies ran while one was open for 0% of the time, Pallas kernels for 25%

profile of v7, /device:TPU:0, one launch (start us, length us, event | category | flops | bytes accessed | tf_op | source)
XLA Modules:
  0.0 25.1 jit_solution(17464865832083987951)
XLA Ops:
  0.0 1.2 %shard_map.91 = (bf16[640,128]{1,0:T(8,128)(2,1)S(1)}, bf16[640,256]{1,0:T(8,128)(2,1)S(1)}) custom-call(bf16[128,1024]{1,0:T(8,128)(2,1)} %gate_ref.1, bf16[128,1024]{1,0:T(8,128)(2,1)} %value_ref.1, bf16[128,1024]{1,0:T(8,128)(2,1)} %filter_ref.1, bf16[128,1024]{1,0:T(8,128)(2,1)} %own_ref.2, bf16[128,1024]{1,0:T(8,128)(2,1)} %own_ref.3), custom_call_target="tpu_custom_call" | custom-call | tf_op jit(solution)/shard_map/pallas_call | solution.py:481
  1.2 0.5 %collective-permute-start = (bf16[640,256]{1,0:T(8,128)(2,1)S(1)}, bf16[640,256]{1,0:T(8,128)(2,1)S(1)}, u32[]{:S(2)}, u32[]{:S(2)}) collective-permute-start(bf16[640,256]{1,0:T(8,128)(2,1)S(1)} %get-tuple-element.22), channel_id=1, source_target_pairs={{0,4},{4,0},{8,12},{12,8},{1,5},{5,1},{9,13},{13,9},{2,6},{6,2},{1... | collective-permute-start | bytes 983048 | tf_op jit(solution)/shard_map/ppermute | solution.py:478
  1.7 2.6 %collective-permute-start.3 = (bf16[640,128]{1,0:T(8,128)(2,1)S(1)}, bf16[640,128]{1,0:T(8,128)(2,1)S(1)}, u32[]{:S(2)}, u32[]{:S(2)}) collective-permute-start(bf16[640,128]{1,0:T(8,128)(2,1)S(1)} %get-tuple-element.26), channel_id=1, source_target_pairs={{0,8},{4,12},{8,0},{12,4},{1,9},{5,13},{9,1},{13,5},{2,10},{6,14},... | collective-permute-start | bytes 491528 | tf_op jit(solution)/shard_map/ppermute | solution.py:478
  4.3 1.1 %shard_map.92 = (bf16[640,128]{1,0:T(8,128)(2,1)S(1)}, bf16[256,256]{1,0:T(8,128)(2,1)S(1)}, bf16[128,256]{1,0:T(8,128)(2,1)S(1)}, bf16[128,256]{1,0:T(8,128)(2,1)S(1)}) custom-call(bf16[128,1024]{1,0:T(8,128)(2,1)} %gate_ref.1, bf16[128,1024]{1,0:T(8,128)(2,1)} %value_ref.1, bf16[128,1024]{1,0:T(8,128)(2,1)} %filter_ref.1, bf16[128,1024]{1,0:T(8,128)(2,1)} %own_ref.2, ...), custom_call_target="tpu_custom_call" | custom-call | tf_op jit(solution)/shard_map/pallas_call | solution.py:481
  5.4 1.3 %collective-permute-start.4 = (bf16[640,128]{1,0:T(8,128)(2,1)S(1)}, bf16[640,128]{1,0:T(8,128)(2,1)S(1)}, u32[]{:S(2)}, u32[]{:S(2)}) collective-permute-start(bf16[640,128]{1,0:T(8,128)(2,1)S(1)} %get-tuple-element.29), channel_id=1, source_target_pairs={{0,12},{4,8},{8,4},{12,0},{1,13},{5,9},{9,5},{13,1},{2,14},{6,10},... | collective-permute-start | bytes 491528 | tf_op jit(solution)/shard_map/ppermute | solution.py:478
  6.8 0.5 %collective-permute-start.1 = (bf16[256,256]{1,0:T(8,128)(2,1)S(1)}, bf16[256,256]{1,0:T(8,128)(2,1)S(1)}, u32[]{:S(2)}, u32[]{:S(2)}) collective-permute-start(bf16[256,256]{1,0:T(8,128)(2,1)S(1)} %get-tuple-element.23), channel_id=1, source_target_pairs={{0,8},{4,12},{8,0},{12,4},{1,9},{5,13},{9,1},{13,5},{2,10},{6,14},... | collective-permute-start | bytes 393224 | tf_op jit(solution)/shard_map/ppermute | solution.py:478
  7.3 1.2 %collective-permute-start.2 = (bf16[128,256]{1,0:T(8,128)(2,1)S(1)}, bf16[128,256]{1,0:T(8,128)(2,1)S(1)}, u32[]{:S(2)}, u32[]{:S(2)}) collective-permute-start(bf16[128,256]{1,0:T(8,128)(2,1)S(1)} %get-tuple-element.24), channel_id=1, source_target_pairs={{0,12},{4,8},{8,4},{12,0},{1,13},{5,9},{9,5},{13,1},{2,14},{6,10},... | collective-permute-start | bytes 196616 | tf_op jit(solution)/shard_map/ppermute | solution.py:478
  8.5 0.6 %collective-permute-start.7 = (bf16[128,256]{1,0:T(8,128)(2,1)S(1)}, bf16[128,256]{1,0:T(8,128)(2,1)S(1)}, u32[]{:S(2)}, u32[]{:S(2)}) collective-permute-start(bf16[128,256]{1,0:T(8,128)(2,1)S(1)} %get-tuple-element.34), channel_id=1, source_target_pairs={{0,12},{4,8},{8,4},{12,0},{1,13},{5,9},{9,5},{13,1},{2,14},{6,10},... | collective-permute-start | bytes 196616 | tf_op jit(solution)/shard_map/ppermute | solution.py:478
  9.4 0.4 %shard_map.93 = (f32[2,256,256]{2,1,0:T(8,128)S(1)}, f32[2,256,256]{2,1,0:T(8,128)S(1)}, f32[256,256]{1,0:T(8,128)S(1)}) custom-call(bf16[128,1024]{1,0:T(8,128)(2,1)S(1)} %copy-done.2, bf16[128,1024]{1,0:T(8,128)(2,1)S(1)} %copy-done.3, bf16[640,256]{1,0:T(8,128)(2,1)S(1)} %collective-permute-done.rest_5_.near_ref, f32[1024,128]{1,0:T(8,128)S(1)} %copy-done.8, ...), custom_call_target="tpu_custom_call" | custom-call | tf_op jit(solution)/shard_map/pallas_call | solution.py:518
  9.8 2.0 %collective-permute-start.5 = (bf16[128,128]{1,0:T(8,128)(2,1)S(1)}, bf16[128,128]{1,0:T(8,128)(2,1)S(1)}, u32[]{:S(2)}, u32[]{:S(2)}) collective-permute-start(bf16[128,128]{1,0:T(8,128)(2,1)S(1)} %slice.8), channel_id=1, source_target_pairs={{0,16},{16,0},{1,17},{17,1},{2,18},{18,2},{3,19},{19,3},{4,20},{20... | collective-permute-start | bytes 98312 | tf_op jit(solution)/shard_map/ppermute | solution.py:533
  11.9 0.5 %collective-permute-done.4.rest_1_ = bf16[640,128]{1,0:T(8,128)(2,1)S(1)} collective-permute-done((bf16[640,128]{1,0:T(8,128)(2,1)S(1)}, bf16[640,128]{1,0:T(8,128)(2,1)S(1)}, u32[]{:S(2)}, u32[]{:S(2)}) %collective-permute-start.4) | collective-permute-done | bytes 163872 | tf_op jit(solution)/shard_map/ppermute | solution.py:478
  12.3 1.6 %collective-permute-start.6 = (bf16[128,128]{1,0:T(8,128)(2,1)S(1)}, bf16[128,128]{1,0:T(8,128)(2,1)S(1)}, u32[]{:S(2)}, u32[]{:S(2)}) collective-permute-start(bf16[128,128]{1,0:T(8,128)(2,1)S(1)} %slice.9), channel_id=1, source_target_pairs={{0,16},{16,0},{1,17},{17,1},{2,18},{18,2},{3,19},{19,3},{4,20},{20... | collective-permute-start | bytes 98312 | tf_op jit(solution)/shard_map/ppermute | solution.py:533
  13.9 1.0 %shard_map.94.line_ref = f32[4,256,256]{2,1,0:T(8,128)S(1)} custom-call(f32[2,256,256]{2,1,0:T(8,128)S(1)} %get-tuple-element.25.gate_spec_ref, f32[256,256]{1,0:T(8,128)S(1)} %get-tuple-element.28.taps_spec_ref, bf16[128,1024]{1,0:T(8,128)(2,1)S(1)} %copy-done, bf16[640,256]{1,0:T(8,128)(2,1)S(1)} %collective-permute-done.rest_5_.near_ref, ...), custom_call_target="tpu_custom_call" | custom-call | tf_op jit(solution)/shard_map/pallas_call | solution.py:540
  14.9 0.8 %shard_map.95.rest_2_ = bf16[4,128,128]{2,1,0:T(8,128)(2,1)S(1)} custom-call(f32[4,256,256]{2,1,0:T(8,128)S(1)} %shard_map.94.line_ref, f32[2,256,256]{2,1,0:T(8,128)S(1)} %get-tuple-element.30.filter_spec_ref, bf16[640,128]{1,0:T(8,128)(2,1)S(1)} %collective-permute-done.3.rest_0_, bf16[640,128]{1,0:T(8,128)(2,1)S(1)} %collective-permute-done.4.rest_1_, ...), custom_call_target="tpu_custom_call" | custom-call | tf_op jit(solution)/shard_map/pallas_call | solution.py:549
  15.8 0.4 %collective-permute-done.6.rest_1_ = bf16[128,128]{1,0:T(8,128)(2,1)S(1)} collective-permute-done((bf16[128,128]{1,0:T(8,128)(2,1)S(1)}, bf16[128,128]{1,0:T(8,128)(2,1)S(1)}, u32[]{:S(2)}, u32[]{:S(2)}) %collective-permute-start.6) | collective-permute-done | bytes 32800 | tf_op jit(solution)/shard_map/ppermute | solution.py:533
  16.2 0.9 %shard_map.96.rest_3_ = bf16[4,128,128]{2,1,0:T(8,128)(2,1)S(1)} custom-call(f32[4,256,256]{2,1,0:T(8,128)S(1)} %shard_map.94.line_ref, f32[2,256,256]{2,1,0:T(8,128)S(1)} %get-tuple-element.30.filter_spec_ref, bf16[128,128]{1,0:T(8,128)(2,1)S(1)} %collective-permute-done.5.rest_0_, bf16[128,128]{1,0:T(8,128)(2,1)S(1)} %collective-permute-done.6.rest_1_, ...), custom_call_target="tpu_custom_call" | custom-call | tf_op jit(solution)/shard_map/pallas_call | solution.py:549
  17.1 0.7 %shard_map.97 = (bf16[2,4,128,512]{3,2,1,0:T(8,128)(2,1)S(1)}, f32[2,4,128,128]{3,2,1,0:T(8,128)S(1)}) custom-call(bf16[128,1024]{1,0:T(8,128)(2,1)S(1)} %copy-done.4, bf16[640,256]{1,0:T(8,128)(2,1)S(1)} %collective-permute-done.rest_5_.near_ref, bf16[256,256]{1,0:T(8,128)(2,1)S(1)} %collective-permute-done.1.rest_0_, ...), custom_call_target="tpu_custom_call" | custom-call | tf_op jit(solution)/shard_map/pallas_call | solution.py:566
  18.0 0.4 %shard_map.98 = (bf16[128,256]{1,0:T(8,128)(2,1)S(1)}, bf16[128,256]{1,0:T(8,128)(2,1)S(1)}, bf16[128,256]{1,0:T(8,128)(2,1)S(1)}, bf16[128,256]{1,0:T(8,128)(2,1)S(1)}) custom-call(bf16[2,4,128,512]{3,2,1,0:T(8,128)(2,1)S(1)} %get-tuple-element.32.weight_ref, f32[2,4,128,128]{3,2,1,0:T(8,128)S(1)} %get-tuple-element.33.part_ref, ...), custom_call_target="tpu_custom_call" | custom-call | tf_op jit(solution)/shard_map/pallas_call | solution.py:579
  18.6 1.7 %collective-permute-start.9 = (bf16[128,256]{1,0:T(8,128)(2,1)S(1)}, bf16[128,256]{1,0:T(8,128)(2,1)S(1)}, u32[]{:S(2)}, u32[]{:S(2)}) collective-permute-start(bf16[128,256]{1,0:T(8,128)(2,1)S(1)} %get-tuple-element.36), channel_id=1, source_target_pairs={{0,8},{4,12},{8,0},{12,4},{1,9},{5,13},{9,1},{13,5},{2,10},{6,14},... | collective-permute-start | bytes 196616 | tf_op jit(solution)/shard_map/ppermute | solution.py:478
  20.4 0.7 %shard_map.99.rest_1_ = bf16[128,1024]{1,0:T(8,128)(2,1)} custom-call(bf16[128,256]{1,0:T(8,128)(2,1)S(1)} %get-tuple-element.37.rest_0_, bf16[128,256]{1,0:T(8,128)(2,1)S(1)} %collective-permute-done.10.rest_1_), custom_call_target="tpu_custom_call" | custom-call | tf_op jit(solution)/shard_map/pallas_call | solution.py:596
  21.1 2.0 %collective-permute-done.9.rest_0_ = bf16[128,256]{1,0:T(8,128)(2,1)S(1)} collective-permute-done((bf16[128,256]{1,0:T(8,128)(2,1)S(1)}, bf16[128,256]{1,0:T(8,128)(2,1)S(1)}, u32[]{:S(2)}, u32[]{:S(2)}) %collective-permute-start.9) | collective-permute-done | bytes 65568 | tf_op jit(solution)/shard_map/ppermute | solution.py:478
  23.0 0.6 %shard_map.100.rest_1_ = bf16[128,1024]{1,0:T(8,128)(2,1)} custom-call(bf16[128,256]{1,0:T(8,128)(2,1)S(1)} %collective-permute-done.9.rest_0_, bf16[128,1024]{1,0:T(8,128)(2,1)} %shard_map.99.rest_1_), custom_call_target="tpu_custom_call", output_to_operand_aliasing={{}: (1, {})} | custom-call | tf_op jit(solution)/shard_map/pallas_call | solution.py:596
  23.7 0.8 %collective-permute-done.8.rest_0_ = bf16[128,256]{1,0:T(8,128)(2,1)S(1)} collective-permute-done((bf16[128,256]{1,0:T(8,128)(2,1)S(1)}, bf16[128,256]{1,0:T(8,128)(2,1)S(1)}, u32[]{:S(2)}, u32[]{:S(2)}) %collective-permute-start.8) | collective-permute-done | bytes 65568 | tf_op jit(solution)/shard_map/ppermute | solution.py:478
  24.5 0.6 %shard_map.101 = bf16[128,1024]{1,0:T(8,128)(2,1)} custom-call(bf16[128,256]{1,0:T(8,128)(2,1)S(1)} %collective-permute-done.8.rest_0_, bf16[128,1024]{1,0:T(8,128)(2,1)} %shard_map.100.rest_1_), custom_call_target="tpu_custom_call", output_to_operand_aliasing={{}: (1, {})} | custom-call | tf_op jit(solution)/shard_map/pallas_call | solution.py:596
  (29 shorter events, 0.8 us)
Async XLA Ops:
  1.2 3.1 %collective-permute-start = (bf16[640,256]{1,0:T(8,128)(2,1)S(1)}, bf16[640,256]{1,0:T(8,128)(2,1)S(1)}, u32[]{:S(2)}, u32[]{:S(2)}) collective-permute-start(bf16[640,256]{1,0:T(8,128)(2,1)S(1)} %get-tuple-element.22), channel_id=1, source_target_pairs={{0,4},{4,0},{8,12},{12,8},{1,5},{5,1},{9,13},{13,9},{2,6},{6,2},{1... | collective-permute-start | bytes 983048 | tf_op jit(solution)/shard_map/ppermute | solution.py:478
  1.7 7.7 %copy-start.2 = (bf16[128,1024]{1,0:T(8,128)(2,1)S(1)}, bf16[128,1024]{1,0:T(8,128)(2,1)}, u32[]{:S(2)}) copy-start(bf16[128,1024]{1,0:T(8,128)(2,1)} %gate_ref.1) | copy-start | bytes 786436
  1.7 7.7 %copy-start.3 = (bf16[128,1024]{1,0:T(8,128)(2,1)S(1)}, bf16[128,1024]{1,0:T(8,128)(2,1)}, u32[]{:S(2)}) copy-start(bf16[128,1024]{1,0:T(8,128)(2,1)} %filter_ref.1) | copy-start | bytes 786436
  1.7 7.7 %copy-start.8 = (f32[1024,128]{1,0:T(8,128)S(1)}, f32[1024,128]{1,0:T(8,128)}, u32[]{:S(2)}) copy-start(f32[1024,128]{1,0:T(8,128)} %taps_ref.1) | copy-start | bytes 1572868
  1.7 7.7 %collective-permute-start.3 = (bf16[640,128]{1,0:T(8,128)(2,1)S(1)}, bf16[640,128]{1,0:T(8,128)(2,1)S(1)}, u32[]{:S(2)}, u32[]{:S(2)}) collective-permute-start(bf16[640,128]{1,0:T(8,128)(2,1)S(1)} %get-tuple-element.26), channel_id=1, source_target_pairs={{0,8},{4,12},{8,0},{12,4},{1,9},{5,13},{9,1},{13,5},{2,10},{6,14},... | collective-permute-start | bytes 491528 | tf_op jit(solution)/shard_map/ppermute | solution.py:478
  4.3 5.1 %copy-start.5 = (bf16[512,128]{1,0:T(8,128)(2,1)S(1)}, bf16[512,128]{1,0:T(8,128)(2,1)}, u32[]{:S(2)}) copy-start(bf16[512,128]{1,0:T(8,128)(2,1)} %constant.4.clone.ahead_ref.rest_2_.rest_3_) | copy-start | bytes 393220
  5.4 6.9 %collective-permute-start.4 = (bf16[640,128]{1,0:T(8,128)(2,1)S(1)}, bf16[640,128]{1,0:T(8,128)(2,1)S(1)}, u32[]{:S(2)}, u32[]{:S(2)}) collective-permute-start(bf16[640,128]{1,0:T(8,128)(2,1)S(1)} %get-tuple-element.29), channel_id=1, source_target_pairs={{0,12},{4,8},{8,4},{12,0},{1,13},{5,9},{9,5},{13,1},{2,14},{6,10},... | collective-permute-start | bytes 491528 | tf_op jit(solution)/shard_map/ppermute | solution.py:478
  6.8 10.4 %collective-permute-start.1 = (bf16[256,256]{1,0:T(8,128)(2,1)S(1)}, bf16[256,256]{1,0:T(8,128)(2,1)S(1)}, u32[]{:S(2)}, u32[]{:S(2)}) collective-permute-start(bf16[256,256]{1,0:T(8,128)(2,1)S(1)} %get-tuple-element.23), channel_id=1, source_target_pairs={{0,8},{4,12},{8,0},{12,4},{1,9},{5,13},{9,1},{13,5},{2,10},{6,14},... | collective-permute-start | bytes 393224 | tf_op jit(solution)/shard_map/ppermute | solution.py:478
  7.3 9.8 %collective-permute-start.2 = (bf16[128,256]{1,0:T(8,128)(2,1)S(1)}, bf16[128,256]{1,0:T(8,128)(2,1)S(1)}, u32[]{:S(2)}, u32[]{:S(2)}) collective-permute-start(bf16[128,256]{1,0:T(8,128)(2,1)S(1)} %get-tuple-element.24), channel_id=1, source_target_pairs={{0,12},{4,8},{8,4},{12,0},{1,13},{5,9},{9,5},{13,1},{2,14},{6,10},... | collective-permute-start | bytes 196616 | tf_op jit(solution)/shard_map/ppermute | solution.py:478
  8.5 9.4 %collective-permute-start.7 = (bf16[128,256]{1,0:T(8,128)(2,1)S(1)}, bf16[128,256]{1,0:T(8,128)(2,1)S(1)}, u32[]{:S(2)}, u32[]{:S(2)}) collective-permute-start(bf16[128,256]{1,0:T(8,128)(2,1)S(1)} %get-tuple-element.34), channel_id=1, source_target_pairs={{0,12},{4,8},{8,4},{12,0},{1,13},{5,9},{9,5},{13,1},{2,14},{6,10},... | collective-permute-start | bytes 196616 | tf_op jit(solution)/shard_map/ppermute | solution.py:478
  9.4 4.5 %copy-start = (bf16[128,1024]{1,0:T(8,128)(2,1)S(1)}, bf16[128,1024]{1,0:T(8,128)(2,1)}, u32[]{:S(2)}) copy-start(bf16[128,1024]{1,0:T(8,128)(2,1)} %value_ref.1) | copy-start | bytes 786436
  9.4 4.5 %copy-start.6 = (bf16[256,256]{1,0:T(8,128)(2,1)S(1)}, bf16[256,256]{1,0:T(8,128)(2,1)}, u32[]{:S(2)}) copy-start(bf16[256,256]{1,0:T(8,128)(2,1)} %constant.5.clone.rest_3_.rest_4_) | copy-start | bytes 393220
  9.8 6.0 %collective-permute-start.5 = (bf16[128,128]{1,0:T(8,128)(2,1)S(1)}, bf16[128,128]{1,0:T(8,128)(2,1)S(1)}, u32[]{:S(2)}, u32[]{:S(2)}) collective-permute-start(bf16[128,128]{1,0:T(8,128)(2,1)S(1)} %slice.8), channel_id=1, source_target_pairs={{0,16},{16,0},{1,17},{17,1},{2,18},{18,2},{3,19},{19,3},{4,20},{20... | collective-permute-start | bytes 98312 | tf_op jit(solution)/shard_map/ppermute | solution.py:533
  12.3 3.9 %collective-permute-start.6 = (bf16[128,128]{1,0:T(8,128)(2,1)S(1)}, bf16[128,128]{1,0:T(8,128)(2,1)S(1)}, u32[]{:S(2)}, u32[]{:S(2)}) collective-permute-start(bf16[128,128]{1,0:T(8,128)(2,1)S(1)} %slice.9), channel_id=1, source_target_pairs={{0,16},{16,0},{1,17},{17,1},{2,18},{18,2},{3,19},{19,3},{4,20},{20... | collective-permute-start | bytes 98312 | tf_op jit(solution)/shard_map/ppermute | solution.py:533
  13.9 1.0 %copy-start.7 = (bf16[8,128,128]{2,1,0:T(8,128)(2,1)S(1)}, bf16[8,128,128]{2,1,0:T(8,128)(2,1)}, u32[]{:S(2)}) copy-start(bf16[8,128,128]{2,1,0:T(8,128)(2,1)} %rest_2_.8) | copy-start | bytes 786436
  15.8 1.4 %copy-start.4 = (bf16[128,1024]{1,0:T(8,128)(2,1)S(1)}, bf16[128,1024]{1,0:T(8,128)(2,1)}, u32[]{:S(2)}) copy-start(bf16[128,1024]{1,0:T(8,128)(2,1)} %own_ref.2) | copy-start | bytes 786436
  17.1 1.0 %copy-start.1 = (bf16[128,1024]{1,0:T(8,128)(2,1)S(1)}, bf16[128,1024]{1,0:T(8,128)(2,1)}, u32[]{:S(2)}) copy-start(bf16[128,1024]{1,0:T(8,128)(2,1)} %own_ref.3) | copy-start | bytes 786436
  18.4 1.9 %collective-permute-start.10 = (bf16[128,256]{1,0:T(8,128)(2,1)S(1)}, bf16[128,256]{1,0:T(8,128)(2,1)S(1)}, u32[]{:S(2)}, u32[]{:S(2)}) collective-permute-start(bf16[128,256]{1,0:T(8,128)(2,1)S(1)} %get-tuple-element.38), channel_id=1, source_target_pairs={{0,4},{4,0},{8,12},{12,8},{1,5},{5,1},{9,13},{13,9},{2,6},{6,2},{1... | collective-permute-start | bytes 196616 | tf_op jit(solution)/shard_map/ppermute | solution.py:478
  18.6 4.4 %collective-permute-start.9 = (bf16[128,256]{1,0:T(8,128)(2,1)S(1)}, bf16[128,256]{1,0:T(8,128)(2,1)S(1)}, u32[]{:S(2)}, u32[]{:S(2)}) collective-permute-start(bf16[128,256]{1,0:T(8,128)(2,1)S(1)} %get-tuple-element.36), channel_id=1, source_target_pairs={{0,8},{4,12},{8,0},{12,4},{1,9},{5,13},{9,1},{13,5},{2,10},{6,14},... | collective-permute-start | bytes 196616 | tf_op jit(solution)/shard_map/ppermute | solution.py:478
  20.3 4.1 %collective-permute-start.8 = (bf16[128,256]{1,0:T(8,128)(2,1)S(1)}, bf16[128,256]{1,0:T(8,128)(2,1)S(1)}, u32[]{:S(2)}, u32[]{:S(2)}) collective-permute-start(bf16[128,256]{1,0:T(8,128)(2,1)S(1)} %get-tuple-element.35), channel_id=1, source_target_pairs={{0,12},{4,8},{8,4},{12,0},{1,13},{5,9},{9,5},{13,1},{2,14},{6,10},... | collective-permute-start | bytes 196616 | tf_op jit(solution)/shard_map/ppermute | solution.py:478

commit v8 on v7

--- a/solution.py
+++ b/solution.py
@@ -498,7 +498,7 @@
     far = range(2, count)
     share = width // groups
     slots = range(groups)
-    streams = [(i, slot) for i in (0, 1) for slot in slots] + [(2, None)]
+    streams = [(i, slot) for i in (0, 1) for slot in slots] + [(2, None if groups > 1 else 0)]
     arrays = [gate_input, value_input, long_filter, key_matrix, value_matrix]
     first, near = packed(
         arrays, [(far[0], share, streams), (1, width, [(n, 0) for n in range(5)])]
@@ -613,7 +613,7 @@
     count = lax.axis_size("seq")
     block, local_width = arrays[0].shape
     even = local_width % (count * HEAD_DIM) == 0
-    if even and count > 1 and count & (count - 1) == 0 and block == TAPS:
+    if even and count > 3 and count & (count - 1) == 0 and block == TAPS:
         return head_shards(*arrays)
     return general_shards(*arrays)
 

time: 25.3 us -> 25.3 us (level)
  no operation moved by 1% of the time
where the time goes in v8:
time: 25.3 us; the launch traced here: 25.1 us
  starting transfers between devices  12.3 us (49%)
  Pallas kernels  8.42 us (33%)
  waiting for transfers between devices  4.02 us (16%)
    ppermute x9, starting transfers between devices, swap(): return lax.ppermute(value, 'seq', [(i, i ^ step) for i in range(count)])  8.66 us
    ppermute x2, starting transfers between devices, head_shards(): lax.ppermute(piece, 'groups', [(i, (i + shift) % groups) for i in range(g...  3.61 us
    ppermute x9, waiting for transfers between devices, swap(): return lax.ppermute(value, 'seq', [(i, i ^ step) for i in range(count)])  3.58 us
    pallas_call x2, Pallas kernels, packed(): pl.pallas_call(functools.partial(pack_kernel, parts=parts, width=width),...  2.29 us
    pallas_call x3, Pallas kernels, joined(): pl.pallas_call(functools.partial(join_kernel, steps=steps, width=width),...  1.94 us
    pallas_call x2, Pallas kernels, head_shards(): pl.pallas_call(functools.partial(conv_kernel, count=count, groups=groups,...  1.68 us
    pallas_call x1, Pallas kernels, head_shards(): pl.pallas_call(functools.partial(smooth_kernel, count=count, block=block)...  1.04 us
    pallas_call x1, Pallas kernels, head_shards(): pl.pallas_call(functools.partial(weigh_kernel, count=count, groups=groups...  0.68 us
  transfers between devices with their start and end apart: 11, of which 5 were waited for; matrix products, arithmetic and copies ran while one was open for 0% of the time, Pallas kernels for 25%

profile of v8, /device:TPU:0, one launch (start us, length us, event | category | flops | bytes accessed | tf_op | source)
XLA Modules:
  0.0 25.1 jit_solution(17464865832083987951)
XLA Ops:
  0.0 1.2 %shard_map.91 = (bf16[640,128]{1,0:T(8,128)(2,1)S(1)}, bf16[640,256]{1,0:T(8,128)(2,1)S(1)}) custom-call(bf16[128,1024]{1,0:T(8,128)(2,1)} %gate_ref.1, bf16[128,1024]{1,0:T(8,128)(2,1)} %value_ref.1, bf16[128,1024]{1,0:T(8,128)(2,1)} %filter_ref.1, bf16[128,1024]{1,0:T(8,128)(2,1)} %own_ref.2, bf16[128,1024]{1,0:T(8,128)(2,1)} %own_ref.3), custom_call_target="tpu_custom_call" | custom-call | tf_op jit(solution)/shard_map/pallas_call | solution.py:481
  1.2 0.5 %collective-permute-start = (bf16[640,256]{1,0:T(8,128)(2,1)S(1)}, bf16[640,256]{1,0:T(8,128)(2,1)S(1)}, u32[]{:S(2)}, u32[]{:S(2)}) collective-permute-start(bf16[640,256]{1,0:T(8,128)(2,1)S(1)} %get-tuple-element.22), channel_id=1, source_target_pairs={{0,4},{4,0},{8,12},{12,8},{1,5},{5,1},{9,13},{13,9},{2,6},{6,2},{1... | collective-permute-start | bytes 983048 | tf_op jit(solution)/shard_map/ppermute | solution.py:478
  1.7 2.6 %collective-permute-start.3 = (bf16[640,128]{1,0:T(8,128)(2,1)S(1)}, bf16[640,128]{1,0:T(8,128)(2,1)S(1)}, u32[]{:S(2)}, u32[]{:S(2)}) collective-permute-start(bf16[640,128]{1,0:T(8,128)(2,1)S(1)} %get-tuple-element.26), channel_id=1, source_target_pairs={{0,8},{4,12},{8,0},{12,4},{1,9},{5,13},{9,1},{13,5},{2,10},{6,14},... | collective-permute-start | bytes 491528 | tf_op jit(solution)/shard_map/ppermute | solution.py:478
  4.3 1.1 %shard_map.92 = (bf16[640,128]{1,0:T(8,128)(2,1)S(1)}, bf16[256,256]{1,0:T(8,128)(2,1)S(1)}, bf16[128,256]{1,0:T(8,128)(2,1)S(1)}, bf16[128,256]{1,0:T(8,128)(2,1)S(1)}) custom-call(bf16[128,1024]{1,0:T(8,128)(2,1)} %gate_ref.1, bf16[128,1024]{1,0:T(8,128)(2,1)} %value_ref.1, bf16[128,1024]{1,0:T(8,128)(2,1)} %filter_ref.1, bf16[128,1024]{1,0:T(8,128)(2,1)} %own_ref.2, ...), custom_call_target="tpu_custom_call" | custom-call | tf_op jit(solution)/shard_map/pallas_call | solution.py:481
  5.4 1.3 %collective-permute-start.4 = (bf16[640,128]{1,0:T(8,128)(2,1)S(1)}, bf16[640,128]{1,0:T(8,128)(2,1)S(1)}, u32[]{:S(2)}, u32[]{:S(2)}) collective-permute-start(bf16[640,128]{1,0:T(8,128)(2,1)S(1)} %get-tuple-element.29), channel_id=1, source_target_pairs={{0,12},{4,8},{8,4},{12,0},{1,13},{5,9},{9,5},{13,1},{2,14},{6,10},... | collective-permute-start | bytes 491528 | tf_op jit(solution)/shard_map/ppermute | solution.py:478
  6.8 0.5 %collective-permute-start.1 = (bf16[256,256]{1,0:T(8,128)(2,1)S(1)}, bf16[256,256]{1,0:T(8,128)(2,1)S(1)}, u32[]{:S(2)}, u32[]{:S(2)}) collective-permute-start(bf16[256,256]{1,0:T(8,128)(2,1)S(1)} %get-tuple-element.23), channel_id=1, source_target_pairs={{0,8},{4,12},{8,0},{12,4},{1,9},{5,13},{9,1},{13,5},{2,10},{6,14},... | collective-permute-start | bytes 393224 | tf_op jit(solution)/shard_map/ppermute | solution.py:478
  7.3 1.2 %collective-permute-start.2 = (bf16[128,256]{1,0:T(8,128)(2,1)S(1)}, bf16[128,256]{1,0:T(8,128)(2,1)S(1)}, u32[]{:S(2)}, u32[]{:S(2)}) collective-permute-start(bf16[128,256]{1,0:T(8,128)(2,1)S(1)} %get-tuple-element.24), channel_id=1, source_target_pairs={{0,12},{4,8},{8,4},{12,0},{1,13},{5,9},{9,5},{13,1},{2,14},{6,10},... | collective-permute-start | bytes 196616 | tf_op jit(solution)/shard_map/ppermute | solution.py:478
  8.5 0.6 %collective-permute-start.7 = (bf16[128,256]{1,0:T(8,128)(2,1)S(1)}, bf16[128,256]{1,0:T(8,128)(2,1)S(1)}, u32[]{:S(2)}, u32[]{:S(2)}) collective-permute-start(bf16[128,256]{1,0:T(8,128)(2,1)S(1)} %get-tuple-element.34), channel_id=1, source_target_pairs={{0,12},{4,8},{8,4},{12,0},{1,13},{5,9},{9,5},{13,1},{2,14},{6,10},... | collective-permute-start | bytes 196616 | tf_op jit(solution)/shard_map/ppermute | solution.py:478
  9.4 0.4 %shard_map.93 = (f32[2,256,256]{2,1,0:T(8,128)S(1)}, f32[2,256,256]{2,1,0:T(8,128)S(1)}, f32[256,256]{1,0:T(8,128)S(1)}) custom-call(bf16[128,1024]{1,0:T(8,128)(2,1)S(1)} %copy-done.2, bf16[128,1024]{1,0:T(8,128)(2,1)S(1)} %copy-done.3, bf16[640,256]{1,0:T(8,128)(2,1)S(1)} %collective-permute-done.rest_5_.near_ref, f32[1024,128]{1,0:T(8,128)S(1)} %copy-done.8, ...), custom_call_target="tpu_custom_call" | custom-call | tf_op jit(solution)/shard_map/pallas_call | solution.py:518
  9.8 2.0 %collective-permute-start.5 = (bf16[128,128]{1,0:T(8,128)(2,1)S(1)}, bf16[128,128]{1,0:T(8,128)(2,1)S(1)}, u32[]{:S(2)}, u32[]{:S(2)}) collective-permute-start(bf16[128,128]{1,0:T(8,128)(2,1)S(1)} %slice.8), channel_id=1, source_target_pairs={{0,16},{16,0},{1,17},{17,1},{2,18},{18,2},{3,19},{19,3},{4,20},{20... | collective-permute-start | bytes 98312 | tf_op jit(solution)/shard_map/ppermute | solution.py:533
  11.9 0.5 %collective-permute-done.4.rest_1_ = bf16[640,128]{1,0:T(8,128)(2,1)S(1)} collective-permute-done((bf16[640,128]{1,0:T(8,128)(2,1)S(1)}, bf16[640,128]{1,0:T(8,128)(2,1)S(1)}, u32[]{:S(2)}, u32[]{:S(2)}) %collective-permute-start.4) | collective-permute-done | bytes 163872 | tf_op jit(solution)/shard_map/ppermute | solution.py:478
  12.3 1.6 %collective-permute-start.6 = (bf16[128,128]{1,0:T(8,128)(2,1)S(1)}, bf16[128,128]{1,0:T(8,128)(2,1)S(1)}, u32[]{:S(2)}, u32[]{:S(2)}) collective-permute-start(bf16[128,128]{1,0:T(8,128)(2,1)S(1)} %slice.9), channel_id=1, source_target_pairs={{0,16},{16,0},{1,17},{17,1},{2,18},{18,2},{3,19},{19,3},{4,20},{20... | collective-permute-start | bytes 98312 | tf_op jit(solution)/shard_map/ppermute | solution.py:533
  13.9 1.0 %shard_map.94.line_ref = f32[4,256,256]{2,1,0:T(8,128)S(1)} custom-call(f32[2,256,256]{2,1,0:T(8,128)S(1)} %get-tuple-element.25.gate_spec_ref, f32[256,256]{1,0:T(8,128)S(1)} %get-tuple-element.28.taps_spec_ref, bf16[128,1024]{1,0:T(8,128)(2,1)S(1)} %copy-done, bf16[640,256]{1,0:T(8,128)(2,1)S(1)} %collective-permute-done.rest_5_.near_ref, ...), custom_call_target="tpu_custom_call" | custom-call | tf_op jit(solution)/shard_map/pallas_call | solution.py:540
  14.9 0.8 %shard_map.95.rest_2_ = bf16[4,128,128]{2,1,0:T(8,128)(2,1)S(1)} custom-call(f32[4,256,256]{2,1,0:T(8,128)S(1)} %shard_map.94.line_ref, f32[2,256,256]{2,1,0:T(8,128)S(1)} %get-tuple-element.30.filter_spec_ref, bf16[640,128]{1,0:T(8,128)(2,1)S(1)} %collective-permute-done.3.rest_0_, bf16[640,128]{1,0:T(8,128)(2,1)S(1)} %collective-permute-done.4.rest_1_, ...), custom_call_target="tpu_custom_call" | custom-call | tf_op jit(solution)/shard_map/pallas_call | solution.py:549
  15.8 0.4 %collective-permute-done.6.rest_1_ = bf16[128,128]{1,0:T(8,128)(2,1)S(1)} collective-permute-done((bf16[128,128]{1,0:T(8,128)(2,1)S(1)}, bf16[128,128]{1,0:T(8,128)(2,1)S(1)}, u32[]{:S(2)}, u32[]{:S(2)}) %collective-permute-start.6) | collective-permute-done | bytes 32800 | tf_op jit(solution)/shard_map/ppermute | solution.py:533
  16.2 0.9 %shard_map.96.rest_3_ = bf16[4,128,128]{2,1,0:T(8,128)(2,1)S(1)} custom-call(f32[4,256,256]{2,1,0:T(8,128)S(1)} %shard_map.94.line_ref, f32[2,256,256]{2,1,0:T(8,128)S(1)} %get-tuple-element.30.filter_spec_ref, bf16[128,128]{1,0:T(8,128)(2,1)S(1)} %collective-permute-done.5.rest_0_, bf16[128,128]{1,0:T(8,128)(2,1)S(1)} %collective-permute-done.6.rest_1_, ...), custom_call_target="tpu_custom_call" | custom-call | tf_op jit(solution)/shard_map/pallas_call | solution.py:549
  17.1 0.7 %shard_map.97 = (bf16[2,4,128,512]{3,2,1,0:T(8,128)(2,1)S(1)}, f32[2,4,128,128]{3,2,1,0:T(8,128)S(1)}) custom-call(bf16[128,1024]{1,0:T(8,128)(2,1)S(1)} %copy-done.4, bf16[640,256]{1,0:T(8,128)(2,1)S(1)} %collective-permute-done.rest_5_.near_ref, bf16[256,256]{1,0:T(8,128)(2,1)S(1)} %collective-permute-done.1.rest_0_, ...), custom_call_target="tpu_custom_call" | custom-call | tf_op jit(solution)/shard_map/pallas_call | solution.py:566
  18.0 0.4 %shard_map.98 = (bf16[128,256]{1,0:T(8,128)(2,1)S(1)}, bf16[128,256]{1,0:T(8,128)(2,1)S(1)}, bf16[128,256]{1,0:T(8,128)(2,1)S(1)}, bf16[128,256]{1,0:T(8,128)(2,1)S(1)}) custom-call(bf16[2,4,128,512]{3,2,1,0:T(8,128)(2,1)S(1)} %get-tuple-element.32.weight_ref, f32[2,4,128,128]{3,2,1,0:T(8,128)S(1)} %get-tuple-element.33.part_ref, ...), custom_call_target="tpu_custom_call" | custom-call | tf_op jit(solution)/shard_map/pallas_call | solution.py:579
  18.6 1.7 %collective-permute-start.9 = (bf16[128,256]{1,0:T(8,128)(2,1)S(1)}, bf16[128,256]{1,0:T(8,128)(2,1)S(1)}, u32[]{:S(2)}, u32[]{:S(2)}) collective-permute-start(bf16[128,256]{1,0:T(8,128)(2,1)S(1)} %get-tuple-element.36), channel_id=1, source_target_pairs={{0,8},{4,12},{8,0},{12,4},{1,9},{5,13},{9,1},{13,5},{2,10},{6,14},... | collective-permute-start | bytes 196616 | tf_op jit(solution)/shard_map/ppermute | solution.py:478
  20.4 0.7 %shard_map.99.rest_1_ = bf16[128,1024]{1,0:T(8,128)(2,1)} custom-call(bf16[128,256]{1,0:T(8,128)(2,1)S(1)} %get-tuple-element.37.rest_0_, bf16[128,256]{1,0:T(8,128)(2,1)S(1)} %collective-permute-done.10.rest_1_), custom_call_target="tpu_custom_call" | custom-call | tf_op jit(solution)/shard_map/pallas_call | solution.py:596
  21.1 2.0 %collective-permute-done.9.rest_0_ = bf16[128,256]{1,0:T(8,128)(2,1)S(1)} collective-permute-done((bf16[128,256]{1,0:T(8,128)(2,1)S(1)}, bf16[128,256]{1,0:T(8,128)(2,1)S(1)}, u32[]{:S(2)}, u32[]{:S(2)}) %collective-permute-start.9) | collective-permute-done | bytes 65568 | tf_op jit(solution)/shard_map/ppermute | solution.py:478
  23.0 0.6 %shard_map.100.rest_1_ = bf16[128,1024]{1,0:T(8,128)(2,1)} custom-call(bf16[128,256]{1,0:T(8,128)(2,1)S(1)} %collective-permute-done.9.rest_0_, bf16[128,1024]{1,0:T(8,128)(2,1)} %shard_map.99.rest_1_), custom_call_target="tpu_custom_call", output_to_operand_aliasing={{}: (1, {})} | custom-call | tf_op jit(solution)/shard_map/pallas_call | solution.py:596
  23.7 0.8 %collective-permute-done.8.rest_0_ = bf16[128,256]{1,0:T(8,128)(2,1)S(1)} collective-permute-done((bf16[128,256]{1,0:T(8,128)(2,1)S(1)}, bf16[128,256]{1,0:T(8,128)(2,1)S(1)}, u32[]{:S(2)}, u32[]{:S(2)}) %collective-permute-start.8) | collective-permute-done | bytes 65568 | tf_op jit(solution)/shard_map/ppermute | solution.py:478
  24.5 0.6 %shard_map.101 = bf16[128,1024]{1,0:T(8,128)(2,1)} custom-call(bf16[128,256]{1,0:T(8,128)(2,1)S(1)} %collective-permute-done.8.rest_0_, bf16[128,1024]{1,0:T(8,128)(2,1)} %shard_map.100.rest_1_), custom_call_target="tpu_custom_call", output_to_operand_aliasing={{}: (1, {})} | custom-call | tf_op jit(solution)/shard_map/pallas_call | solution.py:596
  (29 shorter events, 0.8 us)
Async XLA Ops:
  1.2 3.1 %collective-permute-start = (bf16[640,256]{1,0:T(8,128)(2,1)S(1)}, bf16[640,256]{1,0:T(8,128)(2,1)S(1)}, u32[]{:S(2)}, u32[]{:S(2)}) collective-permute-start(bf16[640,256]{1,0:T(8,128)(2,1)S(1)} %get-tuple-element.22), channel_id=1, source_target_pairs={{0,4},{4,0},{8,12},{12,8},{1,5},{5,1},{9,13},{13,9},{2,6},{6,2},{1... | collective-permute-start | bytes 983048 | tf_op jit(solution)/shard_map/ppermute | solution.py:478
  1.7 7.7 %copy-start.2 = (bf16[128,1024]{1,0:T(8,128)(2,1)S(1)}, bf16[128,1024]{1,0:T(8,128)(2,1)}, u32[]{:S(2)}) copy-start(bf16[128,1024]{1,0:T(8,128)(2,1)} %gate_ref.1) | copy-start | bytes 786436
  1.7 7.7 %copy-start.3 = (bf16[128,1024]{1,0:T(8,128)(2,1)S(1)}, bf16[128,1024]{1,0:T(8,128)(2,1)}, u32[]{:S(2)}) copy-start(bf16[128,1024]{1,0:T(8,128)(2,1)} %filter_ref.1) | copy-start | bytes 786436
  1.7 7.7 %copy-start.8 = (f32[1024,128]{1,0:T(8,128)S(1)}, f32[1024,128]{1,0:T(8,128)}, u32[]{:S(2)}) copy-start(f32[1024,128]{1,0:T(8,128)} %taps_ref.1) | copy-start | bytes 1572868
  1.7 7.7 %collective-permute-start.3 = (bf16[640,128]{1,0:T(8,128)(2,1)S(1)}, bf16[640,128]{1,0:T(8,128)(2,1)S(1)}, u32[]{:S(2)}, u32[]{:S(2)}) collective-permute-start(bf16[640,128]{1,0:T(8,128)(2,1)S(1)} %get-tuple-element.26), channel_id=1, source_target_pairs={{0,8},{4,12},{8,0},{12,4},{1,9},{5,13},{9,1},{13,5},{2,10},{6,14},... | collective-permute-start | bytes 491528 | tf_op jit(solution)/shard_map/ppermute | solution.py:478
  4.3 5.1 %copy-start.5 = (bf16[512,128]{1,0:T(8,128)(2,1)S(1)}, bf16[512,128]{1,0:T(8,128)(2,1)}, u32[]{:S(2)}) copy-start(bf16[512,128]{1,0:T(8,128)(2,1)} %constant.4.clone.ahead_ref.rest_2_.rest_3_) | copy-start | bytes 393220
  5.4 6.9 %collective-permute-start.4 = (bf16[640,128]{1,0:T(8,128)(2,1)S(1)}, bf16[640,128]{1,0:T(8,128)(2,1)S(1)}, u32[]{:S(2)}, u32[]{:S(2)}) collective-permute-start(bf16[640,128]{1,0:T(8,128)(2,1)S(1)} %get-tuple-element.29), channel_id=1, source_target_pairs={{0,12},{4,8},{8,4},{12,0},{1,13},{5,9},{9,5},{13,1},{2,14},{6,10},... | collective-permute-start | bytes 491528 | tf_op jit(solution)/shard_map/ppermute | solution.py:478
  6.8 10.4 %collective-permute-start.1 = (bf16[256,256]{1,0:T(8,128)(2,1)S(1)}, bf16[256,256]{1,0:T(8,128)(2,1)S(1)}, u32[]{:S(2)}, u32[]{:S(2)}) collective-permute-start(bf16[256,256]{1,0:T(8,128)(2,1)S(1)} %get-tuple-element.23), channel_id=1, source_target_pairs={{0,8},{4,12},{8,0},{12,4},{1,9},{5,13},{9,1},{13,5},{2,10},{6,14},... | collective-permute-start | bytes 393224 | tf_op jit(solution)/shard_map/ppermute | solution.py:478
  7.3 9.8 %collective-permute-start.2 = (bf16[128,256]{1,0:T(8,128)(2,1)S(1)}, bf16[128,256]{1,0:T(8,128)(2,1)S(1)}, u32[]{:S(2)}, u32[]{:S(2)}) collective-permute-start(bf16[128,256]{1,0:T(8,128)(2,1)S(1)} %get-tuple-element.24), channel_id=1, source_target_pairs={{0,12},{4,8},{8,4},{12,0},{1,13},{5,9},{9,5},{13,1},{2,14},{6,10},... | collective-permute-start | bytes 196616 | tf_op jit(solution)/shard_map/ppermute | solution.py:478
  8.5 9.4 %collective-permute-start.7 = (bf16[128,256]{1,0:T(8,128)(2,1)S(1)}, bf16[128,256]{1,0:T(8,128)(2,1)S(1)}, u32[]{:S(2)}, u32[]{:S(2)}) collective-permute-start(bf16[128,256]{1,0:T(8,128)(2,1)S(1)} %get-tuple-element.34), channel_id=1, source_target_pairs={{0,12},{4,8},{8,4},{12,0},{1,13},{5,9},{9,5},{13,1},{2,14},{6,10},... | collective-permute-start | bytes 196616 | tf_op jit(solution)/shard_map/ppermute | solution.py:478
  9.4 4.5 %copy-start = (bf16[128,1024]{1,0:T(8,128)(2,1)S(1)}, bf16[128,1024]{1,0:T(8,128)(2,1)}, u32[]{:S(2)}) copy-start(bf16[128,1024]{1,0:T(8,128)(2,1)} %value_ref.1) | copy-start | bytes 786436
  9.4 4.5 %copy-start.6 = (bf16[256,256]{1,0:T(8,128)(2,1)S(1)}, bf16[256,256]{1,0:T(8,128)(2,1)}, u32[]{:S(2)}) copy-start(bf16[256,256]{1,0:T(8,128)(2,1)} %constant.5.clone.rest_3_.rest_4_) | copy-start | bytes 393220
  9.8 6.0 %collective-permute-start.5 = (bf16[128,128]{1,0:T(8,128)(2,1)S(1)}, bf16[128,128]{1,0:T(8,128)(2,1)S(1)}, u32[]{:S(2)}, u32[]{:S(2)}) collective-permute-start(bf16[128,128]{1,0:T(8,128)(2,1)S(1)} %slice.8), channel_id=1, source_target_pairs={{0,16},{16,0},{1,17},{17,1},{2,18},{18,2},{3,19},{19,3},{4,20},{20... | collective-permute-start | bytes 98312 | tf_op jit(solution)/shard_map/ppermute | solution.py:533
  12.3 3.9 %collective-permute-start.6 = (bf16[128,128]{1,0:T(8,128)(2,1)S(1)}, bf16[128,128]{1,0:T(8,128)(2,1)S(1)}, u32[]{:S(2)}, u32[]{:S(2)}) collective-permute-start(bf16[128,128]{1,0:T(8,128)(2,1)S(1)} %slice.9), channel_id=1, source_target_pairs={{0,16},{16,0},{1,17},{17,1},{2,18},{18,2},{3,19},{19,3},{4,20},{20... | collective-permute-start | bytes 98312 | tf_op jit(solution)/shard_map/ppermute | solution.py:533
  13.9 1.0 %copy-start.7 = (bf16[8,128,128]{2,1,0:T(8,128)(2,1)S(1)}, bf16[8,128,128]{2,1,0:T(8,128)(2,1)}, u32[]{:S(2)}) copy-start(bf16[8,128,128]{2,1,0:T(8,128)(2,1)} %rest_2_.8) | copy-start | bytes 786436
  15.8 1.4 %copy-start.4 = (bf16[128,1024]{1,0:T(8,128)(2,1)S(1)}, bf16[128,1024]{1,0:T(8,128)(2,1)}, u32[]{:S(2)}) copy-start(bf16[128,1024]{1,0:T(8,128)(2,1)} %own_ref.2) | copy-start | bytes 786436
  17.1 1.0 %copy-start.1 = (bf16[128,1024]{1,0:T(8,128)(2,1)S(1)}, bf16[128,1024]{1,0:T(8,128)(2,1)}, u32[]{:S(2)}) copy-start(bf16[128,1024]{1,0:T(8,128)(2,1)} %own_ref.3) | copy-start | bytes 786436
  18.4 1.9 %collective-permute-start.10 = (bf16[128,256]{1,0:T(8,128)(2,1)S(1)}, bf16[128,256]{1,0:T(8,128)(2,1)S(1)}, u32[]{:S(2)}, u32[]{:S(2)}) collective-permute-start(bf16[128,256]{1,0:T(8,128)(2,1)S(1)} %get-tuple-element.38), channel_id=1, source_target_pairs={{0,4},{4,0},{8,12},{12,8},{1,5},{5,1},{9,13},{13,9},{2,6},{6,2},{1... | collective-permute-start | bytes 196616 | tf_op jit(solution)/shard_map/ppermute | solution.py:478
  18.6 4.4 %collective-permute-start.9 = (bf16[128,256]{1,0:T(8,128)(2,1)S(1)}, bf16[128,256]{1,0:T(8,128)(2,1)S(1)}, u32[]{:S(2)}, u32[]{:S(2)}) collective-permute-start(bf16[128,256]{1,0:T(8,128)(2,1)S(1)} %get-tuple-element.36), channel_id=1, source_target_pairs={{0,8},{4,12},{8,0},{12,4},{1,9},{5,13},{9,1},{13,5},{2,10},{6,14},... | collective-permute-start | bytes 196616 | tf_op jit(solution)/shard_map/ppermute | solution.py:478
  20.3 4.1 %collective-permute-start.8 = (bf16[128,256]{1,0:T(8,128)(2,1)S(1)}, bf16[128,256]{1,0:T(8,128)(2,1)S(1)}, u32[]{:S(2)}, u32[]{:S(2)}) collective-permute-start(bf16[128,256]{1,0:T(8,128)(2,1)S(1)} %get-tuple-element.35), channel_id=1, source_target_pairs={{0,12},{4,8},{8,4},{12,0},{1,13},{5,9},{9,5},{13,1},{2,14},{6,10},... | collective-permute-start | bytes 196616 | tf_op jit(solution)/shard_map/ppermute | solution.py:478

commit v9 on v8

--- a/solution.py
+++ b/solution.py
@@ -501,16 +501,18 @@
     streams = [(i, slot) for i in (0, 1) for slot in slots] + [(2, None if groups > 1 else 0)]
     arrays = [gate_input, value_input, long_filter, key_matrix, value_matrix]
     first, near = packed(
-        arrays, [(far[0], share, streams), (1, width, [(n, 0) for n in range(5)])]
+        arrays, [(far[0], share, streams), (1, width, [(n, 0) for n in range(3)])]
     )
     near = swap(near, 1)
-    pieces = packed(
+    near_later, *pieces = packed(
         arrays,
-        [(step, share, streams) for step in far[1:]]
+        [(1, width, [(3, 0), (4, 0)])]
+        + [(step, share, streams) for step in far[1:]]
         + [(step, width, [(3, 0), (4, 0)]) for step in far[:-1]]
         + [(far[-1], width, [(n, 0)]) for n in (3, 4)],
         after=[near],
     )
+    near_later = swap(near_later, 1)
     arrived = [swap(piece, step) for step, piece in zip(far, [first, *pieces])]
     later = pieces[len(far) - 1 :]
     tables = jnp.asarray(ahead), jnp.asarray(back)
@@ -527,7 +529,9 @@
         compiler_params=params,
     )(gate_input, long_filter, near, short_filter, tables[0])
     filters = [piece[-block:] for piece in arrived]
-    filters[0], taps_spec = lax.optimization_barrier((filters[0], taps_spec))
+    filters[0], taps_spec, near_later = lax.optimization_barrier(
+        (filters[0], taps_spec, near_later)
+    )
     shares = [arrived] + [
         [
             lax.ppermute(piece, "groups", [(i, (i + shift) % groups) for i in range(groups)])
@@ -575,7 +579,7 @@
         out_specs=[WHOLE] * 2,
         scratch_shapes=[scratch(count)],
         compiler_params=params,
-    )(key_matrix, near, *arrived_keys, *queries)
+    )(key_matrix, near_later, *arrived_keys, *queries)
     pieces = pl.pallas_call(
         functools.partial(
             sum_kernel, count=count, groups=groups, block=block, head_dim=HEAD_DIM
@@ -588,7 +592,7 @@
             scratch(count),
         ],
         compiler_params=params,
-    )(weights, parts, value_matrix, near, *arrived_values)
+    )(weights, parts, value_matrix, near_later, *arrived_values)
     swapped = {step: swap(pieces[step], step) for step in [*far, 1]}
     pieces = [pieces[0]] + [swapped[step] for step in range(1, count)]
 

time: 25.3 us -> 25.2 us (level)
  starting transfers between devices: 12.3 us -> 11.9 us
    ppermute x2, starting transfers between devices: 3.61 us -> 3.15 us  [head_shards(): lax.ppermute(piece, 'groups', [(i, (i + shift) % groups) for i in range(g...]
    ppermute x2, waiting for transfers between devices: 0.44 us -> 0.69 us  [head_shards(): lax.ppermute(piece, 'groups', [(i, (i + shift) % groups) for i in range(g...]
    ppermute x9 -> x10, starting transfers between devices: 8.66 us -> 8.77 us  [swap(): return lax.ppermute(value, 'seq', [(i, i ^ step) for i in range(count)])]
    ppermute x9 -> x10, waiting for transfers between devices: 3.58 us -> 3.54 us  [swap(): return lax.ppermute(value, 'seq', [(i, i ^ step) for i in range(count)])]
  transfers between devices with their start and end apart: 11 -> 12, of which waited for: 5 -> 5; matrix products, arithmetic and copies ran while one was open for 0% -> 0% of each run, Pallas kernels for 25% -> 25%
where the time goes in v9:
time: 25.2 us; the launch traced here: 25 us
  starting transfers between devices  11.9 us (47%)
  Pallas kernels  8.42 us (33%)
  waiting for transfers between devices  4.23 us (17%)
  local copies, waits for them, and re-layouts  0.26 us (1%)
    ppermute x10, starting transfers between devices, swap(): return lax.ppermute(value, 'seq', [(i, i ^ step) for i in range(count)])  8.77 us
    ppermute x10, waiting for transfers between devices, swap(): return lax.ppermute(value, 'seq', [(i, i ^ step) for i in range(count)])  3.54 us
    ppermute x2, starting transfers between devices, head_shards(): lax.ppermute(piece, 'groups', [(i, (i + shift) % groups) for i in range(g...  3.15 us
    pallas_call x2, Pallas kernels, packed(): pl.pallas_call(functools.partial(pack_kernel, parts=parts, width=width),...  2.29 us
    pallas_call x3, Pallas kernels, joined(): pl.pallas_call(functools.partial(join_kernel, steps=steps, width=width),...  1.94 us
    pallas_call x2, Pallas kernels, head_shards(): pl.pallas_call(functools.partial(conv_kernel, count=count, groups=groups,...  1.69 us
    pallas_call x1, Pallas kernels, head_shards(): pl.pallas_call(functools.partial(smooth_kernel, count=count, block=block)...  1.04 us
    ppermute x2, waiting for transfers between devices, head_shards(): lax.ppermute(piece, 'groups', [(i, (i + shift) % groups) for i in range(g...  0.69 us
  transfers between devices with their start and end apart: 12, of which 5 were waited for; matrix products, arithmetic and copies ran while one was open for 0% of the time, Pallas kernels for 25%

profile of v9, /device:TPU:0, one launch (start us, length us, event | category | flops | bytes accessed | tf_op | source)
XLA Modules:
  0.0 25.0 jit_solution(17485110811954520565)
XLA Ops:
  0.0 1.1 %shard_map.91 = (bf16[640,128]{1,0:T(8,128)(2,1)S(1)}, bf16[384,256]{1,0:T(8,128)(2,1)S(1)}) custom-call(bf16[128,1024]{1,0:T(8,128)(2,1)} %rest_0_.3, bf16[128,1024]{1,0:T(8,128)(2,1)} %value_ref.1, bf16[128,1024]{1,0:T(8,128)(2,1)} %rest_2_.6, bf16[128,1024]{1,0:T(8,128)(2,1)} %own_ref.2, bf16[128,1024]{1,0:T(8,128)(2,1)} %own_ref.3), custom_call_target="tpu_custom_call" | custom-call | tf_op jit(solution)/shard_map/pallas_call | solution.py:481
  1.1 0.5 %collective-permute-start.1 = (bf16[384,256]{1,0:T(8,128)(2,1)S(1)}, bf16[384,256]{1,0:T(8,128)(2,1)S(1)}, u32[]{:S(2)}, u32[]{:S(2)}) collective-permute-start(bf16[384,256]{1,0:T(8,128)(2,1)S(1)} %get-tuple-element.25), channel_id=1, source_target_pairs={{0,4},{4,0},{8,12},{12,8},{1,5},{5,1},{9,13},{13,9},{2,6},{6,2},{1... | collective-permute-start | bytes 589832 | tf_op jit(solution)/shard_map/ppermute | solution.py:478
  1.6 2.6 %collective-permute-start = (bf16[640,128]{1,0:T(8,128)(2,1)S(1)}, bf16[640,128]{1,0:T(8,128)(2,1)S(1)}, u32[]{:S(2)}, u32[]{:S(2)}) collective-permute-start(bf16[640,128]{1,0:T(8,128)(2,1)S(1)} %get-tuple-element.24), channel_id=1, source_target_pairs={{0,8},{4,12},{8,0},{12,4},{1,9},{5,13},{9,1},{13,5},{2,10},{6,14},... | collective-permute-start | bytes 491528 | tf_op jit(solution)/shard_map/ppermute | solution.py:478
  4.2 1.2 %shard_map.93 = (bf16[256,256]{1,0:T(8,128)(2,1)S(1)}, bf16[640,128]{1,0:T(8,128)(2,1)S(1)}, bf16[256,256]{1,0:T(8,128)(2,1)S(1)}, bf16[128,256]{1,0:T(8,128)(2,1)S(1)}, bf16[128,256]{1,0:T(8,128)(2,1)S(1)}) custom-call(bf16[128,1024]{1,0:T(8,128)(2,1)} %rest_0_.3, bf16[128,1024]{1,0:T(8,128)(2,1)} %value_ref.1, bf16[128,1024]{1,0:T(8,128)(2,1)} %rest_2_.6, ...), custom_call_target="tpu_custom_call" | custom-call | tf_op jit(solution)/shard_map/pallas_call | solution.py:481
  5.4 1.1 %collective-permute-start.5 = (bf16[640,128]{1,0:T(8,128)(2,1)S(1)}, bf16[640,128]{1,0:T(8,128)(2,1)S(1)}, u32[]{:S(2)}, u32[]{:S(2)}) collective-permute-start(bf16[640,128]{1,0:T(8,128)(2,1)S(1)} %get-tuple-element.33), channel_id=1, source_target_pairs={{0,12},{4,8},{8,4},{12,0},{1,13},{5,9},{9,5},{13,1},{2,14},{6,10},... | collective-permute-start | bytes 491528 | tf_op jit(solution)/shard_map/ppermute | solution.py:478
  6.9 0.7 %collective-permute-start.3 = (bf16[256,256]{1,0:T(8,128)(2,1)S(1)}, bf16[256,256]{1,0:T(8,128)(2,1)S(1)}, u32[]{:S(2)}, u32[]{:S(2)}) collective-permute-start(bf16[256,256]{1,0:T(8,128)(2,1)S(1)} %get-tuple-element.29), channel_id=1, source_target_pairs={{0,8},{4,12},{8,0},{12,4},{1,9},{5,13},{9,1},{13,5},{2,10},{6,14},... | collective-permute-start | bytes 393224 | tf_op jit(solution)/shard_map/ppermute | solution.py:478
  7.6 0.8 %collective-permute-start.4 = (bf16[128,256]{1,0:T(8,128)(2,1)S(1)}, bf16[128,256]{1,0:T(8,128)(2,1)S(1)}, u32[]{:S(2)}, u32[]{:S(2)}) collective-permute-start(bf16[128,256]{1,0:T(8,128)(2,1)S(1)} %get-tuple-element.30), channel_id=1, source_target_pairs={{0,12},{4,8},{8,4},{12,0},{1,13},{5,9},{9,5},{13,1},{2,14},{6,10},... | collective-permute-start | bytes 196616 | tf_op jit(solution)/shard_map/ppermute | solution.py:478
  8.4 0.8 %collective-permute-done.rest_0_ = bf16[640,128]{1,0:T(8,128)(2,1)S(1)} collective-permute-done((bf16[640,128]{1,0:T(8,128)(2,1)S(1)}, bf16[640,128]{1,0:T(8,128)(2,1)S(1)}, u32[]{:S(2)}, u32[]{:S(2)}) %collective-permute-start) | collective-permute-done | bytes 163872 | tf_op jit(solution)/shard_map/ppermute | solution.py:478
  9.3 0.7 %collective-permute-start.8 = (bf16[128,256]{1,0:T(8,128)(2,1)S(1)}, bf16[128,256]{1,0:T(8,128)(2,1)S(1)}, u32[]{:S(2)}, u32[]{:S(2)}) collective-permute-start(bf16[128,256]{1,0:T(8,128)(2,1)S(1)} %get-tuple-element.38), channel_id=1, source_target_pairs={{0,12},{4,8},{8,4},{12,0},{1,13},{5,9},{9,5},{13,1},{2,14},{6,10},... | collective-permute-start | bytes 196616 | tf_op jit(solution)/shard_map/ppermute | solution.py:478
  10.0 0.4 %shard_map.92 = (f32[2,256,256]{2,1,0:T(8,128)S(1)}, f32[2,256,256]{2,1,0:T(8,128)S(1)}, f32[256,256]{1,0:T(8,128)S(1)}) custom-call(bf16[128,1024]{1,0:T(8,128)(2,1)S(1)} %copy-done.2, bf16[128,1024]{1,0:T(8,128)(2,1)S(1)} %copy-done.3, bf16[384,256]{1,0:T(8,128)(2,1)S(1)} %collective-permute-done.1.near_ref.rest_5_, f32[1024,128]{1,0:T(8,128)S(1)} %copy-done.8, ...), custom_call_target="tpu_custom_call" | custom-call | tf_op jit(solution)/shard_map/pallas_call | solution.py:520
  10.5 1.6 %collective-permute-start.6 = (bf16[128,128]{1,0:T(8,128)(2,1)S(1)}, bf16[128,128]{1,0:T(8,128)(2,1)S(1)}, u32[]{:S(2)}, u32[]{:S(2)}) collective-permute-start(bf16[128,128]{1,0:T(8,128)(2,1)S(1)} %slice.8), channel_id=1, source_target_pairs={{0,16},{16,0},{1,17},{17,1},{2,18},{18,2},{3,19},{19,3},{4,20},{20... | collective-permute-start | bytes 98312 | tf_op jit(solution)/shard_map/ppermute | solution.py:537
  12.2 1.6 %collective-permute-start.7 = (bf16[128,128]{1,0:T(8,128)(2,1)S(1)}, bf16[128,128]{1,0:T(8,128)(2,1)S(1)}, u32[]{:S(2)}, u32[]{:S(2)}) collective-permute-start(bf16[128,128]{1,0:T(8,128)(2,1)S(1)} %slice.9), channel_id=1, source_target_pairs={{0,16},{16,0},{1,17},{17,1},{2,18},{18,2},{3,19},{19,3},{4,20},{20... | collective-permute-start | bytes 98312 | tf_op jit(solution)/shard_map/ppermute | solution.py:537
  13.8 1.0 %shard_map.94.line_ref = f32[4,256,256]{2,1,0:T(8,128)S(1)} custom-call(f32[2,256,256]{2,1,0:T(8,128)S(1)} %get-tuple-element.31.gate_spec_ref, f32[256,256]{1,0:T(8,128)S(1)} %get-tuple-element.32.taps_spec_ref, bf16[128,1024]{1,0:T(8,128)(2,1)S(1)} %copy-done.4, bf16[384,256]{1,0:T(8,128)(2,1)S(1)} %collective-permute-done.1.near_ref.rest_5_, ...), custom_call_target="tpu_custom_call" | custom-call | tf_op jit(solution)/shard_map/pallas_call | solution.py:544
  14.9 0.8 %shard_map.95.rest_2_ = bf16[4,128,128]{2,1,0:T(8,128)(2,1)S(1)} custom-call(f32[4,256,256]{2,1,0:T(8,128)S(1)} %shard_map.94.line_ref, f32[2,256,256]{2,1,0:T(8,128)S(1)} %get-tuple-element.34.filter_spec_ref, bf16[640,128]{1,0:T(8,128)(2,1)S(1)} %collective-permute-done.rest_0_, bf16[640,128]{1,0:T(8,128)(2,1)S(1)} %collective-permute-done.5.rest_1_, ...), custom_call_target="tpu_custom_call" | custom-call | tf_op jit(solution)/shard_map/pallas_call | solution.py:553
  15.7 0.7 %collective-permute-done.7.rest_1_ = bf16[128,128]{1,0:T(8,128)(2,1)S(1)} collective-permute-done((bf16[128,128]{1,0:T(8,128)(2,1)S(1)}, bf16[128,128]{1,0:T(8,128)(2,1)S(1)}, u32[]{:S(2)}, u32[]{:S(2)}) %collective-permute-start.7) | collective-permute-done | bytes 32800 | tf_op jit(solution)/shard_map/ppermute | solution.py:537
  16.4 0.9 %shard_map.96.rest_3_ = bf16[4,128,128]{2,1,0:T(8,128)(2,1)S(1)} custom-call(f32[4,256,256]{2,1,0:T(8,128)S(1)} %shard_map.94.line_ref, f32[2,256,256]{2,1,0:T(8,128)S(1)} %get-tuple-element.34.filter_spec_ref, bf16[128,128]{1,0:T(8,128)(2,1)S(1)} %collective-permute-done.6.rest_0_, bf16[128,128]{1,0:T(8,128)(2,1)S(1)} %collective-permute-done.7.rest_1_, ...), custom_call_target="tpu_custom_call" | custom-call | tf_op jit(solution)/shard_map/pallas_call | solution.py:553
  17.3 0.7 %shard_map.97 = (bf16[2,4,128,512]{3,2,1,0:T(8,128)(2,1)S(1)}, f32[2,4,128,128]{3,2,1,0:T(8,128)S(1)}) custom-call(bf16[128,1024]{1,0:T(8,128)(2,1)S(1)} %copy-done.1, bf16[256,256]{1,0:T(8,128)(2,1)S(1)} %collective-permute-done.2.near_ref, bf16[256,256]{1,0:T(8,128)(2,1)S(1)} %collective-permute-done.3.rest_0_, ...), custom_call_target="tpu_custom_call" | custom-call | tf_op jit(solution)/shard_map/pallas_call | solution.py:570
  18.2 0.4 %shard_map.98 = (bf16[128,256]{1,0:T(8,128)(2,1)S(1)}, bf16[128,256]{1,0:T(8,128)(2,1)S(1)}, bf16[128,256]{1,0:T(8,128)(2,1)S(1)}, bf16[128,256]{1,0:T(8,128)(2,1)S(1)}) custom-call(bf16[2,4,128,512]{3,2,1,0:T(8,128)(2,1)S(1)} %get-tuple-element.36.weight_ref, f32[2,4,128,128]{3,2,1,0:T(8,128)S(1)} %get-tuple-element.37.part_ref, ...), custom_call_target="tpu_custom_call" | custom-call | tf_op jit(solution)/shard_map/pallas_call | solution.py:583
  18.7 1.6 %collective-permute-start.10 = (bf16[128,256]{1,0:T(8,128)(2,1)S(1)}, bf16[128,256]{1,0:T(8,128)(2,1)S(1)}, u32[]{:S(2)}, u32[]{:S(2)}) collective-permute-start(bf16[128,256]{1,0:T(8,128)(2,1)S(1)} %get-tuple-element.40), channel_id=1, source_target_pairs={{0,8},{4,12},{8,0},{12,4},{1,9},{5,13},{9,1},{13,5},{2,10},{6,14},... | collective-permute-start | bytes 196616 | tf_op jit(solution)/shard_map/ppermute | solution.py:478
  20.6 0.7 %shard_map.99.rest_1_ = bf16[128,1024]{1,0:T(8,128)(2,1)} custom-call(bf16[128,256]{1,0:T(8,128)(2,1)S(1)} %get-tuple-element.41.rest_0_, bf16[128,256]{1,0:T(8,128)(2,1)S(1)} %collective-permute-done.11.rest_1_), custom_call_target="tpu_custom_call" | custom-call | tf_op jit(solution)/shard_map/pallas_call | solution.py:600
  21.2 2.0 %collective-permute-done.10.rest_0_ = bf16[128,256]{1,0:T(8,128)(2,1)S(1)} collective-permute-done((bf16[128,256]{1,0:T(8,128)(2,1)S(1)}, bf16[128,256]{1,0:T(8,128)(2,1)S(1)}, u32[]{:S(2)}, u32[]{:S(2)}) %collective-permute-start.10) | collective-permute-done | bytes 65568 | tf_op jit(solution)/shard_map/ppermute | solution.py:478
  23.2 0.6 %shard_map.100.rest_1_ = bf16[128,1024]{1,0:T(8,128)(2,1)} custom-call(bf16[128,256]{1,0:T(8,128)(2,1)S(1)} %collective-permute-done.10.rest_0_, bf16[128,1024]{1,0:T(8,128)(2,1)} %shard_map.99.rest_1_), custom_call_target="tpu_custom_call", output_to_operand_aliasing={{}: (1, {})} | custom-call | tf_op jit(solution)/shard_map/pallas_call | solution.py:600
  23.8 0.5 %collective-permute-done.9.rest_0_ = bf16[128,256]{1,0:T(8,128)(2,1)S(1)} collective-permute-done((bf16[128,256]{1,0:T(8,128)(2,1)S(1)}, bf16[128,256]{1,0:T(8,128)(2,1)S(1)}, u32[]{:S(2)}, u32[]{:S(2)}) %collective-permute-start.9) | collective-permute-done | bytes 65568 | tf_op jit(solution)/shard_map/ppermute | solution.py:478
  24.4 0.6 %shard_map.101 = bf16[128,1024]{1,0:T(8,128)(2,1)} custom-call(bf16[128,256]{1,0:T(8,128)(2,1)S(1)} %collective-permute-done.9.rest_0_, bf16[128,1024]{1,0:T(8,128)(2,1)} %shard_map.100.rest_1_), custom_call_target="tpu_custom_call", output_to_operand_aliasing={{}: (1, {})} | custom-call | tf_op jit(solution)/shard_map/pallas_call | solution.py:600
  (31 shorter events, 1.2 us)
Async XLA Ops:
  1.1 3.1 %collective-permute-start.1 = (bf16[384,256]{1,0:T(8,128)(2,1)S(1)}, bf16[384,256]{1,0:T(8,128)(2,1)S(1)}, u32[]{:S(2)}, u32[]{:S(2)}) collective-permute-start(bf16[384,256]{1,0:T(8,128)(2,1)S(1)} %get-tuple-element.25), channel_id=1, source_target_pairs={{0,4},{4,0},{8,12},{12,8},{1,5},{5,1},{9,13},{13,9},{2,6},{6,2},{1... | collective-permute-start | bytes 589832 | tf_op jit(solution)/shard_map/ppermute | solution.py:478
  1.6 8.4 %copy-start.2 = (bf16[128,1024]{1,0:T(8,128)(2,1)S(1)}, bf16[128,1024]{1,0:T(8,128)(2,1)}, u32[]{:S(2)}) copy-start(bf16[128,1024]{1,0:T(8,128)(2,1)} %rest_0_.3) | copy-start | bytes 786436
  1.6 8.4 %copy-start.3 = (bf16[128,1024]{1,0:T(8,128)(2,1)S(1)}, bf16[128,1024]{1,0:T(8,128)(2,1)}, u32[]{:S(2)}) copy-start(bf16[128,1024]{1,0:T(8,128)(2,1)} %rest_2_.6) | copy-start | bytes 786436
  1.6 8.4 %copy-start.8 = (f32[1024,128]{1,0:T(8,128)S(1)}, f32[1024,128]{1,0:T(8,128)}, u32[]{:S(2)}) copy-start(f32[1024,128]{1,0:T(8,128)} %taps_ref.1) | copy-start | bytes 1572868
  1.6 7.7 %collective-permute-start = (bf16[640,128]{1,0:T(8,128)(2,1)S(1)}, bf16[640,128]{1,0:T(8,128)(2,1)S(1)}, u32[]{:S(2)}, u32[]{:S(2)}) collective-permute-start(bf16[640,128]{1,0:T(8,128)(2,1)S(1)} %get-tuple-element.24), channel_id=1, source_target_pairs={{0,8},{4,12},{8,0},{12,4},{1,9},{5,13},{9,1},{13,5},{2,10},{6,14},... | collective-permute-start | bytes 491528 | tf_op jit(solution)/shard_map/ppermute | solution.py:478
  4.2 5.8 %copy-start.5 = (bf16[512,128]{1,0:T(8,128)(2,1)S(1)}, bf16[512,128]{1,0:T(8,128)(2,1)}, u32[]{:S(2)}) copy-start(bf16[512,128]{1,0:T(8,128)(2,1)} %constant.4.clone.ahead_ref.rest_2_.rest_3_) | copy-start | bytes 393220
  5.4 6.8 %collective-permute-start.5 = (bf16[640,128]{1,0:T(8,128)(2,1)S(1)}, bf16[640,128]{1,0:T(8,128)(2,1)S(1)}, u32[]{:S(2)}, u32[]{:S(2)}) collective-permute-start(bf16[640,128]{1,0:T(8,128)(2,1)S(1)} %get-tuple-element.33), channel_id=1, source_target_pairs={{0,12},{4,8},{8,4},{12,0},{1,13},{5,9},{9,5},{13,1},{2,14},{6,10},... | collective-permute-start | bytes 491528 | tf_op jit(solution)/shard_map/ppermute | solution.py:478
  6.6 3.9 %collective-permute-start.2 = (bf16[256,256]{1,0:T(8,128)(2,1)S(1)}, bf16[256,256]{1,0:T(8,128)(2,1)S(1)}, u32[]{:S(2)}, u32[]{:S(2)}) collective-permute-start(bf16[256,256]{1,0:T(8,128)(2,1)S(1)} %get-tuple-element.27), channel_id=1, source_target_pairs={{0,4},{4,0},{8,12},{12,8},{1,5},{5,1},{9,13},{13,9},{2,6},{6,2},{1... | collective-permute-start | bytes 393224 | tf_op jit(solution)/shard_map/ppermute | solution.py:478
  6.9 10.4 %collective-permute-start.3 = (bf16[256,256]{1,0:T(8,128)(2,1)S(1)}, bf16[256,256]{1,0:T(8,128)(2,1)S(1)}, u32[]{:S(2)}, u32[]{:S(2)}) collective-permute-start(bf16[256,256]{1,0:T(8,128)(2,1)S(1)} %get-tuple-element.29), channel_id=1, source_target_pairs={{0,8},{4,12},{8,0},{12,4},{1,9},{5,13},{9,1},{13,5},{2,10},{6,14},... | collective-permute-start | bytes 393224 | tf_op jit(solution)/shard_map/ppermute | solution.py:478
  7.6 9.7 %collective-permute-start.4 = (bf16[128,256]{1,0:T(8,128)(2,1)S(1)}, bf16[128,256]{1,0:T(8,128)(2,1)S(1)}, u32[]{:S(2)}, u32[]{:S(2)}) collective-permute-start(bf16[128,256]{1,0:T(8,128)(2,1)S(1)} %get-tuple-element.30), channel_id=1, source_target_pairs={{0,12},{4,8},{8,4},{12,0},{1,13},{5,9},{9,5},{13,1},{2,14},{6,10},... | collective-permute-start | bytes 196616 | tf_op jit(solution)/shard_map/ppermute | solution.py:478
  9.3 8.8 %collective-permute-start.8 = (bf16[128,256]{1,0:T(8,128)(2,1)S(1)}, bf16[128,256]{1,0:T(8,128)(2,1)S(1)}, u32[]{:S(2)}, u32[]{:S(2)}) collective-permute-start(bf16[128,256]{1,0:T(8,128)(2,1)S(1)} %get-tuple-element.38), channel_id=1, source_target_pairs={{0,12},{4,8},{8,4},{12,0},{1,13},{5,9},{9,5},{13,1},{2,14},{6,10},... | collective-permute-start | bytes 196616 | tf_op jit(solution)/shard_map/ppermute | solution.py:478
  10.0 3.8 %copy-start.4 = (bf16[128,1024]{1,0:T(8,128)(2,1)S(1)}, bf16[128,1024]{1,0:T(8,128)(2,1)}, u32[]{:S(2)}) copy-start(bf16[128,1024]{1,0:T(8,128)(2,1)} %value_ref.1) | copy-start | bytes 786436
  10.0 3.8 %copy-start.6 = (bf16[256,256]{1,0:T(8,128)(2,1)S(1)}, bf16[256,256]{1,0:T(8,128)(2,1)}, u32[]{:S(2)}) copy-start(bf16[256,256]{1,0:T(8,128)(2,1)} %constant.5.clone.rest_3_.rest_4_) | copy-start | bytes 393220
  10.5 5.3 %collective-permute-start.6 = (bf16[128,128]{1,0:T(8,128)(2,1)S(1)}, bf16[128,128]{1,0:T(8,128)(2,1)S(1)}, u32[]{:S(2)}, u32[]{:S(2)}) collective-permute-start(bf16[128,128]{1,0:T(8,128)(2,1)S(1)} %slice.8), channel_id=1, source_target_pairs={{0,16},{16,0},{1,17},{17,1},{2,18},{18,2},{3,19},{19,3},{4,20},{20... | collective-permute-start | bytes 98312 | tf_op jit(solution)/shard_map/ppermute | solution.py:537
  12.2 4.2 %collective-permute-start.7 = (bf16[128,128]{1,0:T(8,128)(2,1)S(1)}, bf16[128,128]{1,0:T(8,128)(2,1)S(1)}, u32[]{:S(2)}, u32[]{:S(2)}) collective-permute-start(bf16[128,128]{1,0:T(8,128)(2,1)S(1)} %slice.9), channel_id=1, source_target_pairs={{0,16},{16,0},{1,17},{17,1},{2,18},{18,2},{3,19},{19,3},{4,20},{20... | collective-permute-start | bytes 98312 | tf_op jit(solution)/shard_map/ppermute | solution.py:537
  13.8 1.0 %copy-start.7 = (bf16[8,128,128]{2,1,0:T(8,128)(2,1)S(1)}, bf16[8,128,128]{2,1,0:T(8,128)(2,1)}, u32[]{:S(2)}) copy-start(bf16[8,128,128]{2,1,0:T(8,128)(2,1)} %rest_2_.8) | copy-start | bytes 786436
  15.7 1.6 %copy-start.1 = (bf16[128,1024]{1,0:T(8,128)(2,1)S(1)}, bf16[128,1024]{1,0:T(8,128)(2,1)}, u32[]{:S(2)}) copy-start(bf16[128,1024]{1,0:T(8,128)(2,1)} %own_ref.2) | copy-start | bytes 786436
  17.3 1.0 %copy-start = (bf16[128,1024]{1,0:T(8,128)(2,1)S(1)}, bf16[128,1024]{1,0:T(8,128)(2,1)}, u32[]{:S(2)}) copy-start(bf16[128,1024]{1,0:T(8,128)(2,1)} %own_ref.3) | copy-start | bytes 786436
  18.6 1.9 %collective-permute-start.11 = (bf16[128,256]{1,0:T(8,128)(2,1)S(1)}, bf16[128,256]{1,0:T(8,128)(2,1)S(1)}, u32[]{:S(2)}, u32[]{:S(2)}) collective-permute-start(bf16[128,256]{1,0:T(8,128)(2,1)S(1)} %get-tuple-element.42), channel_id=1, source_target_pairs={{0,4},{4,0},{8,12},{12,8},{1,5},{5,1},{9,13},{13,9},{2,6},{6,2},{1... | collective-permute-start | bytes 196616 | tf_op jit(solution)/shard_map/ppermute | solution.py:478
  18.7 4.5 %collective-permute-start.10 = (bf16[128,256]{1,0:T(8,128)(2,1)S(1)}, bf16[128,256]{1,0:T(8,128)(2,1)S(1)}, u32[]{:S(2)}, u32[]{:S(2)}) collective-permute-start(bf16[128,256]{1,0:T(8,128)(2,1)S(1)} %get-tuple-element.40), channel_id=1, source_target_pairs={{0,8},{4,12},{8,0},{12,4},{1,9},{5,13},{9,1},{13,5},{2,10},{6,14},... | collective-permute-start | bytes 196616 | tf_op jit(solution)/shard_map/ppermute | solution.py:478
  20.2 4.1 %collective-permute-start.9 = (bf16[128,256]{1,0:T(8,128)(2,1)S(1)}, bf16[128,256]{1,0:T(8,128)(2,1)S(1)}, u32[]{:S(2)}, u32[]{:S(2)}) collective-permute-start(bf16[128,256]{1,0:T(8,128)(2,1)S(1)} %get-tuple-element.39), channel_id=1, source_target_pairs={{0,12},{4,8},{8,4},{12,0},{1,13},{5,9},{9,5},{13,1},{2,14},{6,10},... | collective-permute-start | bytes 196616 | tf_op jit(solution)/shard_map/ppermute | solution.py:478

commit v10 on v9

--- a/solution.py
+++ b/solution.py
@@ -325,8 +325,12 @@
         (smoothed * value_all[b].astype(jnp.float32)).astype(jnp.bfloat16)
         for b, smoothed in enumerate(to_blocks(back, spectra, block))
     ]
-    for b in range(count):
-        line_ref[b] = wide_mxu(ahead, mixed[b])
+    lines = [wide_mxu(ahead, part) for part in mixed]
+    line_ref[0] = lines[0]
+    for b in range(1, count):
+        window_re, window_im = with_block_before(lines[b], lines[b - 1], block)
+        line_ref[b, :block] = window_re
+        line_ref[b, block:] = window_im
 
 
 def share_start(shift, columns, groups):
@@ -351,9 +355,7 @@
     for step, piece in enumerate(arrived, 2):
         spec_all[here ^ step] = wide_mxu(ahead, piece[piece.shape[0] - block :])
     lines = [(line_ref[b, :block, chosen], line_ref[b, block:, chosen]) for b in range(count)]
-    kernels = [(spec_all[0, :block], spec_all[0, block:])] + [
-        with_block_before(spec_all[b], spec_all[b - 1], block) for b in range(1, count)
-    ]
+    kernels = [(spec_all[b, :block], spec_all[b, block:]) for b in range(count)]
     totals = []
     for b in range(count):
         total_re, total_im = 0.0, 0.0

time: 25.2 us -> 25.2 us (level)
  no operation moved by 1% of the time
where the time goes in v10:
time: 25.2 us; the launch traced here: 25 us
  starting transfers between devices  11.9 us (47%)
  Pallas kernels  8.41 us (33%)
  waiting for transfers between devices  4.23 us (17%)
  local copies, waits for them, and re-layouts  0.26 us (1%)
    ppermute x10, starting transfers between devices, swap(): return lax.ppermute(value, 'seq', [(i, i ^ step) for i in range(count)])  8.77 us
    ppermute x10, waiting for transfers between devices, swap(): return lax.ppermute(value, 'seq', [(i, i ^ step) for i in range(count)])  3.54 us
    ppermute x2, starting transfers between devices, head_shards(): lax.ppermute(piece, 'groups', [(i, (i + shift) % groups) for i in range(g...  3.15 us
    pallas_call x2, Pallas kernels, packed(): pl.pallas_call(functools.partial(pack_kernel, parts=parts, width=width),...  2.29 us
    pallas_call x3, Pallas kernels, joined(): pl.pallas_call(functools.partial(join_kernel, steps=steps, width=width),...  1.94 us
    pallas_call x2, Pallas kernels, head_shards(): pl.pallas_call(functools.partial(conv_kernel, count=count, groups=groups,...  1.68 us
    pallas_call x1, Pallas kernels, head_shards(): pl.pallas_call(functools.partial(smooth_kernel, count=count, block=block)...  1.04 us
    ppermute x2, waiting for transfers between devices, head_shards(): lax.ppermute(piece, 'groups', [(i, (i + shift) % groups) for i in range(g...  0.69 us
  transfers between devices with their start and end apart: 12, of which 5 were waited for; matrix products, arithmetic and copies ran while one was open for 0% of the time, Pallas kernels for 25%

profile of v10, /device:TPU:0, one launch (start us, length us, event | category | flops | bytes accessed | tf_op | source)
XLA Modules:
  0.0 25.0 jit_solution(3739057528150486393)
XLA Ops:
  0.0 1.1 %shard_map.91 = (bf16[640,128]{1,0:T(8,128)(2,1)S(1)}, bf16[384,256]{1,0:T(8,128)(2,1)S(1)}) custom-call(bf16[128,1024]{1,0:T(8,128)(2,1)} %rest_0_.3, bf16[128,1024]{1,0:T(8,128)(2,1)} %value_ref.1, bf16[128,1024]{1,0:T(8,128)(2,1)} %rest_2_.6, bf16[128,1024]{1,0:T(8,128)(2,1)} %own_ref.2, bf16[128,1024]{1,0:T(8,128)(2,1)} %own_ref.3), custom_call_target="tpu_custom_call" | custom-call | tf_op jit(solution)/shard_map/pallas_call | solution.py:483
  1.1 0.5 %collective-permute-start.1 = (bf16[384,256]{1,0:T(8,128)(2,1)S(1)}, bf16[384,256]{1,0:T(8,128)(2,1)S(1)}, u32[]{:S(2)}, u32[]{:S(2)}) collective-permute-start(bf16[384,256]{1,0:T(8,128)(2,1)S(1)} %get-tuple-element.25), channel_id=1, source_target_pairs={{0,4},{4,0},{8,12},{12,8},{1,5},{5,1},{9,13},{13,9},{2,6},{6,2},{1... | collective-permute-start | bytes 589832 | tf_op jit(solution)/shard_map/ppermute | solution.py:480
  1.6 2.6 %collective-permute-start = (bf16[640,128]{1,0:T(8,128)(2,1)S(1)}, bf16[640,128]{1,0:T(8,128)(2,1)S(1)}, u32[]{:S(2)}, u32[]{:S(2)}) collective-permute-start(bf16[640,128]{1,0:T(8,128)(2,1)S(1)} %get-tuple-element.24), channel_id=1, source_target_pairs={{0,8},{4,12},{8,0},{12,4},{1,9},{5,13},{9,1},{13,5},{2,10},{6,14},... | collective-permute-start | bytes 491528 | tf_op jit(solution)/shard_map/ppermute | solution.py:480
  4.2 1.2 %shard_map.93 = (bf16[256,256]{1,0:T(8,128)(2,1)S(1)}, bf16[640,128]{1,0:T(8,128)(2,1)S(1)}, bf16[256,256]{1,0:T(8,128)(2,1)S(1)}, bf16[128,256]{1,0:T(8,128)(2,1)S(1)}, bf16[128,256]{1,0:T(8,128)(2,1)S(1)}) custom-call(bf16[128,1024]{1,0:T(8,128)(2,1)} %rest_0_.3, bf16[128,1024]{1,0:T(8,128)(2,1)} %value_ref.1, bf16[128,1024]{1,0:T(8,128)(2,1)} %rest_2_.6, ...), custom_call_target="tpu_custom_call" | custom-call | tf_op jit(solution)/shard_map/pallas_call | solution.py:483
  5.4 1.1 %collective-permute-start.5 = (bf16[640,128]{1,0:T(8,128)(2,1)S(1)}, bf16[640,128]{1,0:T(8,128)(2,1)S(1)}, u32[]{:S(2)}, u32[]{:S(2)}) collective-permute-start(bf16[640,128]{1,0:T(8,128)(2,1)S(1)} %get-tuple-element.33), channel_id=1, source_target_pairs={{0,12},{4,8},{8,4},{12,0},{1,13},{5,9},{9,5},{13,1},{2,14},{6,10},... | collective-permute-start | bytes 491528 | tf_op jit(solution)/shard_map/ppermute | solution.py:480
  6.9 0.7 %collective-permute-start.3 = (bf16[256,256]{1,0:T(8,128)(2,1)S(1)}, bf16[256,256]{1,0:T(8,128)(2,1)S(1)}, u32[]{:S(2)}, u32[]{:S(2)}) collective-permute-start(bf16[256,256]{1,0:T(8,128)(2,1)S(1)} %get-tuple-element.29), channel_id=1, source_target_pairs={{0,8},{4,12},{8,0},{12,4},{1,9},{5,13},{9,1},{13,5},{2,10},{6,14},... | collective-permute-start | bytes 393224 | tf_op jit(solution)/shard_map/ppermute | solution.py:480
  7.6 0.8 %collective-permute-start.4 = (bf16[128,256]{1,0:T(8,128)(2,1)S(1)}, bf16[128,256]{1,0:T(8,128)(2,1)S(1)}, u32[]{:S(2)}, u32[]{:S(2)}) collective-permute-start(bf16[128,256]{1,0:T(8,128)(2,1)S(1)} %get-tuple-element.30), channel_id=1, source_target_pairs={{0,12},{4,8},{8,4},{12,0},{1,13},{5,9},{9,5},{13,1},{2,14},{6,10},... | collective-permute-start | bytes 196616 | tf_op jit(solution)/shard_map/ppermute | solution.py:480
  8.4 0.8 %collective-permute-done.rest_0_ = bf16[640,128]{1,0:T(8,128)(2,1)S(1)} collective-permute-done((bf16[640,128]{1,0:T(8,128)(2,1)S(1)}, bf16[640,128]{1,0:T(8,128)(2,1)S(1)}, u32[]{:S(2)}, u32[]{:S(2)}) %collective-permute-start) | collective-permute-done | bytes 163872 | tf_op jit(solution)/shard_map/ppermute | solution.py:480
  9.3 0.7 %collective-permute-start.8 = (bf16[128,256]{1,0:T(8,128)(2,1)S(1)}, bf16[128,256]{1,0:T(8,128)(2,1)S(1)}, u32[]{:S(2)}, u32[]{:S(2)}) collective-permute-start(bf16[128,256]{1,0:T(8,128)(2,1)S(1)} %get-tuple-element.38), channel_id=1, source_target_pairs={{0,12},{4,8},{8,4},{12,0},{1,13},{5,9},{9,5},{13,1},{2,14},{6,10},... | collective-permute-start | bytes 196616 | tf_op jit(solution)/shard_map/ppermute | solution.py:480
  10.0 0.4 %shard_map.92 = (f32[2,256,256]{2,1,0:T(8,128)S(1)}, f32[2,256,256]{2,1,0:T(8,128)S(1)}, f32[256,256]{1,0:T(8,128)S(1)}) custom-call(bf16[128,1024]{1,0:T(8,128)(2,1)S(1)} %copy-done.2, bf16[128,1024]{1,0:T(8,128)(2,1)S(1)} %copy-done.3, bf16[384,256]{1,0:T(8,128)(2,1)S(1)} %collective-permute-done.1.near_ref.rest_5_, f32[1024,128]{1,0:T(8,128)S(1)} %copy-done.8, ...), custom_call_target="tpu_custom_call" | custom-call | tf_op jit(solution)/shard_map/pallas_call | solution.py:522
  10.5 1.6 %collective-permute-start.6 = (bf16[128,128]{1,0:T(8,128)(2,1)S(1)}, bf16[128,128]{1,0:T(8,128)(2,1)S(1)}, u32[]{:S(2)}, u32[]{:S(2)}) collective-permute-start(bf16[128,128]{1,0:T(8,128)(2,1)S(1)} %slice.8), channel_id=1, source_target_pairs={{0,16},{16,0},{1,17},{17,1},{2,18},{18,2},{3,19},{19,3},{4,20},{20... | collective-permute-start | bytes 98312 | tf_op jit(solution)/shard_map/ppermute | solution.py:539
  12.2 1.6 %collective-permute-start.7 = (bf16[128,128]{1,0:T(8,128)(2,1)S(1)}, bf16[128,128]{1,0:T(8,128)(2,1)S(1)}, u32[]{:S(2)}, u32[]{:S(2)}) collective-permute-start(bf16[128,128]{1,0:T(8,128)(2,1)S(1)} %slice.9), channel_id=1, source_target_pairs={{0,16},{16,0},{1,17},{17,1},{2,18},{18,2},{3,19},{19,3},{4,20},{20... | collective-permute-start | bytes 98312 | tf_op jit(solution)/shard_map/ppermute | solution.py:539
  13.8 1.0 %shard_map.94.line_ref = f32[4,256,256]{2,1,0:T(8,128)S(1)} custom-call(f32[2,256,256]{2,1,0:T(8,128)S(1)} %get-tuple-element.31.gate_spec_ref, f32[256,256]{1,0:T(8,128)S(1)} %get-tuple-element.32.taps_spec_ref, bf16[128,1024]{1,0:T(8,128)(2,1)S(1)} %copy-done.4, bf16[384,256]{1,0:T(8,128)(2,1)S(1)} %collective-permute-done.1.near_ref.rest_5_, ...), custom_call_target="tpu_custom_call" | custom-call | tf_op jit(solution)/shard_map/pallas_call | solution.py:546
  14.9 0.8 %shard_map.95.rest_2_ = bf16[4,128,128]{2,1,0:T(8,128)(2,1)S(1)} custom-call(f32[4,256,256]{2,1,0:T(8,128)S(1)} %shard_map.94.line_ref, f32[2,256,256]{2,1,0:T(8,128)S(1)} %get-tuple-element.34.filter_spec_ref, bf16[640,128]{1,0:T(8,128)(2,1)S(1)} %collective-permute-done.rest_0_, bf16[640,128]{1,0:T(8,128)(2,1)S(1)} %collective-permute-done.5.rest_1_, ...), custom_call_target="tpu_custom_call" | custom-call | tf_op jit(solution)/shard_map/pallas_call | solution.py:555
  15.7 0.7 %collective-permute-done.7.rest_1_ = bf16[128,128]{1,0:T(8,128)(2,1)S(1)} collective-permute-done((bf16[128,128]{1,0:T(8,128)(2,1)S(1)}, bf16[128,128]{1,0:T(8,128)(2,1)S(1)}, u32[]{:S(2)}, u32[]{:S(2)}) %collective-permute-start.7) | collective-permute-done | bytes 32800 | tf_op jit(solution)/shard_map/ppermute | solution.py:539
  16.4 0.8 %shard_map.96.rest_3_ = bf16[4,128,128]{2,1,0:T(8,128)(2,1)S(1)} custom-call(f32[4,256,256]{2,1,0:T(8,128)S(1)} %shard_map.94.line_ref, f32[2,256,256]{2,1,0:T(8,128)S(1)} %get-tuple-element.34.filter_spec_ref, bf16[128,128]{1,0:T(8,128)(2,1)S(1)} %collective-permute-done.6.rest_0_, bf16[128,128]{1,0:T(8,128)(2,1)S(1)} %collective-permute-done.7.rest_1_, ...), custom_call_target="tpu_custom_call" | custom-call | tf_op jit(solution)/shard_map/pallas_call | solution.py:555
  17.3 0.7 %shard_map.97 = (bf16[2,4,128,512]{3,2,1,0:T(8,128)(2,1)S(1)}, f32[2,4,128,128]{3,2,1,0:T(8,128)S(1)}) custom-call(bf16[128,1024]{1,0:T(8,128)(2,1)S(1)} %copy-done.1, bf16[256,256]{1,0:T(8,128)(2,1)S(1)} %collective-permute-done.2.near_ref, bf16[256,256]{1,0:T(8,128)(2,1)S(1)} %collective-permute-done.3.rest_0_, ...), custom_call_target="tpu_custom_call" | custom-call | tf_op jit(solution)/shard_map/pallas_call | solution.py:572
  18.2 0.4 %shard_map.98 = (bf16[128,256]{1,0:T(8,128)(2,1)S(1)}, bf16[128,256]{1,0:T(8,128)(2,1)S(1)}, bf16[128,256]{1,0:T(8,128)(2,1)S(1)}, bf16[128,256]{1,0:T(8,128)(2,1)S(1)}) custom-call(bf16[2,4,128,512]{3,2,1,0:T(8,128)(2,1)S(1)} %get-tuple-element.36.weight_ref, f32[2,4,128,128]{3,2,1,0:T(8,128)S(1)} %get-tuple-element.37.part_ref, ...), custom_call_target="tpu_custom_call" | custom-call | tf_op jit(solution)/shard_map/pallas_call | solution.py:585
  18.7 1.5 %collective-permute-start.10 = (bf16[128,256]{1,0:T(8,128)(2,1)S(1)}, bf16[128,256]{1,0:T(8,128)(2,1)S(1)}, u32[]{:S(2)}, u32[]{:S(2)}) collective-permute-start(bf16[128,256]{1,0:T(8,128)(2,1)S(1)} %get-tuple-element.40), channel_id=1, source_target_pairs={{0,8},{4,12},{8,0},{12,4},{1,9},{5,13},{9,1},{13,5},{2,10},{6,14},... | collective-permute-start | bytes 196616 | tf_op jit(solution)/shard_map/ppermute | solution.py:480
  20.5 0.7 %shard_map.99.rest_1_ = bf16[128,1024]{1,0:T(8,128)(2,1)} custom-call(bf16[128,256]{1,0:T(8,128)(2,1)S(1)} %get-tuple-element.41.rest_0_, bf16[128,256]{1,0:T(8,128)(2,1)S(1)} %collective-permute-done.11.rest_1_), custom_call_target="tpu_custom_call" | custom-call | tf_op jit(solution)/shard_map/pallas_call | solution.py:602
  21.2 2.0 %collective-permute-done.10.rest_0_ = bf16[128,256]{1,0:T(8,128)(2,1)S(1)} collective-permute-done((bf16[128,256]{1,0:T(8,128)(2,1)S(1)}, bf16[128,256]{1,0:T(8,128)(2,1)S(1)}, u32[]{:S(2)}, u32[]{:S(2)}) %collective-permute-start.10) | collective-permute-done | bytes 65568 | tf_op jit(solution)/shard_map/ppermute | solution.py:480
  23.2 0.6 %shard_map.100.rest_1_ = bf16[128,1024]{1,0:T(8,128)(2,1)} custom-call(bf16[128,256]{1,0:T(8,128)(2,1)S(1)} %collective-permute-done.10.rest_0_, bf16[128,1024]{1,0:T(8,128)(2,1)} %shard_map.99.rest_1_), custom_call_target="tpu_custom_call", output_to_operand_aliasing={{}: (1, {})} | custom-call | tf_op jit(solution)/shard_map/pallas_call | solution.py:602
  23.8 0.5 %collective-permute-done.9.rest_0_ = bf16[128,256]{1,0:T(8,128)(2,1)S(1)} collective-permute-done((bf16[128,256]{1,0:T(8,128)(2,1)S(1)}, bf16[128,256]{1,0:T(8,128)(2,1)S(1)}, u32[]{:S(2)}, u32[]{:S(2)}) %collective-permute-start.9) | collective-permute-done | bytes 65568 | tf_op jit(solution)/shard_map/ppermute | solution.py:480
  24.4 0.6 %shard_map.101 = bf16[128,1024]{1,0:T(8,128)(2,1)} custom-call(bf16[128,256]{1,0:T(8,128)(2,1)S(1)} %collective-permute-done.9.rest_0_, bf16[128,1024]{1,0:T(8,128)(2,1)} %shard_map.100.rest_1_), custom_call_target="tpu_custom_call", output_to_operand_aliasing={{}: (1, {})} | custom-call | tf_op jit(solution)/shard_map/pallas_call | solution.py:602
  (31 shorter events, 1.2 us)
Async XLA Ops:
  1.1 3.1 %collective-permute-start.1 = (bf16[384,256]{1,0:T(8,128)(2,1)S(1)}, bf16[384,256]{1,0:T(8,128)(2,1)S(1)}, u32[]{:S(2)}, u32[]{:S(2)}) collective-permute-start(bf16[384,256]{1,0:T(8,128)(2,1)S(1)} %get-tuple-element.25), channel_id=1, source_target_pairs={{0,4},{4,0},{8,12},{12,8},{1,5},{5,1},{9,13},{13,9},{2,6},{6,2},{1... | collective-permute-start | bytes 589832 | tf_op jit(solution)/shard_map/ppermute | solution.py:480
  1.6 8.4 %copy-start.2 = (bf16[128,1024]{1,0:T(8,128)(2,1)S(1)}, bf16[128,1024]{1,0:T(8,128)(2,1)}, u32[]{:S(2)}) copy-start(bf16[128,1024]{1,0:T(8,128)(2,1)} %rest_0_.3) | copy-start | bytes 786436
  1.6 8.4 %copy-start.3 = (bf16[128,1024]{1,0:T(8,128)(2,1)S(1)}, bf16[128,1024]{1,0:T(8,128)(2,1)}, u32[]{:S(2)}) copy-start(bf16[128,1024]{1,0:T(8,128)(2,1)} %rest_2_.6) | copy-start | bytes 786436
  1.6 8.4 %copy-start.8 = (f32[1024,128]{1,0:T(8,128)S(1)}, f32[1024,128]{1,0:T(8,128)}, u32[]{:S(2)}) copy-start(f32[1024,128]{1,0:T(8,128)} %taps_ref.1) | copy-start | bytes 1572868
  1.6 7.7 %collective-permute-start = (bf16[640,128]{1,0:T(8,128)(2,1)S(1)}, bf16[640,128]{1,0:T(8,128)(2,1)S(1)}, u32[]{:S(2)}, u32[]{:S(2)}) collective-permute-start(bf16[640,128]{1,0:T(8,128)(2,1)S(1)} %get-tuple-element.24), channel_id=1, source_target_pairs={{0,8},{4,12},{8,0},{12,4},{1,9},{5,13},{9,1},{13,5},{2,10},{6,14},... | collective-permute-start | bytes 491528 | tf_op jit(solution)/shard_map/ppermute | solution.py:480
  4.2 5.8 %copy-start.5 = (bf16[512,128]{1,0:T(8,128)(2,1)S(1)}, bf16[512,128]{1,0:T(8,128)(2,1)}, u32[]{:S(2)}) copy-start(bf16[512,128]{1,0:T(8,128)(2,1)} %constant.4.clone.ahead_ref.rest_2_.rest_3_) | copy-start | bytes 393220
  5.4 6.8 %collective-permute-start.5 = (bf16[640,128]{1,0:T(8,128)(2,1)S(1)}, bf16[640,128]{1,0:T(8,128)(2,1)S(1)}, u32[]{:S(2)}, u32[]{:S(2)}) collective-permute-start(bf16[640,128]{1,0:T(8,128)(2,1)S(1)} %get-tuple-element.33), channel_id=1, source_target_pairs={{0,12},{4,8},{8,4},{12,0},{1,13},{5,9},{9,5},{13,1},{2,14},{6,10},... | collective-permute-start | bytes 491528 | tf_op jit(solution)/shard_map/ppermute | solution.py:480
  6.6 3.9 %collective-permute-start.2 = (bf16[256,256]{1,0:T(8,128)(2,1)S(1)}, bf16[256,256]{1,0:T(8,128)(2,1)S(1)}, u32[]{:S(2)}, u32[]{:S(2)}) collective-permute-start(bf16[256,256]{1,0:T(8,128)(2,1)S(1)} %get-tuple-element.27), channel_id=1, source_target_pairs={{0,4},{4,0},{8,12},{12,8},{1,5},{5,1},{9,13},{13,9},{2,6},{6,2},{1... | collective-permute-start | bytes 393224 | tf_op jit(solution)/shard_map/ppermute | solution.py:480
  6.9 10.4 %collective-permute-start.3 = (bf16[256,256]{1,0:T(8,128)(2,1)S(1)}, bf16[256,256]{1,0:T(8,128)(2,1)S(1)}, u32[]{:S(2)}, u32[]{:S(2)}) collective-permute-start(bf16[256,256]{1,0:T(8,128)(2,1)S(1)} %get-tuple-element.29), channel_id=1, source_target_pairs={{0,8},{4,12},{8,0},{12,4},{1,9},{5,13},{9,1},{13,5},{2,10},{6,14},... | collective-permute-start | bytes 393224 | tf_op jit(solution)/shard_map/ppermute | solution.py:480
  7.6 9.6 %collective-permute-start.4 = (bf16[128,256]{1,0:T(8,128)(2,1)S(1)}, bf16[128,256]{1,0:T(8,128)(2,1)S(1)}, u32[]{:S(2)}, u32[]{:S(2)}) collective-permute-start(bf16[128,256]{1,0:T(8,128)(2,1)S(1)} %get-tuple-element.30), channel_id=1, source_target_pairs={{0,12},{4,8},{8,4},{12,0},{1,13},{5,9},{9,5},{13,1},{2,14},{6,10},... | collective-permute-start | bytes 196616 | tf_op jit(solution)/shard_map/ppermute | solution.py:480
  9.3 8.8 %collective-permute-start.8 = (bf16[128,256]{1,0:T(8,128)(2,1)S(1)}, bf16[128,256]{1,0:T(8,128)(2,1)S(1)}, u32[]{:S(2)}, u32[]{:S(2)}) collective-permute-start(bf16[128,256]{1,0:T(8,128)(2,1)S(1)} %get-tuple-element.38), channel_id=1, source_target_pairs={{0,12},{4,8},{8,4},{12,0},{1,13},{5,9},{9,5},{13,1},{2,14},{6,10},... | collective-permute-start | bytes 196616 | tf_op jit(solution)/shard_map/ppermute | solution.py:480
  10.0 3.8 %copy-start.4 = (bf16[128,1024]{1,0:T(8,128)(2,1)S(1)}, bf16[128,1024]{1,0:T(8,128)(2,1)}, u32[]{:S(2)}) copy-start(bf16[128,1024]{1,0:T(8,128)(2,1)} %value_ref.1) | copy-start | bytes 786436
  10.0 3.8 %copy-start.6 = (bf16[256,256]{1,0:T(8,128)(2,1)S(1)}, bf16[256,256]{1,0:T(8,128)(2,1)}, u32[]{:S(2)}) copy-start(bf16[256,256]{1,0:T(8,128)(2,1)} %constant.5.clone.rest_3_.rest_4_) | copy-start | bytes 393220
  10.5 5.3 %collective-permute-start.6 = (bf16[128,128]{1,0:T(8,128)(2,1)S(1)}, bf16[128,128]{1,0:T(8,128)(2,1)S(1)}, u32[]{:S(2)}, u32[]{:S(2)}) collective-permute-start(bf16[128,128]{1,0:T(8,128)(2,1)S(1)} %slice.8), channel_id=1, source_target_pairs={{0,16},{16,0},{1,17},{17,1},{2,18},{18,2},{3,19},{19,3},{4,20},{20... | collective-permute-start | bytes 98312 | tf_op jit(solution)/shard_map/ppermute | solution.py:539
  12.2 4.2 %collective-permute-start.7 = (bf16[128,128]{1,0:T(8,128)(2,1)S(1)}, bf16[128,128]{1,0:T(8,128)(2,1)S(1)}, u32[]{:S(2)}, u32[]{:S(2)}) collective-permute-start(bf16[128,128]{1,0:T(8,128)(2,1)S(1)} %slice.9), channel_id=1, source_target_pairs={{0,16},{16,0},{1,17},{17,1},{2,18},{18,2},{3,19},{19,3},{4,20},{20... | collective-permute-start | bytes 98312 | tf_op jit(solution)/shard_map/ppermute | solution.py:539
  13.8 1.1 %copy-start.7 = (bf16[8,128,128]{2,1,0:T(8,128)(2,1)S(1)}, bf16[8,128,128]{2,1,0:T(8,128)(2,1)}, u32[]{:S(2)}) copy-start(bf16[8,128,128]{2,1,0:T(8,128)(2,1)} %rest_2_.8) | copy-start | bytes 786436
  15.7 1.6 %copy-start.1 = (bf16[128,1024]{1,0:T(8,128)(2,1)S(1)}, bf16[128,1024]{1,0:T(8,128)(2,1)}, u32[]{:S(2)}) copy-start(bf16[128,1024]{1,0:T(8,128)(2,1)} %own_ref.2) | copy-start | bytes 786436
  17.3 1.0 %copy-start = (bf16[128,1024]{1,0:T(8,128)(2,1)S(1)}, bf16[128,1024]{1,0:T(8,128)(2,1)}, u32[]{:S(2)}) copy-start(bf16[128,1024]{1,0:T(8,128)(2,1)} %own_ref.3) | copy-start | bytes 786436
  18.6 1.9 %collective-permute-start.11 = (bf16[128,256]{1,0:T(8,128)(2,1)S(1)}, bf16[128,256]{1,0:T(8,128)(2,1)S(1)}, u32[]{:S(2)}, u32[]{:S(2)}) collective-permute-start(bf16[128,256]{1,0:T(8,128)(2,1)S(1)} %get-tuple-element.42), channel_id=1, source_target_pairs={{0,4},{4,0},{8,12},{12,8},{1,5},{5,1},{9,13},{13,9},{2,6},{6,2},{1... | collective-permute-start | bytes 196616 | tf_op jit(solution)/shard_map/ppermute | solution.py:480
  18.7 4.5 %collective-permute-start.10 = (bf16[128,256]{1,0:T(8,128)(2,1)S(1)}, bf16[128,256]{1,0:T(8,128)(2,1)S(1)}, u32[]{:S(2)}, u32[]{:S(2)}) collective-permute-start(bf16[128,256]{1,0:T(8,128)(2,1)S(1)} %get-tuple-element.40), channel_id=1, source_target_pairs={{0,8},{4,12},{8,0},{12,4},{1,9},{5,13},{9,1},{13,5},{2,10},{6,14},... | collective-permute-start | bytes 196616 | tf_op jit(solution)/shard_map/ppermute | solution.py:480
  20.2 4.1 %collective-permute-start.9 = (bf16[128,256]{1,0:T(8,128)(2,1)S(1)}, bf16[128,256]{1,0:T(8,128)(2,1)S(1)}, u32[]{:S(2)}, u32[]{:S(2)}) collective-permute-start(bf16[128,256]{1,0:T(8,128)(2,1)S(1)} %get-tuple-element.39), channel_id=1, source_target_pairs={{0,12},{4,8},{8,4},{12,0},{1,13},{5,9},{9,5},{13,1},{2,14},{6,10},... | collective-permute-start | bytes 196616 | tf_op jit(solution)/shard_map/ppermute | solution.py:480
